TPU v7x, 256 devices: a whole 4x4x8 slice. The times are simulated.
256 devices in a mesh: dp: 4 (over y_hi, core), seq: 64 (over x, y_lo, z).
Axes of the slice: x: 4, y: 4 (y_hi: 2, y_lo: 2; y = y_hi * 2 + y_lo), z: 8, core: 2. Of those that a mesh axis runs over, the one named last changes fastest.
Arguments:
- q_raw: bfloat16 [4, 8192, 1536], P('dp', 'seq'), may hold values from -6 to 6
- k_raw: bfloat16 [4, 8192, 1536], P('dp', 'seq'), may hold values from -6 to 6
- values: bfloat16 [4, 8192, 1536], P('dp', 'seq'), may hold values from -6 to 6
- d_out: bfloat16 [4, 8192, 1536], P('dp', 'seq'), may hold values from -14 to 14
- q_gain: float32 [128], replicated, may hold values from 1 to 2.5
- k_gain: float32 [128], replicated, may hold values from 1 to 2.5
Outputs:
- q_grad: bfloat16 [4, 8192, 1536], P('dp', 'seq')
- k_grad: bfloat16 [4, 8192, 1536], P('dp', 'seq')
- v_grad: bfloat16 [4, 8192, 1536], P('dp', 'seq')
- q_gain_grad: float32 [128], replicated
- k_gain_grad: float32 [128], replicated
All inputs are finite; a program needn't handle non-finite values.
Results may differ from a plain program's by a relative error of at most 0.012.
The roundings to bfloat16 on the way count: a program that leaves them out, or rounds other values in their place, can miss the bound.
Values may be sent and summed in bfloat16 or wider, within the bound.
No kernel may reach another device: no remote copies, remote signals or barrier semaphores. Data moves between devices by JAX's collectives and lax.ppermute only.
A program may use at most 256 MiB of HBM per device.

v0:
```python
import jax
import jax.numpy as jnp
from jax import lax
from jax.sharding import PartitionSpec as P

HEADS = 12
HD = 128
TILE_TOK = 64
BF = 1
BH = 1
BW = 2


EPSILON = 1e-06


def passed_along(value, axis, steps):
    count = lax.axis_size(axis)
    initial, last = (max(0, -steps), min(count, count - steps))
    return lax.ppermute(value, axis, [(source, source + steps) for source in range(initial, last)])


def product(form, left, right):
    return jnp.einsum(form, left, right, preferred_element_type=jnp.float32)


def normalize(source, scaling):
    inputs = source.astype(jnp.float32)
    inverse = lax.rsqrt(jnp.mean(inputs * inputs, axis=-1, keepdims=True) + EPSILON)
    return (inputs, inverse, inputs * inverse * scaling)


def norm_back(inputs, inverse, scaling, cotangent):
    scaled = cotangent * scaling
    input_grad = inverse * scaled - inputs * inverse * inverse * inverse * jnp.mean(
        inputs * scaled, axis=-1, keepdims=True
    )
    gain_grad = jnp.sum((cotangent * inputs * inverse).reshape(-1, inputs.shape[-1]), axis=0)
    return (input_grad, gain_grad)


def offsets():
    return [(a, b, c) for a in (-1, 0, 1) for b in (-1, 0, 1) for c in (-1, 0, 1)]


def window(extended, a, b, c, grid_dims):
    return extended[
        1 + a : 1 + a + grid_dims[0], 1 + b : 1 + b + grid_dims[1], 1 + c : 1 + c + grid_dims[2]
    ]


def tile_mask(inside, a, b, c, grid_dims):
    along_f = inside[0][1 + a : 1 + a + grid_dims[0]]
    along_h = inside[1][1 + b : 1 + b + grid_dims[1]]
    along_w = inside[2][1 + c : 1 + c + grid_dims[2]]
    keep = along_f[:, None, None] & along_h[None, :, None] & along_w[None, None, :]
    return keep.reshape(-1, 1, 1, 1)


def attend(q_tiles, key_ext, value_ext, inside, grid_dims):
    tile_shape = q_tiles.shape
    scale = tile_shape[-1] ** (-0.5)
    logit_list = []
    normalizer = jnp.zeros((tile_shape[0], tile_shape[2], tile_shape[1]), jnp.float32)
    for a, b, c in offsets():
        key_tile = window(key_ext, a, b, c, grid_dims).reshape(tile_shape)
        logits = product("tqhd,tkhd->thqk", q_tiles, key_tile) * scale
        keep = tile_mask(inside, a, b, c, grid_dims)
        logit_list.append((logits, keep))
        normalizer = normalizer + jnp.sum(jnp.where(keep, jnp.exp(logits), 0.0), axis=-1)
    log_norm = jnp.log(normalizer)
    chances = []
    attended = jnp.zeros(tile_shape, jnp.float32)
    for number, (a, b, c) in enumerate(offsets()):
        logits, keep = logit_list[number]
        chance = jnp.where(keep, jnp.exp(logits - log_norm[..., None]), 0.0)
        chances.append(chance)
        value_tile = window(value_ext, a, b, c, grid_dims).reshape(tile_shape)
        attended = attended + product("thqk,tkhd->tqhd", chance.astype(jnp.bfloat16), value_tile)
    return (chances, log_norm, attended)


def query_side(q_tiles, key_ext, value_ext, upstream, chances, row_dot, grid_dims):
    tile_shape = q_tiles.shape
    dot_rows = jnp.transpose(row_dot, (0, 2, 1))[..., None]
    query_grad = jnp.zeros(tile_shape, jnp.float32)
    for number, (a, b, c) in enumerate(offsets()):
        chance = chances[number]
        key_tile = window(key_ext, a, b, c, grid_dims).reshape(tile_shape)
        value_tile = window(value_ext, a, b, c, grid_dims).reshape(tile_shape)
        weight_grad = product("tqhd,tkhd->thqk", upstream, value_tile)
        score_grad = (chance * (weight_grad - dot_rows)).astype(jnp.bfloat16)
        query_grad = query_grad + product("thqk,tkhd->tqhd", score_grad, key_tile)
    return query_grad


def key_side(key_tiles, value_tiles, query_ext, upstream_ext, log_ext, dot_ext, inside, grid_dims):
    tile_shape = key_tiles.shape
    scale = tile_shape[-1] ** (-0.5)
    key_grad = jnp.zeros(tile_shape, jnp.float32)
    value_grad = jnp.zeros(tile_shape, jnp.float32)
    for a, b, c in offsets():
        queries = window(query_ext, a, b, c, grid_dims).reshape(tile_shape)
        upstream = window(upstream_ext, a, b, c, grid_dims).reshape(tile_shape)
        log_norm = jnp.transpose(
            window(log_ext, a, b, c, grid_dims).reshape(tile_shape[:3]), (0, 2, 1)
        )[..., None]
        dot_rows = jnp.transpose(
            window(dot_ext, a, b, c, grid_dims).reshape(tile_shape[:3]), (0, 2, 1)
        )[..., None]
        keep = tile_mask(inside, a, b, c, grid_dims)
        logits = product("tqhd,tkhd->thqk", queries, key_tiles) * scale
        chance = jnp.where(keep, jnp.exp(logits - log_norm), 0.0)
        weight_grad = product("tqhd,tkhd->thqk", upstream, value_tiles)
        score_grad = (chance * (weight_grad - dot_rows)).astype(jnp.bfloat16)
        key_grad = key_grad + product("thqk,tqhd->tkhd", score_grad, queries)
        value_grad = value_grad + product("thqk,tqhd->tkhd", chance.astype(jnp.bfloat16), upstream)
    return (key_grad, value_grad)


def pick(offset, length):
    if offset < 0:
        return slice(length - 1, length)
    if offset > 0:
        return slice(0, 1)
    return slice(0, length)


def place(offset, length):
    if offset < 0:
        return slice(0, 1)
    if offset > 0:
        return slice(length + 1, length + 2)
    return slice(1, length + 1)


def send_direct(slab_part, distance, label):
    if label == "stats":
        return passed_along(slab_part, "seq", distance)
    if label == "query":
        return passed_along(slab_part, "seq", distance)
    return passed_along(slab_part, "seq", distance)


def direct_extend(block, strides, label):
    grid_dims = block.shape[1:4]
    extended = jnp.zeros(
        block.shape[:1] + tuple((n + 2 for n in grid_dims)) + block.shape[4:], block.dtype
    )
    extended = extended.at[(slice(None),) + tuple((place(0, n) for n in grid_dims))].set(block)
    for a, b, c in offsets():
        if a == 0 and b == 0 and (c == 0):
            continue
        direction = (a, b, c)
        slab_part = block[
            (slice(None),) + tuple((pick(o, n) for o, n in zip(direction, grid_dims)))
        ]
        distance = -(a * strides[0] + b * strides[1] + c * strides[2])
        arrived = send_direct(slab_part, distance, label)
        extended = extended.at[
            (slice(None),) + tuple((place(o, n) for o, n in zip(direction, grid_dims)))
        ].set(arrived)
    return extended


def on_device(q_raw, k_raw, values, d_out, q_gain, k_gain):
    seq_count = lax.axis_size("seq")
    grid_wide = min(4, seq_count // 4)
    grid_high = 2
    grid_deep = seq_count // (grid_high * grid_wide)
    device_index = lax.axis_index("seq")
    column_block = device_index % grid_wide
    row_block = device_index // grid_wide % grid_high
    frame_block = device_index // (grid_wide * grid_high)
    strides = (grid_high * grid_wide, grid_wide, 1)
    block_dims = (BF, BH, BW)
    width = HEADS * HD
    tile_shape = (BF * BH * BW, TILE_TOK, HEADS, HD)
    grid_shape = block_dims + (TILE_TOK, HEADS, HD)
    inside = tuple(
        (
            (start * n + jnp.arange(n + 2) - 1 >= 0)
            & (start * n + jnp.arange(n + 2) - 1 < whole * n)
            for start, n, whole in (
                (frame_block, BF, grid_deep),
                (row_block, BH, grid_high),
                (column_block, BW, grid_wide),
            )
        )
    )

    def extend(block, label):
        return direct_extend(block, strides, label)

    q_source, q_inverse, q_normed = normalize(q_raw.reshape(grid_shape), q_gain)
    k_source, k_inverse, k_normed = normalize(k_raw.reshape(grid_shape), k_gain)
    q_block = q_normed.astype(jnp.bfloat16)
    k_block = k_normed.astype(jnp.bfloat16)
    q_tiles = q_block.reshape(tile_shape)
    flat_dims = block_dims + (TILE_TOK, width)
    pair = jnp.stack([k_block.reshape(flat_dims), values.reshape(flat_dims)])
    pair_ext = extend(pair, "pair")
    ext_dims = pair_ext.shape[1:4]
    ext_shape = ext_dims + (TILE_TOK, HEADS, HD)
    key_ext = pair_ext[0].reshape(ext_shape)
    value_ext = pair_ext[1].reshape(ext_shape)
    upstream = d_out.reshape(tile_shape)
    chances, log_norm, attended = attend(q_tiles, key_ext, value_ext, inside, block_dims)
    row_dot = jnp.sum(upstream.astype(jnp.float32) * attended, axis=-1)
    scale = HD ** (-0.5)
    query_grad = query_side(q_tiles, key_ext, value_ext, upstream, chances, row_dot, block_dims)
    carried = jnp.stack([q_block.reshape(flat_dims), d_out.reshape(flat_dims)])
    carried_ext = extend(carried, "query")
    stats = jnp.stack(
        [
            jnp.transpose(log_norm, (0, 2, 1)).reshape(block_dims + (TILE_TOK, HEADS)),
            row_dot.reshape(block_dims + (TILE_TOK, HEADS)),
        ]
    )
    stats_ext = extend(stats, "stats")
    key_grad, value_grad = key_side(
        k_block.reshape(tile_shape),
        values.reshape(tile_shape),
        carried_ext[0].reshape(ext_shape),
        carried_ext[1].reshape(ext_shape),
        stats_ext[0],
        stats_ext[1],
        inside,
        block_dims,
    )
    query_grad = scale * query_grad
    key_grad = scale * key_grad
    q_input_grad, q_gain_part = norm_back(
        q_source, q_inverse, q_gain, query_grad.reshape(grid_shape)
    )
    k_input_grad, k_gain_part = norm_back(k_source, k_inverse, k_gain, key_grad.reshape(grid_shape))
    q_gain_grad, k_gain_grad = lax.psum((q_gain_part, k_gain_part), ("dp", "seq"))
    out_shape = q_raw.shape
    return (
        q_input_grad.astype(jnp.bfloat16).reshape(out_shape),
        k_input_grad.astype(jnp.bfloat16).reshape(out_shape),
        value_grad.astype(jnp.bfloat16).reshape(out_shape),
        q_gain_grad,
        k_gain_grad,
    )


def solution(mesh):
    return jax.shard_map(
        on_device,
        mesh=mesh,
        in_specs=(
            P("dp", "seq", None),
            P("dp", "seq", None),
            P("dp", "seq", None),
            P("dp", "seq", None),
            P(),
            P(),
        ),
        out_specs=(P("dp", "seq", None), P("dp", "seq", None), P("dp", "seq", None), P(), P()),
        check_vma=False,
    )
```

profile of v0, /device:TPU:2, one launch (start us, length us, event | category | flops | bytes accessed | tf_op | source)
XLA Modules:
  0.0 1187.9 jit_solution(1418901989297325616)
XLA Ops:
  8.6 9.7 collective-permute-start
  36.6 6.3 collective-permute-start.20
  67.4 7.9 scatter.270
  75.3 6.8 scatter.315
  86.5 16.9 %collective-permute-done.20 = bf16[2,1,1,1,64,1536]{5,4,3,2,1,0:T(8,128)(2,1)} collective-permute-done((bf16[2,1,1,1,64,1536]{5,4,3,2,1,0:T(8,128)(2,1)}, bf16[2,1,1,1,64,1536]{5,4,3,2,1,0:T(8,128)(2,1)}, u32[]{:S(2)}, u32[]{:S(2)}) %collective-permute-start.20) | collective-permute-done | bytes 393248 | tf_op jit(solution)/shard_map/ppermute | solution.py:20
  108.6 7.7 collective-permute-start.6
  126.4 7.2 collective-permute-start.9
  139.3 35.3 %collective-permute-done.6 = bf16[2,1,1,1,64,1536]{5,4,3,2,1,0:T(8,128)(2,1)S(1)} collective-permute-done((bf16[2,1,1,1,64,1536]{5,4,3,2,1,0:T(8,128)(2,1)}, bf16[2,1,1,1,64,1536]{5,4,3,2,1,0:T(8,128)(2,1)S(1)}, u32[]{:S(2)}, u32[]{:S(2)}) %collective-permute-start.6) | collective-permute-done | bytes 393248 | tf_op jit(solution)/shard_map/ppermute | solution.py:20
  180.3 5.4 collective-permute-done.8
  185.7 8.5 collective-permute-start.13
  197.4 31.0 %collective-permute-done.9 = bf16[2,1,1,1,64,1536]{5,4,3,2,1,0:T(8,128)(2,1)S(1)} collective-permute-done((bf16[2,1,1,1,64,1536]{5,4,3,2,1,0:T(8,128)(2,1)}, bf16[2,1,1,1,64,1536]{5,4,3,2,1,0:T(8,128)(2,1)S(1)}, u32[]{:S(2)}, u32[]{:S(2)}) %collective-permute-start.9) | collective-permute-done | bytes 393248 | tf_op jit(solution)/shard_map/ppermute | solution.py:20
  231.2 17.1 %collective-permute-start.15 = (bf16[2,1,1,2,64,1536]{5,4,3,2,1,0:T(8,128)(2,1)}, bf16[2,1,1,2,64,1536]{5,4,3,2,1,0:T(8,128)(2,1)S(1)}, u32[]{:S(2)}, u32[]{:S(2)}) collective-permute-start(bf16[2,1,1,2,64,1536]{5,4,3,2,1,0:T(8,128)(2,1)} %pad_maximum_fusion), channel_id=1, source_target_pairs={{8,0},{9,1},{10,2},{11,3},{12,4},{13,5},{14,6},{15,7},{16,8},{17,9... | collective-permute-start | bytes 2359304 | tf_op jit(solution)/shard_map/ppermute | solution.py:20
  259.9 29.3 %collective-permute-done.14 = bf16[2,1,1,1,64,1536]{5,4,3,2,1,0:T(8,128)(2,1)S(1)} collective-permute-done((bf16[2,1,1,1,64,1536]{5,4,3,2,1,0:T(8,128)(2,1)}, bf16[2,1,1,1,64,1536]{5,4,3,2,1,0:T(8,128)(2,1)S(1)}, u32[]{:S(2)}, u32[]{:S(2)}) %collective-permute-start.14) | collective-permute-done | bytes 393248 | tf_op jit(solution)/shard_map/ppermute | solution.py:20
  297.5 24.3 %collective-permute-done.17 = bf16[2,1,1,1,64,1536]{5,4,3,2,1,0:T(8,128)(2,1)S(1)} collective-permute-done((bf16[2,1,1,1,64,1536]{5,4,3,2,1,0:T(8,128)(2,1)}, bf16[2,1,1,1,64,1536]{5,4,3,2,1,0:T(8,128)(2,1)S(1)}, u32[]{:S(2)}, u32[]{:S(2)}) %collective-permute-start.17) | collective-permute-done | bytes 393248 | tf_op jit(solution)/shard_map/ppermute | solution.py:20
  321.8 8.4 collective-permute-start.24
  330.9 25.7 %collective-permute-start.22 = (bf16[2,1,1,1,64,1536]{5,4,3,2,1,0:T(8,128)(2,1)}, bf16[2,1,1,1,64,1536]{5,4,3,2,1,0:T(8,128)(2,1)}, u32[]{:S(2)}, u32[]{:S(2)}) collective-permute-start(bf16[2,1,1,1,64,1536]{5,4,3,2,1,0:T(8,128)(2,1)} %get-tuple-element.1097), channel_id=1, source_target_pairs={{0,11},{1,12},{2,13},{3,14},{4,15},{5,16},{6,17},{7,18},{8,19},{9,... | collective-permute-start | bytes 1179656 | tf_op jit(solution)/shard_map/ppermute | solution.py:20
  357.6 6.5 collective-permute-done.19
  367.2 10.2 fusion.627
  377.4 13.6 %reshape_squeeze.13 = bf16[3,3,4,64,12,128]{5,4,3,2,1,0:T(8,128)(2,1)} reshape(bf16[1,3,3,4,64,1536]{5,4,3,2,1,0:T(8,128)(2,1)} %get-tuple-element.987) | data formatting | bytes 14155776 | tf_op jit(solution)/shard_map/reshape;squeeze | solution.py:206
  391.0 13.6 %reshape_squeeze.12 = bf16[3,3,4,64,12,128]{5,4,3,2,1,0:T(8,128)(2,1)} reshape(bf16[1,3,3,4,64,1536]{5,4,3,2,1,0:T(8,128)(2,1)} %get-tuple-element.988) | data formatting | bytes 14155776 | tf_op jit(solution)/shard_map/reshape;squeeze | solution.py:205
  404.6 7.0 fusion.634
  411.7 6.9 fusion.633
  493.0 5.4 collective-permute-start.28
  502.0 5.5 collective-permute-start.29
  509.7 25.1 %collective-permute-start.30 = (bf16[2,1,1,1,64,1536]{5,4,3,2,1,0:T(8,128)(2,1)}, bf16[2,1,1,1,64,1536]{5,4,3,2,1,0:T(8,128)(2,1)S(1)}, u32[]{:S(2)}, u32[]{:S(2)}) collective-permute-start(bf16[2,1,1,1,64,1536]{5,4,3,2,1,0:T(8,128)(2,1)} %get-tuple-element.1097), channel_id=1, source_target_pairs={{1,0},{2,1},{3,2},{4,3},{5,4},{6,5},{7,6},{8,7},{9,8},{10,9},{11,1... | collective-permute-start | bytes 1179656 | tf_op jit(solution)/shard_map/ppermute | solution.py:20
  541.1 10.1 collective-permute-start.32
  552.3 4.6 collective-permute-done.28
  556.8 6.2 collective-permute-start.33
  564.2 32.5 %collective-permute-done.29 = bf16[2,1,1,1,64,1536]{5,4,3,2,1,0:T(8,128)(2,1)S(1)} collective-permute-done((bf16[2,1,1,1,64,1536]{5,4,3,2,1,0:T(8,128)(2,1)}, bf16[2,1,1,1,64,1536]{5,4,3,2,1,0:T(8,128)(2,1)S(1)}, u32[]{:S(2)}, u32[]{:S(2)}) %collective-permute-start.29) | collective-permute-done | bytes 393248 | tf_op jit(solution)/shard_map/ppermute | solution.py:20
  599.7 20.7 %collective-permute-start.35 = (bf16[2,1,1,2,64,1536]{5,4,3,2,1,0:T(8,128)(2,1)S(1)}, bf16[2,1,1,2,64,1536]{5,4,3,2,1,0:T(8,128)(2,1)S(1)}, u32[]{:S(2)}, u32[]{:S(2)}) collective-permute-start(bf16[2,1,1,2,64,1536]{5,4,3,2,1,0:T(8,128)(2,1)S(1)} %copy-done.53), channel_id=1, source_target_pairs={{8,0},{9,1},{10,2},{11,3},{12,4},{13,5},{14,6},{15,7},{16,8},{17,9... | collective-permute-start | bytes 2359304 | tf_op jit(solution)/shard_map/ppermute | solution.py:20
  626.9 4.0 collective-permute-start.37
  635.4 4.8 collective-permute-start.39
  641.1 12.9 %collective-permute-start.41 = (f32[2,1,1,2,64,12]{4,5,3,2,1,0:T(8,128)S(1)}, f32[2,1,1,2,64,12]{4,5,3,2,1,0:T(8,128)S(1)}, u32[]{:S(2)}, u32[]{:S(2)}) collective-permute-start(f32[2,1,1,2,64,12]{4,5,3,2,1,0:T(8,128)S(1)} %pad_maximum_fusion.2), channel_id=1, source_target_pairs={{0,12},{1,13},{2,14},{3,15},{4,16},{5,17},{6,18},{7,19},{8,20},{9,... | collective-permute-start | bytes 36872 | tf_op jit(solution)/shard_map/ppermute | solution.py:20
  654.7 19.0 %collective-permute-done.36 = bf16[2,1,1,1,64,1536]{5,4,3,2,1,0:T(8,128)(2,1)S(1)} collective-permute-done((bf16[2,1,1,1,64,1536]{5,4,3,2,1,0:T(8,128)(2,1)}, bf16[2,1,1,1,64,1536]{5,4,3,2,1,0:T(8,128)(2,1)S(1)}, u32[]{:S(2)}, u32[]{:S(2)}) %collective-permute-start.36) | collective-permute-done | bytes 393248 | tf_op jit(solution)/shard_map/ppermute | solution.py:20
  673.7 9.8 collective-permute-start.40
  686.9 13.1 %collective-permute-start.43 = (f32[2,1,1,1,64,12]{4,5,3,2,1,0:T(8,128)}, f32[2,1,1,1,64,12]{4,5,3,2,1,0:T(8,128)S(1)}, u32[]{:S(2)}, u32[]{:S(2)}) collective-permute-start(f32[2,1,1,1,64,12]{4,5,3,2,1,0:T(8,128)} %get-tuple-element.1158), channel_id=1, source_target_pairs={{0,9},{1,10},{2,11},{3,12},{4,13},{5,14},{6,15},{7,16},{8,17},{9,1... | collective-permute-start | bytes 18440 | tf_op jit(solution)/shard_map/ppermute | solution.py:20
  702.0 4.3 collective-permute-done.39
  706.4 5.5 fusion.626
  711.9 13.6 %reshape_squeeze.15 = bf16[3,3,4,64,12,128]{5,4,3,2,1,0:T(8,128)(2,1)} reshape(bf16[1,3,3,4,64,1536]{5,4,3,2,1,0:T(8,128)(2,1)} %get-tuple-element.985) | data formatting | bytes 14155776 | tf_op jit(solution)/shard_map/reshape;squeeze | solution.py:225
  725.5 13.6 %reshape_squeeze.14 = bf16[3,3,4,64,12,128]{5,4,3,2,1,0:T(8,128)(2,1)} reshape(bf16[1,3,3,4,64,1536]{5,4,3,2,1,0:T(8,128)(2,1)} %get-tuple-element.986) | data formatting | bytes 14155776 | tf_op jit(solution)/shard_map/reshape;squeeze | solution.py:224
  739.1 8.0 fusion.629
  747.1 7.0 fusion.630
  847.4 12.6 %collective-permute-start.45 = (f32[2,1,1,1,64,12]{4,5,3,2,1,0:T(8,128)}, f32[2,1,1,1,64,12]{4,5,3,2,1,0:T(8,128)S(1)}, u32[]{:S(2)}, u32[]{:S(2)}) collective-permute-start(f32[2,1,1,1,64,12]{4,5,3,2,1,0:T(8,128)} %get-tuple-element.1157), channel_id=1, source_target_pairs={{0,7},{1,8},{2,9},{3,10},{4,11},{5,12},{6,13},{7,14},{8,15},{9,16}... | collective-permute-start | bytes 18440 | tf_op jit(solution)/shard_map/ppermute | solution.py:20
  866.7 6.5 collective-permute-start.48
  877.2 8.3 collective-permute-start.50
  888.6 5.3 collective-permute-start.52
  894.6 7.6 collective-permute-start.53
  1101.3 86.5 %all-reduce.3 = (f32[128]{0:T(128)}, f32[128]{0:T(128)}) all-reduce(f32[128]{0:T(128)S(1)} %copy-done.161, f32[128]{0:T(128)S(1)} %get-tuple-element.977), channel_id=1, replica_groups=mesh['dp'=4,'seq'=64] {'dp','seq'}, use_global_device_ids=true, to_apply=%region_33.34 | all-reduce | flops 256 | bytes 2048 | tf_op jit(solution)/shard_map/psum | solution.py:237
  (735 shorter events, 514.8 us)
Async XLA Ops:
  8.6 74.1 %collective-permute-start = (bf16[2,1,1,1,64,1536]{5,4,3,2,1,0:T(8,128)(2,1)}, bf16[2,1,1,1,64,1536]{5,4,3,2,1,0:T(8,128)(2,1)}, u32[]{:S(2)}, u32[]{:S(2)}) collective-permute-start(bf16[2,1,1,1,64,1536]{5,4,3,2,1,0:T(8,128)(2,1)} %get-tuple-element.1100), channel_id=1, source_target_pairs={{0,13},{1,14},{2,15},{3,16},{4,17},{5,18},{6,19},{7,20},{8,21},{9,... | collective-permute-start | bytes 1179656 | tf_op jit(solution)/shard_map/ppermute | solution.py:20
  18.3 104.3 %collective-permute-start.3 = (bf16[2,1,1,1,64,1536]{5,4,3,2,1,0:T(8,128)(2,1)}, bf16[2,1,1,1,64,1536]{5,4,3,2,1,0:T(8,128)(2,1)}, u32[]{:S(2)}, u32[]{:S(2)}) collective-permute-start(bf16[2,1,1,1,64,1536]{5,4,3,2,1,0:T(8,128)(2,1)} %get-tuple-element.1100), channel_id=1, source_target_pairs={{0,9},{1,10},{2,11},{3,12},{4,13},{5,14},{6,15},{7,16},{8,17},{9,1... | collective-permute-start | bytes 1179656 | tf_op jit(solution)/shard_map/ppermute | solution.py:20
  24.0 84.6 %collective-permute-start.1 = (bf16[2,1,1,2,64,1536]{5,4,3,2,1,0:T(8,128)(2,1)}, bf16[2,1,1,2,64,1536]{5,4,3,2,1,0:T(8,128)(2,1)}, u32[]{:S(2)}, u32[]{:S(2)}) collective-permute-start(bf16[2,1,1,2,64,1536]{5,4,3,2,1,0:T(8,128)(2,1)} %pad_maximum_fusion), channel_id=1, source_target_pairs={{0,12},{1,13},{2,14},{3,15},{4,16},{5,17},{6,18},{7,19},{8,20},{9,... | collective-permute-start | bytes 2359304 | tf_op jit(solution)/shard_map/ppermute | solution.py:20
  27.1 99.3 %collective-permute-start.4 = (bf16[2,1,1,2,64,1536]{5,4,3,2,1,0:T(8,128)(2,1)}, bf16[2,1,1,2,64,1536]{5,4,3,2,1,0:T(8,128)(2,1)}, u32[]{:S(2)}, u32[]{:S(2)}) collective-permute-start(bf16[2,1,1,2,64,1536]{5,4,3,2,1,0:T(8,128)(2,1)} %pad_maximum_fusion), channel_id=1, source_target_pairs={{0,8},{1,9},{2,10},{3,11},{4,12},{5,13},{6,14},{7,15},{8,16},{9,17... | collective-permute-start | bytes 2359304 | tf_op jit(solution)/shard_map/ppermute | solution.py:20
  36.6 66.8 %collective-permute-start.20 = (bf16[2,1,1,1,64,1536]{5,4,3,2,1,0:T(8,128)(2,1)}, bf16[2,1,1,1,64,1536]{5,4,3,2,1,0:T(8,128)(2,1)}, u32[]{:S(2)}, u32[]{:S(2)}) collective-permute-start(bf16[2,1,1,1,64,1536]{5,4,3,2,1,0:T(8,128)(2,1)} %get-tuple-element.1098), channel_id=1, source_target_pairs={{0,13},{1,14},{2,15},{3,16},{4,17},{5,18},{6,19},{7,20},{8,21},{9,... | collective-permute-start | bytes 1179656 | tf_op jit(solution)/shard_map/ppermute | solution.py:20
  82.8 35.7 %collective-permute-start.2 = (bf16[2,1,1,1,64,1536]{5,4,3,2,1,0:T(8,128)(2,1)}, bf16[2,1,1,1,64,1536]{5,4,3,2,1,0:T(8,128)(2,1)S(1)}, u32[]{:S(2)}, u32[]{:S(2)}) collective-permute-start(bf16[2,1,1,1,64,1536]{5,4,3,2,1,0:T(8,128)(2,1)} %get-tuple-element.1099), channel_id=1, source_target_pairs={{0,11},{1,12},{2,13},{3,14},{4,15},{5,16},{6,17},{7,18},{8,19},{9,... | collective-permute-start | bytes 1179656 | tf_op jit(solution)/shard_map/ppermute | solution.py:20
  103.3 32.4 %collective-permute-start.5 = (bf16[2,1,1,1,64,1536]{5,4,3,2,1,0:T(8,128)(2,1)}, bf16[2,1,1,1,64,1536]{5,4,3,2,1,0:T(8,128)(2,1)S(1)}, u32[]{:S(2)}, u32[]{:S(2)}) collective-permute-start(bf16[2,1,1,1,64,1536]{5,4,3,2,1,0:T(8,128)(2,1)} %get-tuple-element.1099), channel_id=1, source_target_pairs={{0,7},{1,8},{2,9},{3,10},{4,11},{5,12},{6,13},{7,14},{8,15},{9,16}... | collective-permute-start | bytes 1179656 | tf_op jit(solution)/shard_map/ppermute | solution.py:20
  108.6 66.0 %collective-permute-start.6 = (bf16[2,1,1,1,64,1536]{5,4,3,2,1,0:T(8,128)(2,1)}, bf16[2,1,1,1,64,1536]{5,4,3,2,1,0:T(8,128)(2,1)S(1)}, u32[]{:S(2)}, u32[]{:S(2)}) collective-permute-start(bf16[2,1,1,1,64,1536]{5,4,3,2,1,0:T(8,128)(2,1)} %get-tuple-element.1100), channel_id=1, source_target_pairs={{0,5},{1,6},{2,7},{3,8},{4,9},{5,10},{6,11},{7,12},{8,13},{9,14},{... | collective-permute-start | bytes 1179656 | tf_op jit(solution)/shard_map/ppermute | solution.py:20
  118.4 58.9 %collective-permute-start.7 = (bf16[2,1,1,2,64,1536]{5,4,3,2,1,0:T(8,128)(2,1)}, bf16[2,1,1,2,64,1536]{5,4,3,2,1,0:T(8,128)(2,1)S(1)}, u32[]{:S(2)}, u32[]{:S(2)}) collective-permute-start(bf16[2,1,1,2,64,1536]{5,4,3,2,1,0:T(8,128)(2,1)} %pad_maximum_fusion), channel_id=1, source_target_pairs={{0,4},{1,5},{2,6},{3,7},{4,8},{5,9},{6,10},{7,11},{8,12},{9,13},{1... | collective-permute-start | bytes 2359304 | tf_op jit(solution)/shard_map/ppermute | solution.py:20
  122.6 63.1 %collective-permute-start.8 = (bf16[2,1,1,1,64,1536]{5,4,3,2,1,0:T(8,128)(2,1)}, bf16[2,1,1,1,64,1536]{5,4,3,2,1,0:T(8,128)(2,1)S(1)}, u32[]{:S(2)}, u32[]{:S(2)}) collective-permute-start(bf16[2,1,1,1,64,1536]{5,4,3,2,1,0:T(8,128)(2,1)} %get-tuple-element.1099), channel_id=1, source_target_pairs={{0,3},{1,4},{2,5},{3,6},{4,7},{5,8},{6,9},{7,10},{8,11},{9,12},{10... | collective-permute-start | bytes 1179656 | tf_op jit(solution)/shard_map/ppermute | solution.py:20
  126.4 102.0 %collective-permute-start.9 = (bf16[2,1,1,1,64,1536]{5,4,3,2,1,0:T(8,128)(2,1)}, bf16[2,1,1,1,64,1536]{5,4,3,2,1,0:T(8,128)(2,1)S(1)}, u32[]{:S(2)}, u32[]{:S(2)}) collective-permute-start(bf16[2,1,1,1,64,1536]{5,4,3,2,1,0:T(8,128)(2,1)} %get-tuple-element.1100), channel_id=1, source_target_pairs={{0,1},{1,2},{2,3},{3,4},{4,5},{5,6},{6,7},{7,8},{8,9},{9,10},{10,1... | collective-permute-start | bytes 1179656 | tf_op jit(solution)/shard_map/ppermute | solution.py:20
  135.7 95.4 %collective-permute-start.10 = (bf16[2,1,1,1,64,1536]{5,4,3,2,1,0:T(8,128)(2,1)}, bf16[2,1,1,1,64,1536]{5,4,3,2,1,0:T(8,128)(2,1)S(1)}, u32[]{:S(2)}, u32[]{:S(2)}) collective-permute-start(bf16[2,1,1,1,64,1536]{5,4,3,2,1,0:T(8,128)(2,1)} %get-tuple-element.1099), channel_id=1, source_target_pairs={{1,0},{2,1},{3,2},{4,3},{5,4},{6,5},{7,6},{8,7},{9,8},{10,9},{11,1... | collective-permute-start | bytes 1179656 | tf_op jit(solution)/shard_map/ppermute | solution.py:20
  174.7 74.4 %collective-permute-start.11 = (bf16[2,1,1,1,64,1536]{5,4,3,2,1,0:T(8,128)(2,1)}, bf16[2,1,1,1,64,1536]{5,4,3,2,1,0:T(8,128)(2,1)S(1)}, u32[]{:S(2)}, u32[]{:S(2)}) collective-permute-start(bf16[2,1,1,1,64,1536]{5,4,3,2,1,0:T(8,128)(2,1)} %get-tuple-element.1100), channel_id=1, source_target_pairs={{3,0},{4,1},{5,2},{6,3},{7,4},{8,5},{9,6},{10,7},{11,8},{12,9},{13... | collective-permute-start | bytes 1179656 | tf_op jit(solution)/shard_map/ppermute | solution.py:20
  177.4 74.4 %collective-permute-start.12 = (bf16[2,1,1,2,64,1536]{5,4,3,2,1,0:T(8,128)(2,1)}, bf16[2,1,1,2,64,1536]{5,4,3,2,1,0:T(8,128)(2,1)S(1)}, u32[]{:S(2)}, u32[]{:S(2)}) collective-permute-start(bf16[2,1,1,2,64,1536]{5,4,3,2,1,0:T(8,128)(2,1)} %pad_maximum_fusion), channel_id=1, source_target_pairs={{4,0},{5,1},{6,2},{7,3},{8,4},{9,5},{10,6},{11,7},{12,8},{13,9},{1... | collective-permute-start | bytes 2359304 | tf_op jit(solution)/shard_map/ppermute | solution.py:20
  185.7 69.0 %collective-permute-start.13 = (bf16[2,1,1,1,64,1536]{5,4,3,2,1,0:T(8,128)(2,1)}, bf16[2,1,1,1,64,1536]{5,4,3,2,1,0:T(8,128)(2,1)S(1)}, u32[]{:S(2)}, u32[]{:S(2)}) collective-permute-start(bf16[2,1,1,1,64,1536]{5,4,3,2,1,0:T(8,128)(2,1)} %get-tuple-element.1099), channel_id=1, source_target_pairs={{5,0},{6,1},{7,2},{8,3},{9,4},{10,5},{11,6},{12,7},{13,8},{14,9},{... | collective-permute-start | bytes 1179656 | tf_op jit(solution)/shard_map/ppermute | solution.py:20
  228.5 60.7 %collective-permute-start.14 = (bf16[2,1,1,1,64,1536]{5,4,3,2,1,0:T(8,128)(2,1)}, bf16[2,1,1,1,64,1536]{5,4,3,2,1,0:T(8,128)(2,1)S(1)}, u32[]{:S(2)}, u32[]{:S(2)}) collective-permute-start(bf16[2,1,1,1,64,1536]{5,4,3,2,1,0:T(8,128)(2,1)} %get-tuple-element.1100), channel_id=1, source_target_pairs={{7,0},{8,1},{9,2},{10,3},{11,4},{12,5},{13,6},{14,7},{15,8},{16,9}... | collective-permute-start | bytes 1179656 | tf_op jit(solution)/shard_map/ppermute | solution.py:20
  231.2 60.7 %collective-permute-start.15 = (bf16[2,1,1,2,64,1536]{5,4,3,2,1,0:T(8,128)(2,1)}, bf16[2,1,1,2,64,1536]{5,4,3,2,1,0:T(8,128)(2,1)S(1)}, u32[]{:S(2)}, u32[]{:S(2)}) collective-permute-start(bf16[2,1,1,2,64,1536]{5,4,3,2,1,0:T(8,128)(2,1)} %pad_maximum_fusion), channel_id=1, source_target_pairs={{8,0},{9,1},{10,2},{11,3},{12,4},{13,5},{14,6},{15,7},{16,8},{17,9... | collective-permute-start | bytes 2359304 | tf_op jit(solution)/shard_map/ppermute | solution.py:20
  249.1 45.7 %collective-permute-start.16 = (bf16[2,1,1,1,64,1536]{5,4,3,2,1,0:T(8,128)(2,1)S(1)}, bf16[2,1,1,1,64,1536]{5,4,3,2,1,0:T(8,128)(2,1)S(1)}, u32[]{:S(2)}, u32[]{:S(2)}) collective-permute-start(bf16[2,1,1,1,64,1536]{5,4,3,2,1,0:T(8,128)(2,1)S(1)} %copy-done.129), channel_id=1, source_target_pairs={{9,0},{10,1},{11,2},{12,3},{13,4},{14,5},{15,6},{16,7},{17,8},{18,... | collective-permute-start | bytes 1179656 | tf_op jit(solution)/shard_map/ppermute | solution.py:20
  251.8 70.0 %collective-permute-start.17 = (bf16[2,1,1,1,64,1536]{5,4,3,2,1,0:T(8,128)(2,1)}, bf16[2,1,1,1,64,1536]{5,4,3,2,1,0:T(8,128)(2,1)S(1)}, u32[]{:S(2)}, u32[]{:S(2)}) collective-permute-start(bf16[2,1,1,1,64,1536]{5,4,3,2,1,0:T(8,128)(2,1)} %get-tuple-element.1100), channel_id=1, source_target_pairs={{11,0},{12,1},{13,2},{14,3},{15,4},{16,5},{17,6},{18,7},{19,8},{20... | collective-permute-start | bytes 1179656 | tf_op jit(solution)/shard_map/ppermute | solution.py:20
  254.6 76.3 %collective-permute-start.18 = (bf16[2,1,1,2,64,1536]{5,4,3,2,1,0:T(8,128)(2,1)}, bf16[2,1,1,2,64,1536]{5,4,3,2,1,0:T(8,128)(2,1)S(1)}, u32[]{:S(2)}, u32[]{:S(2)}) collective-permute-start(bf16[2,1,1,2,64,1536]{5,4,3,2,1,0:T(8,128)(2,1)} %pad_maximum_fusion), channel_id=1, source_target_pairs={{12,0},{13,1},{14,2},{15,3},{16,4},{17,5},{18,6},{19,7},{20,8},{21... | collective-permute-start | bytes 2359304 | tf_op jit(solution)/shard_map/ppermute | solution.py:20
  289.2 74.9 %collective-permute-start.19 = (bf16[2,1,1,1,64,1536]{5,4,3,2,1,0:T(8,128)(2,1)S(1)}, bf16[2,1,1,1,64,1536]{5,4,3,2,1,0:T(8,128)(2,1)S(1)}, u32[]{:S(2)}, u32[]{:S(2)}) collective-permute-start(bf16[2,1,1,1,64,1536]{5,4,3,2,1,0:T(8,128)(2,1)S(1)} %copy-done.129), channel_id=1, source_target_pairs={{13,0},{14,1},{15,2},{16,3},{17,4},{18,5},{19,6},{20,7},{21,8},{22... | collective-permute-start | bytes 1179656 | tf_op jit(solution)/shard_map/ppermute | solution.py:20
  291.9 191.9 %collective-permute-start.21 = (bf16[2,1,1,2,64,1536]{5,4,3,2,1,0:T(8,128)(2,1)S(1)}, bf16[2,1,1,2,64,1536]{5,4,3,2,1,0:T(8,128)(2,1)}, u32[]{:S(2)}, u32[]{:S(2)}) collective-permute-start(bf16[2,1,1,2,64,1536]{5,4,3,2,1,0:T(8,128)(2,1)S(1)} %copy-done.53), channel_id=1, source_target_pairs={{0,12},{1,13},{2,14},{3,15},{4,16},{5,17},{6,18},{7,19},{8,20},{9,... | collective-permute-start | bytes 2359304 | tf_op jit(solution)/shard_map/ppermute | solution.py:20
  294.8 198.2 %collective-permute-start.23 = (bf16[2,1,1,1,64,1536]{5,4,3,2,1,0:T(8,128)(2,1)}, bf16[2,1,1,1,64,1536]{5,4,3,2,1,0:T(8,128)(2,1)}, u32[]{:S(2)}, u32[]{:S(2)}) collective-permute-start(bf16[2,1,1,1,64,1536]{5,4,3,2,1,0:T(8,128)(2,1)} %get-tuple-element.1098), channel_id=1, source_target_pairs={{0,9},{1,10},{2,11},{3,12},{4,13},{5,14},{6,15},{7,16},{8,17},{9,1... | collective-permute-start | bytes 1179656 | tf_op jit(solution)/shard_map/ppermute | solution.py:20
  321.8 180.2 %collective-permute-start.24 = (bf16[2,1,1,2,64,1536]{5,4,3,2,1,0:T(8,128)(2,1)S(1)}, bf16[2,1,1,2,64,1536]{5,4,3,2,1,0:T(8,128)(2,1)}, u32[]{:S(2)}, u32[]{:S(2)}) collective-permute-start(bf16[2,1,1,2,64,1536]{5,4,3,2,1,0:T(8,128)(2,1)S(1)} %copy-done.53), channel_id=1, source_target_pairs={{0,8},{1,9},{2,10},{3,11},{4,12},{5,13},{6,14},{7,15},{8,16},{9,17... | collective-permute-start | bytes 2359304 | tf_op jit(solution)/shard_map/ppermute | solution.py:20
  330.9 157.6 %collective-permute-start.22 = (bf16[2,1,1,1,64,1536]{5,4,3,2,1,0:T(8,128)(2,1)}, bf16[2,1,1,1,64,1536]{5,4,3,2,1,0:T(8,128)(2,1)}, u32[]{:S(2)}, u32[]{:S(2)}) collective-permute-start(bf16[2,1,1,1,64,1536]{5,4,3,2,1,0:T(8,128)(2,1)} %get-tuple-element.1097), channel_id=1, source_target_pairs={{0,11},{1,12},{2,13},{3,14},{4,15},{5,16},{6,17},{7,18},{8,19},{9,... | collective-permute-start | bytes 1179656 | tf_op jit(solution)/shard_map/ppermute | solution.py:20
  364.0 145.7 %collective-permute-start.25 = (bf16[2,1,1,1,64,1536]{5,4,3,2,1,0:T(8,128)(2,1)}, bf16[2,1,1,1,64,1536]{5,4,3,2,1,0:T(8,128)(2,1)}, u32[]{:S(2)}, u32[]{:S(2)}) collective-permute-start(bf16[2,1,1,1,64,1536]{5,4,3,2,1,0:T(8,128)(2,1)} %get-tuple-element.1097), channel_id=1, source_target_pairs={{0,7},{1,8},{2,9},{3,10},{4,11},{5,12},{6,13},{7,14},{8,15},{9,16}... | collective-permute-start | bytes 1179656 | tf_op jit(solution)/shard_map/ppermute | solution.py:20
  483.8 53.2 %collective-permute-start.26 = (bf16[2,1,1,1,64,1536]{5,4,3,2,1,0:T(8,128)(2,1)}, bf16[2,1,1,1,64,1536]{5,4,3,2,1,0:T(8,128)(2,1)S(1)}, u32[]{:S(2)}, u32[]{:S(2)}) collective-permute-start(bf16[2,1,1,1,64,1536]{5,4,3,2,1,0:T(8,128)(2,1)} %get-tuple-element.1098), channel_id=1, source_target_pairs={{0,5},{1,6},{2,7},{3,8},{4,9},{5,10},{6,11},{7,12},{8,13},{9,14},{... | collective-permute-start | bytes 1179656 | tf_op jit(solution)/shard_map/ppermute | solution.py:20
  488.5 52.6 %collective-permute-start.27 = (bf16[2,1,1,2,64,1536]{5,4,3,2,1,0:T(8,128)(2,1)S(1)}, bf16[2,1,1,2,64,1536]{5,4,3,2,1,0:T(8,128)(2,1)S(1)}, u32[]{:S(2)}, u32[]{:S(2)}) collective-permute-start(bf16[2,1,1,2,64,1536]{5,4,3,2,1,0:T(8,128)(2,1)S(1)} %copy-done.53), channel_id=1, source_target_pairs={{0,4},{1,5},{2,6},{3,7},{4,8},{5,9},{6,10},{7,11},{8,12},{9,13},{1... | collective-permute-start | bytes 2359304 | tf_op jit(solution)/shard_map/ppermute | solution.py:20
  493.0 63.8 %collective-permute-start.28 = (bf16[2,1,1,1,64,1536]{5,4,3,2,1,0:T(8,128)(2,1)}, bf16[2,1,1,1,64,1536]{5,4,3,2,1,0:T(8,128)(2,1)S(1)}, u32[]{:S(2)}, u32[]{:S(2)}) collective-permute-start(bf16[2,1,1,1,64,1536]{5,4,3,2,1,0:T(8,128)(2,1)} %get-tuple-element.1097), channel_id=1, source_target_pairs={{0,3},{1,4},{2,5},{3,6},{4,7},{5,8},{6,9},{7,10},{8,11},{9,12},{10... | collective-permute-start | bytes 1179656 | tf_op jit(solution)/shard_map/ppermute | solution.py:20
  502.0 94.7 %collective-permute-start.29 = (bf16[2,1,1,1,64,1536]{5,4,3,2,1,0:T(8,128)(2,1)}, bf16[2,1,1,1,64,1536]{5,4,3,2,1,0:T(8,128)(2,1)S(1)}, u32[]{:S(2)}, u32[]{:S(2)}) collective-permute-start(bf16[2,1,1,1,64,1536]{5,4,3,2,1,0:T(8,128)(2,1)} %get-tuple-element.1098), channel_id=1, source_target_pairs={{0,1},{1,2},{2,3},{3,4},{4,5},{5,6},{6,7},{7,8},{8,9},{9,10},{10,1... | collective-permute-start | bytes 1179656 | tf_op jit(solution)/shard_map/ppermute | solution.py:20
  509.7 90.0 %collective-permute-start.30 = (bf16[2,1,1,1,64,1536]{5,4,3,2,1,0:T(8,128)(2,1)}, bf16[2,1,1,1,64,1536]{5,4,3,2,1,0:T(8,128)(2,1)S(1)}, u32[]{:S(2)}, u32[]{:S(2)}) collective-permute-start(bf16[2,1,1,1,64,1536]{5,4,3,2,1,0:T(8,128)(2,1)} %get-tuple-element.1097), channel_id=1, source_target_pairs={{1,0},{2,1},{3,2},{4,3},{5,4},{6,5},{7,6},{8,7},{9,8},{10,9},{11,1... | collective-permute-start | bytes 1179656 | tf_op jit(solution)/shard_map/ppermute | solution.py:20
  537.0 84.5 %collective-permute-start.31 = (bf16[2,1,1,1,64,1536]{5,4,3,2,1,0:T(8,128)(2,1)}, bf16[2,1,1,1,64,1536]{5,4,3,2,1,0:T(8,128)(2,1)S(1)}, u32[]{:S(2)}, u32[]{:S(2)}) collective-permute-start(bf16[2,1,1,1,64,1536]{5,4,3,2,1,0:T(8,128)(2,1)} %get-tuple-element.1098), channel_id=1, source_target_pairs={{3,0},{4,1},{5,2},{6,3},{7,4},{8,5},{9,6},{10,7},{11,8},{12,9},{13... | collective-permute-start | bytes 1179656 | tf_op jit(solution)/shard_map/ppermute | solution.py:20
  541.1 85.8 %collective-permute-start.32 = (bf16[2,1,1,2,64,1536]{5,4,3,2,1,0:T(8,128)(2,1)S(1)}, bf16[2,1,1,2,64,1536]{5,4,3,2,1,0:T(8,128)(2,1)S(1)}, u32[]{:S(2)}, u32[]{:S(2)}) collective-permute-start(bf16[2,1,1,2,64,1536]{5,4,3,2,1,0:T(8,128)(2,1)S(1)} %copy-done.53), channel_id=1, source_target_pairs={{4,0},{5,1},{6,2},{7,3},{8,4},{9,5},{10,6},{11,7},{12,8},{13,9},{1... | collective-permute-start | bytes 2359304 | tf_op jit(solution)/shard_map/ppermute | solution.py:20
  556.8 75.2 %collective-permute-start.33 = (bf16[2,1,1,1,64,1536]{5,4,3,2,1,0:T(8,128)(2,1)}, bf16[2,1,1,1,64,1536]{5,4,3,2,1,0:T(8,128)(2,1)S(1)}, u32[]{:S(2)}, u32[]{:S(2)}) collective-permute-start(bf16[2,1,1,1,64,1536]{5,4,3,2,1,0:T(8,128)(2,1)} %get-tuple-element.1097), channel_id=1, source_target_pairs={{5,0},{6,1},{7,2},{8,3},{9,4},{10,5},{11,6},{12,7},{13,8},{14,9},{... | collective-permute-start | bytes 1179656 | tf_op jit(solution)/shard_map/ppermute | solution.py:20
  596.7 38.6 %collective-permute-start.34 = (bf16[2,1,1,1,64,1536]{5,4,3,2,1,0:T(8,128)(2,1)}, bf16[2,1,1,1,64,1536]{5,4,3,2,1,0:T(8,128)(2,1)S(1)}, u32[]{:S(2)}, u32[]{:S(2)}) collective-permute-start(bf16[2,1,1,1,64,1536]{5,4,3,2,1,0:T(8,128)(2,1)} %get-tuple-element.1098), channel_id=1, source_target_pairs={{7,0},{8,1},{9,2},{10,3},{11,4},{12,5},{13,6},{14,7},{15,8},{16,9}... | collective-permute-start | bytes 1179656 | tf_op jit(solution)/shard_map/ppermute | solution.py:20
  599.7 41.4 %collective-permute-start.35 = (bf16[2,1,1,2,64,1536]{5,4,3,2,1,0:T(8,128)(2,1)S(1)}, bf16[2,1,1,2,64,1536]{5,4,3,2,1,0:T(8,128)(2,1)S(1)}, u32[]{:S(2)}, u32[]{:S(2)}) collective-permute-start(bf16[2,1,1,2,64,1536]{5,4,3,2,1,0:T(8,128)(2,1)S(1)} %copy-done.53), channel_id=1, source_target_pairs={{8,0},{9,1},{10,2},{11,3},{12,4},{13,5},{14,6},{15,7},{16,8},{17,9... | collective-permute-start | bytes 2359304 | tf_op jit(solution)/shard_map/ppermute | solution.py:20
  621.5 52.2 %collective-permute-start.36 = (bf16[2,1,1,1,64,1536]{5,4,3,2,1,0:T(8,128)(2,1)}, bf16[2,1,1,1,64,1536]{5,4,3,2,1,0:T(8,128)(2,1)S(1)}, u32[]{:S(2)}, u32[]{:S(2)}) collective-permute-start(bf16[2,1,1,1,64,1536]{5,4,3,2,1,0:T(8,128)(2,1)} %get-tuple-element.1097), channel_id=1, source_target_pairs={{9,0},{10,1},{11,2},{12,3},{13,4},{14,5},{15,6},{16,7},{17,8},{18,... | collective-permute-start | bytes 1179656 | tf_op jit(solution)/shard_map/ppermute | solution.py:20
  626.9 59.9 %collective-permute-start.37 = (bf16[2,1,1,1,64,1536]{5,4,3,2,1,0:T(8,128)(2,1)}, bf16[2,1,1,1,64,1536]{5,4,3,2,1,0:T(8,128)(2,1)S(1)}, u32[]{:S(2)}, u32[]{:S(2)}) collective-permute-start(bf16[2,1,1,1,64,1536]{5,4,3,2,1,0:T(8,128)(2,1)} %get-tuple-element.1098), channel_id=1, source_target_pairs={{11,0},{12,1},{13,2},{14,3},{15,4},{16,5},{17,6},{18,7},{19,8},{20... | collective-permute-start | bytes 1179656 | tf_op jit(solution)/shard_map/ppermute | solution.py:20
  632.1 68.0 %collective-permute-start.38 = (bf16[2,1,1,2,64,1536]{5,4,3,2,1,0:T(8,128)(2,1)S(1)}, bf16[2,1,1,2,64,1536]{5,4,3,2,1,0:T(8,128)(2,1)S(1)}, u32[]{:S(2)}, u32[]{:S(2)}) collective-permute-start(bf16[2,1,1,2,64,1536]{5,4,3,2,1,0:T(8,128)(2,1)S(1)} %copy-done.53), channel_id=1, source_target_pairs={{12,0},{13,1},{14,2},{15,3},{16,4},{17,5},{18,6},{19,7},{20,8},{21... | collective-permute-start | bytes 2359304 | tf_op jit(solution)/shard_map/ppermute | solution.py:20
  635.4 71.0 %collective-permute-start.39 = (bf16[2,1,1,1,64,1536]{5,4,3,2,1,0:T(8,128)(2,1)}, bf16[2,1,1,1,64,1536]{5,4,3,2,1,0:T(8,128)(2,1)S(1)}, u32[]{:S(2)}, u32[]{:S(2)}) collective-permute-start(bf16[2,1,1,1,64,1536]{5,4,3,2,1,0:T(8,128)(2,1)} %get-tuple-element.1097), channel_id=1, source_target_pairs={{13,0},{14,1},{15,2},{16,3},{17,4},{18,5},{19,6},{20,7},{21,8},{22... | collective-permute-start | bytes 1179656 | tf_op jit(solution)/shard_map/ppermute | solution.py:20
  641.1 220.2 %collective-permute-start.41 = (f32[2,1,1,2,64,12]{4,5,3,2,1,0:T(8,128)S(1)}, f32[2,1,1,2,64,12]{4,5,3,2,1,0:T(8,128)S(1)}, u32[]{:S(2)}, u32[]{:S(2)}) collective-permute-start(f32[2,1,1,2,64,12]{4,5,3,2,1,0:T(8,128)S(1)} %pad_maximum_fusion.2), channel_id=1, source_target_pairs={{0,12},{1,13},{2,14},{3,15},{4,16},{5,17},{6,18},{7,19},{8,20},{9,... | collective-permute-start | bytes 36872 | tf_op jit(solution)/shard_map/ppermute | solution.py:20
  673.7 173.7 %collective-permute-start.40 = (f32[2,1,1,1,64,12]{4,5,3,2,1,0:T(8,128)}, f32[2,1,1,1,64,12]{4,5,3,2,1,0:T(8,128)}, u32[]{:S(2)}, u32[]{:S(2)}) collective-permute-start(f32[2,1,1,1,64,12]{4,5,3,2,1,0:T(8,128)} %get-tuple-element.1158), channel_id=1, source_target_pairs={{0,13},{1,14},{2,15},{3,16},{4,17},{5,18},{6,19},{7,20},{8,21},{9,... | collective-permute-start | bytes 18440 | tf_op jit(solution)/shard_map/ppermute | solution.py:20
  686.9 179.9 %collective-permute-start.43 = (f32[2,1,1,1,64,12]{4,5,3,2,1,0:T(8,128)}, f32[2,1,1,1,64,12]{4,5,3,2,1,0:T(8,128)S(1)}, u32[]{:S(2)}, u32[]{:S(2)}) collective-permute-start(f32[2,1,1,1,64,12]{4,5,3,2,1,0:T(8,128)} %get-tuple-element.1158), channel_id=1, source_target_pairs={{0,9},{1,10},{2,11},{3,12},{4,13},{5,14},{6,15},{7,16},{8,17},{9,1... | collective-permute-start | bytes 18440 | tf_op jit(solution)/shard_map/ppermute | solution.py:20
  700.0 173.9 %collective-permute-start.44 = (f32[2,1,1,2,64,12]{4,5,3,2,1,0:T(8,128)S(1)}, f32[2,1,1,2,64,12]{4,5,3,2,1,0:T(8,128)}, u32[]{:S(2)}, u32[]{:S(2)}) collective-permute-start(f32[2,1,1,2,64,12]{4,5,3,2,1,0:T(8,128)S(1)} %pad_maximum_fusion.2), channel_id=1, source_target_pairs={{0,8},{1,9},{2,10},{3,11},{4,12},{5,13},{6,14},{7,15},{8,16},{9,17... | collective-permute-start | bytes 36872 | tf_op jit(solution)/shard_map/ppermute | solution.py:20
  847.4 29.8 %collective-permute-start.45 = (f32[2,1,1,1,64,12]{4,5,3,2,1,0:T(8,128)}, f32[2,1,1,1,64,12]{4,5,3,2,1,0:T(8,128)S(1)}, u32[]{:S(2)}, u32[]{:S(2)}) collective-permute-start(f32[2,1,1,1,64,12]{4,5,3,2,1,0:T(8,128)} %get-tuple-element.1157), channel_id=1, source_target_pairs={{0,7},{1,8},{2,9},{3,10},{4,11},{5,12},{6,13},{7,14},{8,15},{9,16}... | collective-permute-start | bytes 18440 | tf_op jit(solution)/shard_map/ppermute | solution.py:20
  866.7 27.8 %collective-permute-start.48 = (f32[2,1,1,1,64,12]{4,5,3,2,1,0:T(8,128)}, f32[2,1,1,1,64,12]{4,5,3,2,1,0:T(8,128)S(1)}, u32[]{:S(2)}, u32[]{:S(2)}) collective-permute-start(f32[2,1,1,1,64,12]{4,5,3,2,1,0:T(8,128)} %get-tuple-element.1157), channel_id=1, source_target_pairs={{0,3},{1,4},{2,5},{3,6},{4,7},{5,8},{6,9},{7,10},{8,11},{9,12},{10... | collective-permute-start | bytes 18440 | tf_op jit(solution)/shard_map/ppermute | solution.py:20
  873.9 30.7 %collective-permute-start.49 = (f32[2,1,1,1,64,12]{4,5,3,2,1,0:T(8,128)}, f32[2,1,1,1,64,12]{4,5,3,2,1,0:T(8,128)S(1)}, u32[]{:S(2)}, u32[]{:S(2)}) collective-permute-start(f32[2,1,1,1,64,12]{4,5,3,2,1,0:T(8,128)} %get-tuple-element.1158), channel_id=1, source_target_pairs={{0,1},{1,2},{2,3},{3,4},{4,5},{5,6},{6,7},{7,8},{8,9},{9,10},{10,1... | collective-permute-start | bytes 18440 | tf_op jit(solution)/shard_map/ppermute | solution.py:20
  877.2 29.9 %collective-permute-start.50 = (f32[2,1,1,1,64,12]{4,5,3,2,1,0:T(8,128)}, f32[2,1,1,1,64,12]{4,5,3,2,1,0:T(8,128)S(1)}, u32[]{:S(2)}, u32[]{:S(2)}) collective-permute-start(f32[2,1,1,1,64,12]{4,5,3,2,1,0:T(8,128)} %get-tuple-element.1157), channel_id=1, source_target_pairs={{1,0},{2,1},{3,2},{4,3},{5,4},{6,5},{7,6},{8,7},{9,8},{10,9},{11,1... | collective-permute-start | bytes 18440 | tf_op jit(solution)/shard_map/ppermute | solution.py:20
  (184 other events, 7627.0 us)
where the time goes:
time: 1210 us; the launch traced here: 1190 us
  starting transfers between devices  328 us (27%)
  matrix products  324 us (27%)
  waiting for transfers between devices  217 us (18%)
  local copies, waits for them, and re-layouts  192 us (16%)
  blocking collectives  86.5 us (7%)
  other arithmetic  24.6 us (2%)
  between operations  15.4 us (1%)
    ppermute x60, starting transfers between devices, passed_along(): lax.ppermute(value, axis, [(source, source + steps) for source in range(i...  328 us
    dot_general x162, matrix products, product(): return jnp.einsum(form, left, right, preferred_element_type=jnp.float32)  324 us
    ppermute x60, waiting for transfers between devices, passed_along(): lax.ppermute(value, axis, [(source, source + steps) for source in range(i...  217 us
    psum x1, blocking collectives, on_device(): lax.psum((q_gain_part, k_gain_part), ('dp', 'seq'))  86.5 us
    scatter x78, local copies, waits for them, and re-layouts, direct_extend(): extended = extended.at[(slice(None),) + tuple((place(o, n) for o, n in zi...  51.2 us
    slice x6, local copies, waits for them, and re-layouts, window(): extended[1 + a:1 + a + grid_dims[0], 1 + b:1 + b + grid_dims[1], 1 + c:1...  35.5 us
  transfers between devices with their start and end apart: 60, of which 14 were waited for; matrix products, arithmetic and copies ran while one was open for 30% of the time, Pallas kernels for 0%

commit v1 on v0

v1 whole, which is shorter than its diff:
```python
import functools

import jax
import jax.numpy as jnp
from jax import lax
from jax.experimental import pallas as pl
from jax.experimental.pallas import tpu as pltpu
from jax.sharding import Mesh
from jax.sharding import PartitionSpec as P

HEADS = 12
HD = 128
TILE = 64
PAIR = 2 * TILE
GROUP = 16
HALF = 8
COLS = 4
WIDE = 8
EXTRA = 16
EPSILON = 1e-06
SCALE = HD ** (-0.5)
SCALE_LOG2E = SCALE * 1.4426950408889634
F32 = jnp.float32
BF16 = jnp.bfloat16
VMEM_BYTES = 48 * 1024 * 1024

SLAB = 2 * TILE
COLUMN = 4 * SLAB
PARTS = ((0, SLAB, 0, SLAB), (SLAB, 2 * SLAB, 0, 2 * SLAB), (3 * SLAB, SLAB, SLAB, SLAB))


def nt(left, right):
    return lax.dot_general(left, right, (((1,), (1,)), ((), ())), preferred_element_type=F32)


def nn(left, right):
    return lax.dot_general(left, right, (((1,), (0,)), ((), ())), preferred_element_type=F32)


def inverse_rms(inputs):
    return lax.rsqrt(jnp.mean(inputs * inputs, axis=-1, keepdims=True) + EPSILON)


def norm_back(inputs, inverse, gain, cotangent):
    scaled = cotangent * gain
    mean = jnp.mean(inputs * scaled, axis=-1, keepdims=True)
    return inverse * scaled - inputs * (inverse * inverse * inverse * mean)


def pack_kernel(first_ref, second_ref, out_ref):
    for head in range(HEADS):
        lanes = slice(head * HD, (head + 1) * HD)
        out_ref[head, 0] = first_ref[0, :, lanes]
        out_ref[head, 1] = second_ref[0, :, lanes]
    for head in range(HEADS, GROUP):
        out_ref[head] = jnp.zeros(out_ref.shape[1:], out_ref.dtype)


def pack(first, second):
    return pl.pallas_call(
        pack_kernel,
        out_shape=jax.ShapeDtypeStruct((GROUP, 2, PAIR, HD), BF16),
        name="pack",
        compiler_params=pltpu.CompilerParams(vmem_limit_bytes=VMEM_BYTES),
    )(first, second)


def attention_kernel(
    flags_ref,
    kv_ref,
    low_ref,
    high_ref,
    qd_ref,
    q_gain_ref,
    k_gain_ref,
    dq_ref,
    own_ref,
    to_low_ref,
    to_high_ref,
    kn,
    knt,
    vv,
    qn,
    dd,
    dk,
    dv,
    gains,
):
    q_gain = q_gain_ref[...]
    k_gain = k_gain_ref[...]

    def key_block(source, index, frame, row, col):
        raw = source[index, 0].astype(F32)
        normed = (raw * inverse_rms(raw) * k_gain).astype(BF16)
        for part in range(2):
            at = (2 * col + part) * COLUMN + frame * SLAB + row * TILE
            kn[at : at + TILE] = normed[part * TILE : (part + 1) * TILE]
            vv[at : at + TILE] = source[index, 1, part * TILE : (part + 1) * TILE]

    for row in range(2):
        for col in range(COLS):
            key_block(low_ref, row * COLS + col, 0, row, col)
            key_block(kv_ref, row * COLS + col, 1, row, col)
            key_block(kv_ref, HALF + row * COLS + col, 2, row, col)
            key_block(high_ref, row * COLS + col, 3, row, col)
    for block in range(WIDE * COLUMN // HD):
        rows = slice(block * HD, (block + 1) * HD)
        knt[:, rows] = kn[rows].T
    for frame in range(2):
        for row in range(2):
            for col in range(COLS):
                index = frame * HALF + row * COLS + col
                raw = qd_ref[index, 0].astype(F32)
                normed = (raw * inverse_rms(raw) * q_gain).astype(BF16)
                for part in range(2):
                    at = (2 * col + part) * 2 * SLAB + frame * SLAB + row * TILE
                    qn[at : at + TILE] = normed[part * TILE : (part + 1) * TILE]
                    dd[at : at + TILE] = qd_ref[index, 1, part * TILE : (part + 1) * TILE]
    dk[...] = jnp.zeros_like(dk)
    dv[...] = jnp.zeros_like(dv)
    gains[...] = jnp.zeros_like(gains)
    low_valid = flags_ref[0].astype(F32)
    high_valid = flags_ref[1].astype(F32)
    valid = (low_valid, None, high_valid)

    def column(w, steps):
        q_rows = pl.ds(pl.multiple_of(w * (2 * SLAB), 2 * SLAB), 2 * SLAB)
        q_tile = qn[q_rows]
        d_tile = dd[q_rows]
        pieces = []
        total = [jnp.zeros((1, SLAB), F32), jnp.zeros((1, SLAB), F32)]
        for step in steps:
            base = (w + step) * COLUMN
            for number, (first, count, q_first, q_count) in enumerate(PARTS):
                rows = pl.ds(pl.multiple_of(base + first, SLAB), count)
                queries = slice(q_first, q_first + q_count)
                weights = jnp.exp2(nt(kn[rows], q_tile[queries]) * SCALE_LOG2E)
                if valid[number] is not None:
                    weights = weights * valid[number]
                sums = jnp.sum(weights, axis=0, keepdims=True)
                for frame in range(2):
                    if q_first <= frame * SLAB < q_first + q_count:
                        at = frame * SLAB - q_first
                        total[frame] = total[frame] + sums[:, at : at + SLAB]
                weight_grad = nt(vv[rows], d_tile[queries])
                pieces.append((rows, queries, weights, weight_grad))
        reciprocal = 1.0 / jnp.concatenate(total, axis=1)
        dots = [jnp.zeros((1, SLAB), F32), jnp.zeros((1, SLAB), F32)]
        chances = []
        for rows, queries, weights, weight_grad in pieces:
            chance = weights * reciprocal[:, queries]
            rounded = chance.astype(BF16)
            sums = jnp.sum(rounded.astype(F32) * weight_grad, axis=0, keepdims=True)
            for frame in range(2):
                if queries.start <= frame * SLAB < queries.stop:
                    at = frame * SLAB - queries.start
                    dots[frame] = dots[frame] + sums[:, at : at + SLAB]
            chances.append(chance)
            dv[rows] += nn(rounded, d_tile[queries])
        row_dot = jnp.concatenate(dots, axis=1)
        query_grad = [jnp.zeros((HD, SLAB), F32), jnp.zeros((HD, SLAB), F32)]
        for (rows, queries, _, weight_grad), chance in zip(pieces, chances):
            score_grad = (chance * (weight_grad - row_dot[:, queries])).astype(BF16)
            dk[rows] += nn(score_grad, q_tile[queries])
            part_grad = nn(knt[:, rows], score_grad)
            for frame in range(2):
                if queries.start <= frame * SLAB < queries.stop:
                    at = frame * SLAB - queries.start
                    query_grad[frame] = query_grad[frame] + part_grad[:, at : at + SLAB]
        col = w // 2
        place = pl.ds(pl.multiple_of((w % 2) * TILE, TILE), TILE)
        for frame in range(2):
            grad = query_grad[frame].T * SCALE
            for row in range(2):
                index = frame * HALF + row * COLS + col
                raw = qd_ref[index, 0, place].astype(F32)
                inverse = inverse_rms(raw)
                part = grad[row * TILE : (row + 1) * TILE]
                gains[0:8] += jnp.sum((part * raw * inverse).reshape(-1, 8, HD), axis=0)
                dq_ref[index, place] = norm_back(raw, inverse, q_gain, part).astype(BF16)

    column(0, (0, 1))

    def middle(w, carry):
        column(w, (-1, 0, 1))
        return carry

    lax.fori_loop(1, WIDE - 1, middle, 0)
    column(WIDE - 1, (-1, 0))

    def finish(source, index, frame, row, col):
        raw = source[index, 0].astype(F32)
        inverse = inverse_rms(raw)
        keys, vals = [], []
        for part in range(2):
            at = (2 * col + part) * COLUMN + frame * SLAB + row * TILE
            keys.append(dk[at : at + TILE])
            vals.append(dv[at : at + TILE])
        key_grad = jnp.concatenate(keys, axis=0) * SCALE
        gains[8:16] += jnp.sum((key_grad * raw * inverse).reshape(-1, 8, HD), axis=0)
        return key_grad, jnp.concatenate(vals, axis=0)

    for row in range(2):
        for col in range(COLS):
            index = row * COLS + col
            for source, target, frame in ((low_ref, to_low_ref, 0), (high_ref, to_high_ref, 3)):
                key_grad, value_grad = finish(source, index, frame, row, col)
                target[index, 0] = key_grad.astype(BF16)
                target[index, 1] = value_grad.astype(BF16)
            for frame in (1, 2):
                here = (frame - 1) * HALF + index
                key_grad, value_grad = finish(kv_ref, here, frame, row, col)
                own_ref[here, 0] = key_grad
                own_ref[here, 1] = value_grad

    owner = flags_ref[2] > 0
    lines = []
    for first in (0, 8):
        line = jnp.sum(gains[first : first + 8], axis=0, keepdims=True)
        line = jnp.where(owner, line, 0.0)
        for _ in range(3):
            rounded = line.astype(BF16).astype(F32)
            lines.append(rounded)
            line = line - rounded
    lines.append(jnp.zeros((EXTRA - 6, HD), F32))
    block = jnp.concatenate(lines, axis=0).astype(BF16)
    for index in range(GROUP):
        dq_ref[index, PAIR : PAIR + EXTRA] = block


def attention(flags, kv, low, high, qd, q_gain, k_gain):
    rows = WIDE * COLUMN
    vmem = pl.BlockSpec(memory_space=pltpu.VMEM)
    products = 5 * 44 * SLAB * SLAB * 6 * HD
    return pl.pallas_call(
        attention_kernel,
        in_specs=[pl.BlockSpec(memory_space=pltpu.SMEM)] + [vmem] * 6,
        out_specs=[vmem] * 4,
        out_shape=[
            jax.ShapeDtypeStruct((GROUP, PAIR + EXTRA, HD), BF16),
            jax.ShapeDtypeStruct((GROUP, 2, PAIR, HD), F32),
            jax.ShapeDtypeStruct((HALF, 2, PAIR, HD), BF16),
            jax.ShapeDtypeStruct((HALF, 2, PAIR, HD), BF16),
        ],
        scratch_shapes=[
            pltpu.VMEM((rows, HD), BF16),
            pltpu.VMEM((HD, rows), BF16),
            pltpu.VMEM((rows, HD), BF16),
            pltpu.VMEM((rows // 2, HD), BF16),
            pltpu.VMEM((rows // 2, HD), BF16),
            pltpu.VMEM((rows, HD), F32),
            pltpu.VMEM((rows, HD), F32),
            pltpu.VMEM((16, HD), F32),
        ],
        name="attention",
        cost_estimate=pl.CostEstimate(flops=products, bytes_accessed=8 << 20, transcendentals=4 << 20),
        compiler_params=pltpu.CompilerParams(vmem_limit_bytes=VMEM_BYTES),
    )(flags, kv, low, high, qd, q_gain, k_gain)


def finish_kernel(kv_ref, own_ref, low_ref, high_ref, k_gain_ref, out_ref):
    k_gain = k_gain_ref[...]
    for index in range(GROUP):
        arrived = low_ref if index < HALF else high_ref
        raw = kv_ref[index, 0].astype(F32)
        key_grad = own_ref[index, 0] + arrived[index % HALF, 0].astype(F32)
        value_grad = own_ref[index, 1] + arrived[index % HALF, 1].astype(F32)
        out_ref[index, 0] = norm_back(raw, inverse_rms(raw), k_gain, key_grad).astype(BF16)
        out_ref[index, 1] = value_grad.astype(BF16)


def finish(kv, own, low, high, k_gain):
    return pl.pallas_call(
        finish_kernel,
        out_shape=jax.ShapeDtypeStruct((GROUP, 2, PAIR, HD), BF16),
        name="finish",
        compiler_params=pltpu.CompilerParams(vmem_limit_bytes=VMEM_BYTES),
    )(kv, own, low, high, k_gain)


def unpack_query_kernel(in_ref, out_ref, gains_ref):
    for head in range(HEADS):
        out_ref[0, :, head * HD : (head + 1) * HD] = in_ref[head, :PAIR]
    total = in_ref[0, PAIR : PAIR + EXTRA].astype(F32)
    for index in range(1, GROUP):
        total = total + in_ref[index, PAIR : PAIR + EXTRA].astype(F32)
    gains_ref[...] = total


def unpack_query(arrived):
    return pl.pallas_call(
        unpack_query_kernel,
        out_shape=[
            jax.ShapeDtypeStruct((1, PAIR, HEADS * HD), BF16),
            jax.ShapeDtypeStruct((EXTRA, HD), F32),
        ],
        name="unpack_query",
        compiler_params=pltpu.CompilerParams(vmem_limit_bytes=VMEM_BYTES),
    )(arrived)


def unpack_kernel(in_ref, key_ref, value_ref):
    for head in range(HEADS):
        key_ref[0, :, head * HD : (head + 1) * HD] = in_ref[head, 0]
        value_ref[0, :, head * HD : (head + 1) * HD] = in_ref[head, 1]


def unpack(arrived):
    return pl.pallas_call(
        unpack_kernel,
        out_shape=[jax.ShapeDtypeStruct((1, PAIR, HEADS * HD), BF16)] * 2,
        name="unpack",
        compiler_params=pltpu.CompilerParams(vmem_limit_bytes=VMEM_BYTES),
    )(arrived)


def swap(array, axis):
    return lax.all_to_all(array, axis, 0, 0)


def on_device(blocks, q_raw, k_raw, values, d_out, q_gain, k_gain):
    block = lax.axis_index("x")
    member = lax.axis_index("g")
    flags = jnp.stack([block > 0, block < blocks - 1, member < HEADS]).astype(jnp.int32)
    up = [(source, source + 1) for source in range(blocks - 1)]
    down = [(source + 1, source) for source in range(blocks - 1)]
    q_line = q_gain.reshape(1, HD)
    k_line = k_gain.reshape(1, HD)

    kv = swap(pack(k_raw, values), "g")
    low = lax.ppermute(kv[HALF:], "x", up)
    high = lax.ppermute(kv[:HALF], "x", down)
    qd = swap(pack(q_raw, d_out), "g")
    dq, own, to_low, to_high = attention(flags, kv, low, high, qd, q_line, k_line)
    from_low = lax.ppermute(to_high, "x", up)
    from_high = lax.ppermute(to_low, "x", down)
    q_grad, sums = unpack_query(swap(dq, "g"))
    grads = finish(kv, own, from_low, from_high, k_line)
    k_grad, v_grad = unpack(swap(grads, "g"))
    sums = jnp.stack([jnp.sum(sums[0:3], axis=0), jnp.sum(sums[3:6], axis=0)])
    count = lax.axis_size("dp") * blocks
    sums = swap(jnp.broadcast_to(sums[None], (count, 2, HD)), ("dp", "x"))
    sums = jnp.sum(sums, axis=0)
    return (q_grad, k_grad, v_grad, sums[0], sums[1])


def solution(mesh):
    videos, seq = mesh.devices.shape
    blocks = seq // GROUP
    split = Mesh(mesh.devices.reshape(videos, blocks, GROUP), ("dp", "x", "g"))
    tokens = P("dp", ("x", "g"), None)
    return jax.shard_map(
        functools.partial(on_device, blocks),
        mesh=split,
        in_specs=(tokens, tokens, tokens, tokens, P(), P()),
        out_specs=(tokens, tokens, tokens, P(), P()),
        check_vma=False,
    )
```

time: 1210 us -> 161 us (0.13); the launches traced: 1190 us -> 160 us
  matrix products: 324 us -> 0 us
  starting transfers between devices: 328 us -> 41.5 us
  local copies, waits for them, and re-layouts: 192 us -> 8.4 us
  waiting for transfers between devices: 217 us -> 87 us
  blocking collectives: 86.5 us -> 0 us
  other arithmetic: 24.6 us -> 0.13 us
  Pallas kernels: 0 us -> 22 us
  between operations: 15.4 us -> 0.77 us
    dot_general x162 -> x0, matrix products: 324 us -> none  [product(): return jnp.einsum(form, left, right, preferred_element_type=jnp.float32)]
    ppermute x60 -> x4, starting transfers between devices: 328 us -> 11.7 us  [the longest x1 3.41 us: on_device(): from_low = lax.ppermute(to_high, 'x', up)]
    ppermute x60 -> x4, waiting for transfers between devices: 217 us -> 0.01 us  [the longest x1 0.01 us: on_device(): high = lax.ppermute(kv[:HALF], 'x', down)]
    all_to_all x0 -> x5, waiting for transfers between devices: none -> 87 us  [swap(): return lax.all_to_all(array, axis, 0, 0)]
    psum x1 -> x0, blocking collectives: 86.5 us -> none  [on_device(): lax.psum((q_gain_part, k_gain_part), ('dp', 'seq'))]
    scatter x81 -> x0, local copies, waits for them, and re-layouts: 66.8 us -> none  [the longest x78 51.2 us: direct_extend(): extended = extended.at[(slice(None),) + tuple((place(o, n) for o, n in zi...]
    another operation x4 -> x0, local copies, waits for them, and re-layouts: 54.5 us -> none  [the longest x1 13.6 us: on_device(): value_ext = pair_ext[1].reshape(ext_shape)]
    slice x10 -> x1, local copies, waits for them, and re-layouts: 52.6 us -> 1.05 us  [on_device(): high = lax.ppermute(kv[:HALF], 'x', down)]
  transfers between devices with their start and end apart: 60 -> 9, of which waited for: 14 -> 5; matrix products, arithmetic and copies ran while one was open for 30% -> 1% of each run, Pallas kernels for 0% -> 2%
where the time goes in v1:
time: 161 us; the launch traced here: 160 us
  waiting for transfers between devices  87 us (54%)
  starting transfers between devices  41.5 us (26%)
  Pallas kernels  22 us (14%)
  local copies, waits for them, and re-layouts  8.4 us (5%)
    all_to_all x5, waiting for transfers between devices, swap(): return lax.all_to_all(array, axis, 0, 0)  87 us
    all_to_all x5, starting transfers between devices, swap(): return lax.all_to_all(array, axis, 0, 0)  29.8 us
    pallas_call x1, Pallas kernels, attention(): pl.pallas_call(attention_kernel, in_specs=[pl.BlockSpec(memory_space=pltp...  16.2 us
    unnamed x20, local copies, waits for them, and re-layouts  6.22 us
    ppermute x1, starting transfers between devices, on_device(): from_low = lax.ppermute(to_high, 'x', up)  3.41 us
    ppermute x1, starting transfers between devices, on_device(): low = lax.ppermute(kv[HALF:], 'x', up)  3.4 us
  transfers between devices with their start and end apart: 9, of which 5 were waited for; matrix products, arithmetic and copies ran while one was open for 1% of the time, Pallas kernels for 2%

profile of v1, /device:TPU:2, one launch (start us, length us, event | category | flops | bytes accessed | tf_op | source)
XLA Modules:
  0.0 159.9 jit_solution(8226061260740126153)
XLA Ops:
  0.6 0.0 copy-start.1
  0.6 1.0 copy-done.1
  1.6 0.0 copy-start.2
  1.6 1.0 copy-done.2
  2.6 0.0 copy-start.3
  2.6 0.0 copy-start.4
  2.6 1.1 pack.2
  3.8 9.6 %all-to-all-start = ((bf16[16,2,128,128]{3,2,1,0:T(8,128)(2,1)}), bf16[16,2,128,128]{3,2,1,0:T(8,128)(2,1)S(1)}, u32[]{:S(2)}, u32[]{:S(2)}) async-start(bf16[16,2,128,128]{3,2,1,0:T(8,128)(2,1)} %pack.2), calls=%async_computation | async-start | bytes 2097152 | tf_op jit(solution)/shard_map/all_to_all | solution.py:318
  13.4 0.0 copy-done.3
  13.4 0.0 copy-done.4
  13.4 1.2 pack.3
  14.5 0.0 copy-start.5
  14.5 0.0 copy-start.9
  14.5 25.9 %all-to-all-done.kv_ref = bf16[16,2,128,128]{3,2,1,0:T(8,128)(2,1)S(1)} async-done(((bf16[16,2,128,128]{3,2,1,0:T(8,128)(2,1)}), bf16[16,2,128,128]{3,2,1,0:T(8,128)(2,1)S(1)}, u32[]{:S(2)}, u32[]{:S(2)}) %all-to-all-start) | async-done | bytes 1048608 | tf_op jit(solution)/shard_map/all_to_all | solution.py:318
  40.4 4.4 %all-to-all-start.1 = ((bf16[16,2,128,128]{3,2,1,0:T(8,128)(2,1)}), bf16[16,2,128,128]{3,2,1,0:T(8,128)(2,1)S(1)}, u32[]{:S(2)}, u32[]{:S(2)}) async-start(bf16[16,2,128,128]{3,2,1,0:T(8,128)(2,1)} %pack.3), calls=%async_computation.1 | async-start | bytes 2097152 | tf_op jit(solution)/shard_map/all_to_all | solution.py:318
  44.9 1.0 fusion
  45.9 2.4 %collective-permute-start.1 = (bf16[8,2,128,128]{3,2,1,0:T(8,128)(2,1)}, bf16[8,2,128,128]{3,2,1,0:T(8,128)(2,1)S(1)}, u32[]{:S(2)}, u32[]{:S(2)}) collective-permute-start(bf16[8,2,128,128]{3,2,1,0:T(8,128)(2,1)} %get-tuple-element.23), channel_id=1, source_target_pairs={{16,0},{32,16},{48,32},{17,1},{33,17},{49,33},{18,2},{34,18},{50,3... | collective-permute-start | bytes 1572872 | tf_op jit(solution)/shard_map/ppermute | solution.py:332
  48.3 3.4 %collective-permute-start = (bf16[8,2,128,128]{3,2,1,0:T(8,128)(2,1)}, bf16[8,2,128,128]{3,2,1,0:T(8,128)(2,1)S(1)}, u32[]{:S(2)}, u32[]{:S(2)}) collective-permute-start(bf16[8,2,128,128]{3,2,1,0:T(8,128)(2,1)} %get-tuple-element.24), channel_id=1, source_target_pairs={{0,16},{16,32},{32,48},{1,17},{17,33},{33,49},{2,18},{18,34},{34,5... | collective-permute-start | bytes 1572872 | tf_op jit(solution)/shard_map/ppermute | solution.py:331
  51.8 0.1 add_convert_fusion.flags_ref
  51.8 20.3 %all-to-all-done.1.qd_ref = bf16[16,2,128,128]{3,2,1,0:T(8,128)(2,1)S(1)} async-done(((bf16[16,2,128,128]{3,2,1,0:T(8,128)(2,1)}), bf16[16,2,128,128]{3,2,1,0:T(8,128)(2,1)S(1)}, u32[]{:S(2)}, u32[]{:S(2)}) %all-to-all-start.1) | async-done | bytes 1048608 | tf_op jit(solution)/shard_map/all_to_all | solution.py:318
  72.1 0.0 collective-permute-done.1.high_ref
  72.1 0.0 collective-permute-done.low_ref
  72.1 0.0 copy-start.6
  72.1 0.8 copy-done.6
  72.9 0.0 copy-done.5
  72.9 0.0 copy-done.9
  72.9 0.0 copy-start.7
  72.9 1.0 copy-done.7
  74.0 16.2 %attention.1 = (bf16[16,144,128]{2,1,0:T(8,128)(2,1)}, f32[16,2,128,128]{3,2,1,0:T(8,128)}, bf16[8,2,128,128]{3,2,1,0:T(8,128)(2,1)S(1)}, bf16[8,2,128,128]{3,2,1,0:T(8,128)(2,1)S(1)}) custom-call(s32[3]{0:T(128)S(1)} %add_convert_fusion.flags_ref, bf16[16,2,128,128]{3,2,1,0:T(8,128)(2,1)S(1)} %all-to-all-done.kv_ref, ...), custom_call_target="tpu_custom_call" | custom-call | flops 2768240640 | bytes 8388608 | tf_op jit(solution)/shard_map/attention/pallas_call | solution.py:235
  90.2 0.0 copy-start.8
  90.2 0.8 copy-done.8
  91.0 4.4 %all-to-all-start.2 = ((bf16[16,144,128]{2,1,0:T(8,128)(2,1)}), bf16[16,144,128]{2,1,0:T(8,128)(2,1)S(1)}, u32[]{:S(2)}, u32[]{:S(2)}) async-start(bf16[16,144,128]{2,1,0:T(8,128)(2,1)} %get-tuple-element.13), calls=%async_computation.2 | async-start | bytes 1179648 | tf_op jit(solution)/shard_map/all_to_all | solution.py:318
  95.4 3.4 %collective-permute-start.2 = (bf16[8,2,128,128]{3,2,1,0:T(8,128)(2,1)}, bf16[8,2,128,128]{3,2,1,0:T(8,128)(2,1)S(1)}, u32[]{:S(2)}, u32[]{:S(2)}) collective-permute-start(bf16[8,2,128,128]{3,2,1,0:T(8,128)(2,1)} %copy-done.8), channel_id=1, source_target_pairs={{0,16},{16,32},{32,48},{1,17},{17,33},{33,49},{2,18},{18,34},{34,5... | collective-permute-start | bytes 1572872 | tf_op jit(solution)/shard_map/ppermute | solution.py:335
  98.9 2.5 %collective-permute-start.3 = (bf16[8,2,128,128]{3,2,1,0:T(8,128)(2,1)S(1)}, bf16[8,2,128,128]{3,2,1,0:T(8,128)(2,1)S(1)}, u32[]{:S(2)}, u32[]{:S(2)}) collective-permute-start(bf16[8,2,128,128]{3,2,1,0:T(8,128)(2,1)S(1)} %get-tuple-element.17), channel_id=1, source_target_pairs={{16,0},{32,16},{48,32},{17,1},{33,17},{49,33},{18,2},{34,18},{50,3... | collective-permute-start | bytes 1572872 | tf_op jit(solution)/shard_map/ppermute | solution.py:336
  101.3 11.1 %all-to-all-done.2.in_ref = bf16[16,144,128]{2,1,0:T(8,128)(2,1)S(1)} async-done(((bf16[16,144,128]{2,1,0:T(8,128)(2,1)}), bf16[16,144,128]{2,1,0:T(8,128)(2,1)S(1)}, u32[]{:S(2)}, u32[]{:S(2)}) %all-to-all-start.2) | async-done | bytes 589856 | tf_op jit(solution)/shard_map/all_to_all | solution.py:318
  112.4 0.8 unpack_query.1
  113.2 0.6 broadcast_in_dim.2
  113.8 7.2 %all-to-all-start.4 = ((f32[16,2,128]{2,1,0:T(2,128)}), f32[16,2,128]{2,1,0:T(2,128)S(1)}, u32[]{:S(2)}, u32[]{:S(2)}) async-start(f32[16,2,128]{2,1,0:T(2,128)} %broadcast_in_dim.2), calls=%async_computation.4 | async-start | bytes 32768 | tf_op jit(solution)/shard_map/all_to_all | solution.py:318
  121.0 0.0 collective-permute-done.2.low_ref
  121.0 0.0 collective-permute-done.3.high_ref
  121.0 0.0 copy-start
  121.1 1.6 copy-done
  122.6 1.7 %finish.1 = bf16[16,2,128,128]{3,2,1,0:T(8,128)(2,1)} custom-call(bf16[16,2,128,128]{3,2,1,0:T(8,128)(2,1)S(1)} %all-to-all-done.kv_ref, f32[16,2,128,128]{3,2,1,0:T(8,128)S(1)} %copy-done, bf16[8,2,128,128]{3,2,1,0:T(8,128)(2,1)S(1)} %collective-permute-done.2.low_ref, bf16[8,2,128,128]{3,2,1,0:T(8,128)(2,1)S(1)} %collective-permute-done.3.high_ref, ...), custom_call_target="tpu_custom_call" | custom-call | tf_op jit(solution)/shard_map/finish/pallas_call | solution.py:273
  124.3 2.9 %all-to-all-done.4 = f32[16,2,128]{2,1,0:T(2,128)S(1)} async-done(((f32[16,2,128]{2,1,0:T(2,128)}), f32[16,2,128]{2,1,0:T(2,128)S(1)}, u32[]{:S(2)}, u32[]{:S(2)}) %all-to-all-start.4) | async-done | bytes 16416 | tf_op jit(solution)/shard_map/all_to_all | solution.py:318
  127.3 4.2 %all-to-all-start.3 = ((bf16[16,2,128,128]{3,2,1,0:T(8,128)(2,1)}), bf16[16,2,128,128]{3,2,1,0:T(8,128)(2,1)S(1)}, u32[]{:S(2)}, u32[]{:S(2)}) async-start(bf16[16,2,128,128]{3,2,1,0:T(8,128)(2,1)} %finish.1), calls=%async_computation.3 | async-start | bytes 2097152 | tf_op jit(solution)/shard_map/all_to_all | solution.py:318
  131.5 0.5 slice_bitcast_fusion
  132.0 26.8 %all-to-all-done.3.in_ref = bf16[16,2,128,128]{3,2,1,0:T(8,128)(2,1)S(1)} async-done(((bf16[16,2,128,128]{3,2,1,0:T(8,128)(2,1)}), bf16[16,2,128,128]{3,2,1,0:T(8,128)(2,1)S(1)}, u32[]{:S(2)}, u32[]{:S(2)}) %all-to-all-start.3) | async-done | bytes 1048608 | tf_op jit(solution)/shard_map/all_to_all | solution.py:318
  158.9 1.0 unpack.1
  (3 shorter events, 0.1 us)
Async XLA Ops:
  0.6 1.0 copy-start.1
  1.6 1.0 copy-start.2
  2.6 10.7 %copy-start.3 = (bf16[1,128,1536]{2,1,0:T(8,128)(2,1)S(1)}, bf16[1,128,1536]{2,1,0:T(8,128)(2,1)}, u32[]{:S(2)}) copy-start(bf16[1,128,1536]{2,1,0:T(8,128)(2,1)} %first_ref.3) | copy-start | bytes 1179652
  2.6 10.7 %copy-start.4 = (bf16[1,128,1536]{2,1,0:T(8,128)(2,1)S(1)}, bf16[1,128,1536]{2,1,0:T(8,128)(2,1)}, u32[]{:S(2)}) copy-start(bf16[1,128,1536]{2,1,0:T(8,128)(2,1)} %second_ref.3) | copy-start | bytes 1179652
  3.8 36.7 %all-to-all-start = ((bf16[16,2,128,128]{3,2,1,0:T(8,128)(2,1)}), bf16[16,2,128,128]{3,2,1,0:T(8,128)(2,1)S(1)}, u32[]{:S(2)}, u32[]{:S(2)}) async-start(bf16[16,2,128,128]{3,2,1,0:T(8,128)(2,1)} %pack.2), calls=%async_computation | async-start | bytes 2097152 | tf_op jit(solution)/shard_map/all_to_all | solution.py:318
  14.5 58.4 %copy-start.5 = (f32[128]{0:T(128)S(1)}, f32[128]{0:T(128)}, u32[]{:S(2)}) copy-start(f32[128]{0:T(128)} %param.11) | copy-start | bytes 1540
  14.5 58.4 %copy-start.9 = (f32[128]{0:T(128)S(1)}, f32[128]{0:T(128)}, u32[]{:S(2)}) copy-start(f32[128]{0:T(128)} %param.10) | copy-start | bytes 1540
  40.4 31.7 %all-to-all-start.1 = ((bf16[16,2,128,128]{3,2,1,0:T(8,128)(2,1)}), bf16[16,2,128,128]{3,2,1,0:T(8,128)(2,1)S(1)}, u32[]{:S(2)}, u32[]{:S(2)}) async-start(bf16[16,2,128,128]{3,2,1,0:T(8,128)(2,1)} %pack.3), calls=%async_computation.1 | async-start | bytes 2097152 | tf_op jit(solution)/shard_map/all_to_all | solution.py:318
  45.9 26.2 %collective-permute-start.1 = (bf16[8,2,128,128]{3,2,1,0:T(8,128)(2,1)}, bf16[8,2,128,128]{3,2,1,0:T(8,128)(2,1)S(1)}, u32[]{:S(2)}, u32[]{:S(2)}) collective-permute-start(bf16[8,2,128,128]{3,2,1,0:T(8,128)(2,1)} %get-tuple-element.23), channel_id=1, source_target_pairs={{16,0},{32,16},{48,32},{17,1},{33,17},{49,33},{18,2},{34,18},{50,3... | collective-permute-start | bytes 1572872 | tf_op jit(solution)/shard_map/ppermute | solution.py:332
  48.3 23.8 %collective-permute-start = (bf16[8,2,128,128]{3,2,1,0:T(8,128)(2,1)}, bf16[8,2,128,128]{3,2,1,0:T(8,128)(2,1)S(1)}, u32[]{:S(2)}, u32[]{:S(2)}) collective-permute-start(bf16[8,2,128,128]{3,2,1,0:T(8,128)(2,1)} %get-tuple-element.24), channel_id=1, source_target_pairs={{0,16},{16,32},{32,48},{1,17},{17,33},{33,49},{2,18},{18,34},{34,5... | collective-permute-start | bytes 1572872 | tf_op jit(solution)/shard_map/ppermute | solution.py:331
  72.1 0.8 copy-start.6
  72.9 1.0 copy-start.7
  90.2 0.8 copy-start.8
  91.0 21.4 %all-to-all-start.2 = ((bf16[16,144,128]{2,1,0:T(8,128)(2,1)}), bf16[16,144,128]{2,1,0:T(8,128)(2,1)S(1)}, u32[]{:S(2)}, u32[]{:S(2)}) async-start(bf16[16,144,128]{2,1,0:T(8,128)(2,1)} %get-tuple-element.13), calls=%async_computation.2 | async-start | bytes 1179648 | tf_op jit(solution)/shard_map/all_to_all | solution.py:318
  95.4 25.6 %collective-permute-start.2 = (bf16[8,2,128,128]{3,2,1,0:T(8,128)(2,1)}, bf16[8,2,128,128]{3,2,1,0:T(8,128)(2,1)S(1)}, u32[]{:S(2)}, u32[]{:S(2)}) collective-permute-start(bf16[8,2,128,128]{3,2,1,0:T(8,128)(2,1)} %copy-done.8), channel_id=1, source_target_pairs={{0,16},{16,32},{32,48},{1,17},{17,33},{33,49},{2,18},{18,34},{34,5... | collective-permute-start | bytes 1572872 | tf_op jit(solution)/shard_map/ppermute | solution.py:335
  98.9 22.2 %collective-permute-start.3 = (bf16[8,2,128,128]{3,2,1,0:T(8,128)(2,1)S(1)}, bf16[8,2,128,128]{3,2,1,0:T(8,128)(2,1)S(1)}, u32[]{:S(2)}, u32[]{:S(2)}) collective-permute-start(bf16[8,2,128,128]{3,2,1,0:T(8,128)(2,1)S(1)} %get-tuple-element.17), channel_id=1, source_target_pairs={{16,0},{32,16},{48,32},{17,1},{33,17},{49,33},{18,2},{34,18},{50,3... | collective-permute-start | bytes 1572872 | tf_op jit(solution)/shard_map/ppermute | solution.py:336
  113.8 13.4 %all-to-all-start.4 = ((f32[16,2,128]{2,1,0:T(2,128)}), f32[16,2,128]{2,1,0:T(2,128)S(1)}, u32[]{:S(2)}, u32[]{:S(2)}) async-start(f32[16,2,128]{2,1,0:T(2,128)} %broadcast_in_dim.2), calls=%async_computation.4 | async-start | bytes 32768 | tf_op jit(solution)/shard_map/all_to_all | solution.py:318
  121.0 1.6 copy-start
  127.3 31.6 %all-to-all-start.3 = ((bf16[16,2,128,128]{3,2,1,0:T(8,128)(2,1)}), bf16[16,2,128,128]{3,2,1,0:T(8,128)(2,1)S(1)}, u32[]{:S(2)}, u32[]{:S(2)}) async-start(bf16[16,2,128,128]{3,2,1,0:T(8,128)(2,1)} %finish.1), calls=%async_computation.3 | async-start | bytes 2097152 | tf_op jit(solution)/shard_map/all_to_all | solution.py:318

commit v2 on v1

v2 whole, which is shorter than its diff:
```python
import functools

import jax
import jax.numpy as jnp
from jax import lax
from jax.experimental import pallas as pl
from jax.experimental.pallas import tpu as pltpu
from jax.sharding import Mesh
from jax.sharding import PartitionSpec as P

HEADS = 12
HD = 128
TILE = 64
PAIR = 2 * TILE
GROUP = 16
HALF = 8
COLS = 4
EXTRA = 16
WIDE = 8
EPSILON = 1e-06
SCALE = HD ** (-0.5)
SCALE_LOG2E = SCALE * 1.4426950408889634
F32 = jnp.float32
BF16 = jnp.bfloat16
MIB = 1024 * 1024


def nt(left, right):
    return lax.dot_general(left, right, (((1,), (1,)), ((), ())), preferred_element_type=F32)


def nn(left, right):
    return lax.dot_general(left, right, (((1,), (0,)), ((), ())), preferred_element_type=F32)


def inverse_rms(inputs):
    return lax.rsqrt(jnp.mean(inputs * inputs, axis=-1, keepdims=True) + EPSILON)


def norm_back(inputs, inverse, gain, cotangent):
    scaled = cotangent * gain
    mean = jnp.mean(inputs * scaled, axis=-1, keepdims=True)
    return inverse * scaled - inputs * (inverse * inverse * inverse * mean)


def call(kernel, name, out_shape, arguments, flags=False, scratch=(), flops=0, limit=60):
    vmem = pl.BlockSpec(memory_space=pltpu.VMEM)
    in_specs = [vmem] * len(arguments)
    if flags:
        in_specs[0] = pl.BlockSpec(memory_space=pltpu.SMEM)
    return pl.pallas_call(
        kernel,
        in_specs=in_specs,
        out_specs=[vmem] * len(out_shape),
        out_shape=[jax.ShapeDtypeStruct(shape, dtype) for shape, dtype in out_shape],
        scratch_shapes=list(scratch),
        name=name,
        cost_estimate=pl.CostEstimate(flops=flops, bytes_accessed=4 * MIB, transcendentals=0),
        compiler_params=pltpu.CompilerParams(vmem_limit_bytes=limit * MIB),
    )(*arguments)


def pack_kernel(k_ref, v_ref, q_ref, d_ref, kv_ref, qd_ref, sem):
    copies = []
    for target, sources in ((kv_ref, (k_ref, v_ref)), (qd_ref, (q_ref, d_ref))):
        for head in range(HEADS):
            lanes = pl.ds(head * HD, HD)
            for number, source in enumerate(sources):
                copies.append(pltpu.make_async_copy(source.at[0, :, lanes], target.at[head, number], sem))
    for copy in copies:
        copy.start()
    for target in (kv_ref, qd_ref):
        for head in range(HEADS, GROUP):
            target[head] = jnp.zeros(target.shape[1:], target.dtype)
    for copy in copies:
        copy.wait()


def pack(*sources):
    out = jax.ShapeDtypeStruct((GROUP, 2, PAIR, HD), BF16)
    return pl.pallas_call(
        pack_kernel,
        in_specs=[pl.BlockSpec(memory_space=pl.ANY)] * 4,
        out_specs=[pl.BlockSpec(memory_space=pltpu.VMEM)] * 2,
        out_shape=[out, out],
        scratch_shapes=[pltpu.SemaphoreType.DMA],
        name="pack",
        compiler_params=pltpu.CompilerParams(vmem_limit_bytes=60 * MIB),
    )(*sources)


def blocks_of(frames):
    for frame in range(frames):
        for row in range(2):
            for col in range(COLS):
                yield frame * HALF + row * COLS + col, frame, row, col


def spread(parts):
    return parts[0] + jnp.concatenate(parts[1:], axis=1)


def raw_column(source, w, frame):
    place = slice((w % 2) * TILE, (w % 2 + 1) * TILE)
    index = frame * HALF + w // 2
    return jnp.concatenate([source[index, 0, place], source[index + COLS, 0, place]], axis=0).astype(F32)


def attention_kernel(
    flags_ref,
    kv_ref,
    low_ref,
    high_ref,
    qd_ref,
    q_gain_ref,
    k_gain_ref,
    dq_ref,
    own_ref,
    to_low,
    to_high,
    kn_own,
    knt_own,
    vv_own,
    kn_l,
    knt_l,
    vv_l,
    kn_h,
    knt_h,
    vv_h,
    qn,
    dd,
    q_side,
    d_side,
    chance_own,
    chance_l,
    chance_h,
    score_own,
    score_l,
    score_h,
    gains_ref,
):
    q_gain = q_gain_ref[...]
    k_gain = k_gain_ref[...]
    def prepare(col):
        for source, frames, kn, knt, vv in (
            (kv_ref, 2, kn_own, knt_own, vv_own),
            (low_ref, 1, kn_l, knt_l, vv_l),
            (high_ref, 1, kn_h, knt_h, vv_h),
        ):
            for frame in range(frames):
                for row in range(2):
                    index = frame * HALF + row * COLS + col
                    raw = source[index, 0].astype(F32)
                    normed = (raw * inverse_rms(raw) * k_gain).astype(BF16)
                    for part in range(2):
                        at = ((2 * col + part) * frames + frame) * PAIR + row * TILE
                        kn[at : at + TILE] = normed[part * TILE : (part + 1) * TILE]
                        vv[at : at + TILE] = source[index, 1, part * TILE : (part + 1) * TILE]
            for block in range(2 * col * frames, 2 * (col + 1) * frames):
                rows = slice(block * PAIR, (block + 1) * PAIR)
                knt[:, rows] = kn[rows].T
        for frame in range(2):
            for row in range(2):
                index = frame * HALF + row * COLS + col
                raw = qd_ref[index, 0].astype(F32)
                normed = (raw * inverse_rms(raw) * q_gain).astype(BF16)
                for part in range(2):
                    place = slice(part * TILE, (part + 1) * TILE)
                    at = ((2 * col + part) * 2 + frame) * PAIR + row * TILE
                    qn[at : at + TILE] = normed[place]
                    dd[at : at + TILE] = qd_ref[index, 1, place]
                    at = (2 * col + part) * PAIR + row * TILE
                    q_side[frame, at : at + TILE] = normed[place]
                    d_side[frame, at : at + TILE] = qd_ref[index, 1, place]

    gains_ref[...] = jnp.zeros_like(gains_ref)
    sources = (
        (kn_own, knt_own, vv_own, chance_own, score_own, 2, 0, 2 * PAIR, None),
        (kn_l, knt_l, vv_l, chance_l, score_l, 1, 0, PAIR, flags_ref[0].astype(F32)),
        (kn_h, knt_h, vv_h, chance_h, score_h, 1, PAIR, PAIR, flags_ref[1].astype(F32)),
    )

    def first_half(w, before, count):
        q_rows = pl.ds(w * (2 * PAIR), 2 * PAIR)
        q_tile = qn[q_rows]
        d_tile = dd[q_rows]
        weights, weight_grads, sums = [], [], []
        for kn, _, vv, _, _, frames, first, width, valid in sources:
            rows = pl.ds((w - before) * (frames * PAIR), count * frames * PAIR)
            queries = slice(first, first + width)
            weight = jnp.exp2(nt(kn[rows], q_tile[queries]) * SCALE_LOG2E)
            if valid is not None:
                weight = weight * valid
            weights.append(weight)
            sums.append(jnp.sum(weight, axis=0, keepdims=True))
            weight_grads.append(nt(vv[rows], d_tile[queries]))
        return q_tile, d_tile, weights, weight_grads, sums

    def second_half(w, before, count, q_tile, d_tile, weights, weight_grads, sums):
        reciprocal = 1.0 / spread(sums)
        chances, dots = [], []
        for number, (_, _, _, store, _, frames, first, width, _) in enumerate(sources):
            chance = weights[number] * reciprocal[:, first : first + width]
            rounded = chance.astype(BF16)
            dots.append(jnp.sum(rounded.astype(F32) * weight_grads[number], axis=0, keepdims=True))
            chances.append(chance)
            for step in range(count):
                place = (1 - (step - before)) * width
                store[w - before + step, :, place : place + width] = rounded[
                    step * frames * PAIR : (step + 1) * frames * PAIR
                ]
        row_dot = spread(dots)
        grads = []
        for number, (_, knt, _, _, store, frames, first, width, _) in enumerate(sources):
            score = chances[number] * (weight_grads[number] - row_dot[:, first : first + width])
            score = score.astype(BF16)
            for step in range(count):
                place = (1 - (step - before)) * width
                store[w - before + step, :, place : place + width] = score[
                    step * frames * PAIR : (step + 1) * frames * PAIR
                ]
            lanes = pl.ds((w - before) * (frames * PAIR), count * frames * PAIR)
            grads.append(nn(knt[:, lanes], score))
        grad = spread(grads).T * SCALE
        col = w // 2
        place = pl.ds((w % 2) * TILE, TILE)
        for frame in range(2):
            for row in range(2):
                index = frame * HALF + row * COLS + col
                raw = qd_ref[index, 0, place].astype(F32)
                inverse = inverse_rms(raw)
                part = grad[frame * PAIR + row * TILE : frame * PAIR + (row + 1) * TILE]
                gains_ref[...] += jnp.sum((part * raw * inverse).reshape(-1, 8, HD), axis=0)
                dq_ref[index, place] = norm_back(raw, inverse, q_gain, part).astype(BF16)

    def key_sums(chance, score, queries, cotangents, w, width):
        first, last = max(w - 1, 0), min(w + 1, WIDE - 1)
        lanes = slice((first - w + 1) * width, (last - w + 2) * width)
        rows = slice(first * width, (last + 1) * width)
        value_grad = nn(chance[w, :, lanes], cotangents[rows])
        key_grad = nn(score[w, :, lanes], queries[rows]) * SCALE
        return key_grad, value_grad

    def gain_part(key_grad, raw):
        return jnp.sum((key_grad * raw * inverse_rms(raw)).reshape(-1, 8, HD), axis=0)

    sides = ((chance_l, score_l, low_ref, to_low), (chance_h, score_h, high_ref, to_high))

    def key_column(w, gain_sum):
        for frame, (chance, score, raw_ref, out_ref) in enumerate(sides):
            key_grad, value_grad = key_sums(chance, score, q_side.at[frame], d_side.at[frame], w, PAIR)
            out_ref[w, 0] = key_grad.astype(BF16)
            out_ref[w, 1] = value_grad.astype(BF16)
            gain_sum += gain_part(key_grad, raw_column(raw_ref, w, 0))
        key_grad, value_grad = key_sums(chance_own, score_own, qn, dd, w, 2 * PAIR)
        own_ref[w, 0] = key_grad
        own_ref[w, 1] = value_grad
        for frame in range(2):
            gain_sum += gain_part(key_grad[frame * PAIR : (frame + 1) * PAIR], raw_column(kv_ref, w, frame))
        return gain_sum

    def extent(w):
        return w, min(w, 1), 2 if w in (0, WIDE - 1) else 3

    gain_sum = jnp.zeros((8, HD), F32)
    prepare(0)
    held = first_half(*extent(0))
    for w in range(WIDE):
        if w % 2 == 0 and w // 2 + 1 < COLS:
            prepare(w // 2 + 1)
        following = first_half(*extent(w + 1)) if w + 1 < WIDE else None
        second_half(*extent(w), *held)
        held = following
        if w > 0:
            gain_sum = key_column(w - 1, gain_sum)
    gain_sum = key_column(WIDE - 1, gain_sum)


    q_sum = jnp.sum(gains_ref[...], axis=0, keepdims=True)
    k_sum = jnp.sum(gain_sum, axis=0, keepdims=True)
    lines = []
    for line in (q_sum, k_sum):
        line = jnp.where(flags_ref[2] > 0, line, 0.0)
        for _ in range(3):
            rounded = line.astype(BF16).astype(F32)
            lines.append(rounded)
            line = line - rounded
    lines.append(jnp.zeros((EXTRA - 6, HD), F32))
    block = jnp.concatenate(lines, axis=0).astype(BF16)
    for index in range(GROUP):
        dq_ref[index, PAIR : PAIR + EXTRA] = block


def attention(flags, kv, low, high, qd, q_gain, k_gain):
    own, halo = WIDE * 2 * PAIR, WIDE * PAIR
    scratch = []
    for rows in (own, halo, halo):
        scratch += [pltpu.VMEM((rows, HD), BF16), pltpu.VMEM((HD, rows), BF16), pltpu.VMEM((rows, HD), BF16)]
    scratch += [pltpu.VMEM((own, HD), BF16)] * 2 + [pltpu.VMEM((2, halo, HD), BF16)] * 2
    stores = [pltpu.VMEM((WIDE, 2 * PAIR, 6 * PAIR), BF16)] + [pltpu.VMEM((WIDE, PAIR, 3 * PAIR), BF16)] * 2
    scratch += stores + stores + [pltpu.VMEM((8, HD), F32)]
    to_side = ((WIDE, 2, PAIR, HD), BF16)
    out_shape = [((GROUP, PAIR + EXTRA, HD), BF16), ((WIDE, 2, 2 * PAIR, HD), F32), to_side, to_side]
    return call(
        attention_kernel,
        "attention",
        out_shape,
        (flags, kv, low, high, qd, q_gain, k_gain),
        flags=True,
        scratch=scratch,
        flops=5 * 66 * PAIR * PAIR * PAIR * 2,
        limit=60,
    )


def finish_kernel(kv_ref, own_ref, low_ref, high_ref, k_gain_ref, out_ref):
    k_gain = k_gain_ref[...]
    for w in range(WIDE):
        place = slice((w % 2) * TILE, (w % 2 + 1) * TILE)
        for frame, arrived in enumerate((low_ref, high_ref)):
            rows = slice(frame * PAIR, (frame + 1) * PAIR)
            raw = raw_column(kv_ref, w, frame)
            key_grad = own_ref[w, 0, rows] + arrived[w, 0].astype(F32)
            value_grad = (own_ref[w, 1, rows] + arrived[w, 1].astype(F32)).astype(BF16)
            key_grad = norm_back(raw, inverse_rms(raw), k_gain, key_grad).astype(BF16)
            for row in range(2):
                index = frame * HALF + row * COLS + w // 2
                out_ref[index, 0, place] = key_grad[row * TILE : (row + 1) * TILE]
                out_ref[index, 1, place] = value_grad[row * TILE : (row + 1) * TILE]


def finish(kv, own, low, high, k_gain):
    out_shape = [((GROUP, 2, PAIR, HD), BF16)]
    return call(finish_kernel, "finish", out_shape, (kv, own, low, high, k_gain))[0]


def unpack_query_kernel(in_ref, out_ref, lines_ref):
    for head in range(HEADS):
        out_ref[0, :, head * HD : (head + 1) * HD] = in_ref[head, :PAIR]
    total = in_ref[0, PAIR : PAIR + EXTRA].astype(F32)
    for index in range(1, GROUP):
        total = total + in_ref[index, PAIR : PAIR + EXTRA].astype(F32)
    sums = [jnp.sum(total[first : first + 3], axis=0, keepdims=True) for first in (0, 3)]
    lines_ref[...] = jnp.concatenate(sums + [jnp.zeros((6, HD), F32)], axis=0)


def unpack_kernel(in_ref, key_ref, value_ref):
    for head in range(HEADS):
        key_ref[0, :, head * HD : (head + 1) * HD] = in_ref[head, 0]
        value_ref[0, :, head * HD : (head + 1) * HD] = in_ref[head, 1]


def swap(array):
    return lax.all_to_all(array, "g", 0, 0)


def sum_over(lines, axis, steps):
    count = lax.axis_size(axis)
    total = lines
    for step in steps:
        total = total + lax.ppermute(lines, axis, [(source, source ^ step) for source in range(count)])
    return total


def on_device(blocks, q_raw, k_raw, values, d_out, q_gain, k_gain):
    block = lax.axis_index("x")
    member = lax.axis_index("g")
    flags = jnp.stack([block > 0, block < blocks - 1, member < HEADS]).astype(jnp.int32)
    up = [(source, source + 1) for source in range(blocks - 1)]
    down = [(source + 1, source) for source in range(blocks - 1)]
    q_line = q_gain.reshape(1, HD)
    k_line = k_gain.reshape(1, HD)
    tokens = ((1, PAIR, HEADS * HD), BF16)

    kv, qd = pack(k_raw, values, q_raw, d_out)
    kv = swap(kv)
    low = lax.ppermute(kv[HALF:], "x", up)
    high = lax.ppermute(kv[:HALF], "x", down)
    qd = swap(qd)
    dq, own, to_low, to_high = attention(flags, kv, low, high, qd, q_line, k_line)
    arrived = swap(dq)
    from_low = lax.ppermute(to_high, "x", up)
    from_high = lax.ppermute(to_low, "x", down)
    q_grad, lines = call(unpack_query_kernel, "unpack_query", [tokens, ((8, HD), F32)], (arrived,))
    grads = finish(kv, own, from_low, from_high, k_line)
    k_grad, v_grad = call(unpack_kernel, "unpack", [tokens, tokens], (swap(grads),))
    lines = sum_over(lines, "dp", (1, 2, 3))
    lines = sum_over(lines, "x", (1, 2, 3))
    return (q_grad, k_grad, v_grad, lines[0], lines[1])


def solution(mesh):
    videos, seq = mesh.devices.shape
    blocks = seq // GROUP
    split = Mesh(mesh.devices.reshape(videos, blocks, GROUP), ("dp", "x", "g"))
    tokens = P("dp", ("x", "g"), None)
    return jax.shard_map(
        functools.partial(on_device, blocks),
        mesh=split,
        in_specs=(tokens, tokens, tokens, tokens, P(), P()),
        out_specs=(tokens, tokens, tokens, P(), P()),
        check_vma=False,
    )
```

time: 161 us -> 150 us (0.932)
  waiting for transfers between devices: 87 us -> 47 us
  blocking collectives: 0 us -> 36.5 us
  starting transfers between devices: 41.5 us -> 36.8 us
  local copies, waits for them, and re-layouts: 8.4 us -> 3.74 us
    all_to_all x5 -> x3, waiting for transfers between devices: 87 us -> 29.4 us  [swap(): return lax.all_to_all(array, 'g', 0, 0)]
    all_to_all x0 -> x1, blocking collectives: none -> 36.5 us  [swap(): return lax.all_to_all(array, 'g', 0, 0)]
    all_to_all x5 -> x3, starting transfers between devices: 29.8 us -> 17.6 us  [swap(): return lax.all_to_all(array, 'g', 0, 0)]
    ppermute x1, waiting for transfers between devices: 0.01 us -> 9.78 us  [on_device(): from_low = lax.ppermute(to_high, 'x', up)]
    ppermute x0 -> x6, starting transfers between devices: none -> 7.46 us  [sum_over(): lax.ppermute(lines, axis, [(source, source ^ step) for source in range(co...]
    ppermute x0 -> x6, waiting for transfers between devices: none -> 4.76 us  [sum_over(): lax.ppermute(lines, axis, [(source, source ^ step) for source in range(co...]
    ppermute x1, waiting for transfers between devices: 0.01 us -> 3.12 us  [on_device(): from_high = lax.ppermute(to_low, 'x', down)]
    unnamed x20 -> x16, local copies, waits for them, and re-layouts: 6.22 us -> 3.12 us
  transfers between devices with their start and end apart: 9 -> 13, of which waited for: 5 -> 7; matrix products, arithmetic and copies ran while one was open for 1% -> 1% of each run, Pallas kernels for 2% -> 4%
where the time goes in v2:
time: 150 us; the launch traced here: 149 us
  waiting for transfers between devices  47 us (31%)
  starting transfers between devices  36.8 us (25%)
  blocking collectives  36.5 us (24%)
  Pallas kernels  23.3 us (16%)
  local copies, waits for them, and re-layouts  3.74 us (2%)
    all_to_all x1, blocking collectives, swap(): return lax.all_to_all(array, 'g', 0, 0)  36.5 us
    all_to_all x3, waiting for transfers between devices, swap(): return lax.all_to_all(array, 'g', 0, 0)  29.4 us
    pallas_call x4, Pallas kernels, call(): pl.pallas_call(kernel, in_specs=in_specs, out_specs=[vmem] * len(out_shap...  20.6 us
    all_to_all x3, starting transfers between devices, swap(): return lax.all_to_all(array, 'g', 0, 0)  17.6 us
    ppermute x1, waiting for transfers between devices, on_device(): from_low = lax.ppermute(to_high, 'x', up)  9.78 us
    ppermute x6, starting transfers between devices, sum_over(): lax.ppermute(lines, axis, [(source, source ^ step) for source in range(co...  7.46 us
    ppermute x6, waiting for transfers between devices, sum_over(): lax.ppermute(lines, axis, [(source, source ^ step) for source in range(co...  4.76 us
    ppermute x1, starting transfers between devices, on_device(): low = lax.ppermute(kv[HALF:], 'x', up)  3.4 us
  transfers between devices with their start and end apart: 13, of which 7 were waited for; matrix products, arithmetic and copies ran while one was open for 1% of the time, Pallas kernels for 4%

profile of v2, /device:TPU:2, one launch (start us, length us, event | category | flops | bytes accessed | tf_op | source)
XLA Modules:
  0.0 149.4 jit_solution(5440454685891271376)
XLA Ops:
  0.6 2.7 %pack.1 = (bf16[16,2,128,128]{3,2,1,0:T(8,128)(2,1)}, bf16[16,2,128,128]{3,2,1,0:T(8,128)(2,1)}) custom-call(bf16[1,128,1536]{2,1,0:T(8,128)(2,1)} %k_ref.1, bf16[1,128,1536]{2,1,0:T(8,128)(2,1)} %v_ref.1, bf16[1,128,1536]{2,1,0:T(8,128)(2,1)} %q_ref.1, bf16[1,128,1536]{2,1,0:T(8,128)(2,1)} %d_ref.1), custom_call_target="tpu_custom_call" | custom-call | tf_op jit(solution)/shard_map/pack/pallas_call | solution.py:81
  3.3 36.5 %all_to_all.20.kv_ref = bf16[16,2,128,128]{3,2,1,0:T(8,128)(2,1)S(1)} all-to-all(bf16[16,2,128,128]{3,2,1,0:T(8,128)(2,1)} %get-tuple-element.15), channel_id=1, replica_groups=mesh['dp'=4,'x'=4,'g'=16] {'g'}, dimensions={0} | all-to-all | bytes 2097152 | tf_op jit(solution)/shard_map/all_to_all | solution.py:354
  39.8 0.0 copy-start
  39.9 4.5 %all-to-all-start.1 = ((bf16[16,2,128,128]{3,2,1,0:T(8,128)(2,1)}), bf16[16,2,128,128]{3,2,1,0:T(8,128)(2,1)S(1)}, u32[]{:S(2)}, u32[]{:S(2)}) async-start(bf16[16,2,128,128]{3,2,1,0:T(8,128)(2,1)} %get-tuple-element.16), calls=%async_computation.1 | async-start | bytes 2097152 | tf_op jit(solution)/shard_map/all_to_all | solution.py:354
  44.4 0.1 fusion
  44.5 0.0 copy-done
  44.5 2.4 %collective-permute-start.1 = (bf16[8,2,128,128]{3,2,1,0:T(8,128)(2,1)S(1)}, bf16[8,2,128,128]{3,2,1,0:T(8,128)(2,1)S(1)}, u32[]{:S(2)}, u32[]{:S(2)}) collective-permute-start(bf16[8,2,128,128]{3,2,1,0:T(8,128)(2,1)S(1)} %get-tuple-element.25), channel_id=1, source_target_pairs={{16,0},{32,16},{48,32},{17,1},{33,17},{49,33},{18,2},{34,18},{50,3... | collective-permute-start | bytes 1572872 | tf_op jit(solution)/shard_map/ppermute | solution.py:378
  47.0 3.4 %collective-permute-start = (bf16[8,2,128,128]{3,2,1,0:T(8,128)(2,1)S(1)}, bf16[8,2,128,128]{3,2,1,0:T(8,128)(2,1)S(1)}, u32[]{:S(2)}, u32[]{:S(2)}) collective-permute-start(bf16[8,2,128,128]{3,2,1,0:T(8,128)(2,1)S(1)} %get-tuple-element.26), channel_id=1, source_target_pairs={{0,16},{16,32},{32,48},{1,17},{17,33},{33,49},{2,18},{18,34},{34,5... | collective-permute-start | bytes 1572872 | tf_op jit(solution)/shard_map/ppermute | solution.py:377
  50.4 0.6 add_convert_fusion.flags_ref
  51.0 19.1 %all-to-all-done.1.qd_ref = bf16[16,2,128,128]{3,2,1,0:T(8,128)(2,1)S(1)} async-done(((bf16[16,2,128,128]{3,2,1,0:T(8,128)(2,1)}), bf16[16,2,128,128]{3,2,1,0:T(8,128)(2,1)S(1)}, u32[]{:S(2)}, u32[]{:S(2)}) %all-to-all-start.1) | async-done | bytes 1048608 | tf_op jit(solution)/shard_map/all_to_all | solution.py:354
  70.1 0.0 copy-start.3
  70.1 0.0 collective-permute-done.1.high_ref
  70.1 0.0 copy-start.6
  70.1 0.0 collective-permute-done.low_ref
  70.1 0.0 copy-start.7
  70.1 0.9 copy-done.3
  71.1 0.2 copy-done.6
  71.2 0.2 copy-done.7
  71.4 12.7 %attention.1 = (bf16[16,144,128]{2,1,0:T(8,128)(2,1)}, f32[8,2,256,128]{3,2,1,0:T(8,128)}, bf16[8,2,128,128]{3,2,1,0:T(8,128)(2,1)}, bf16[8,2,128,128]{3,2,1,0:T(8,128)(2,1)}) custom-call(s32[3]{0:T(128)} %add_convert_fusion.flags_ref, bf16[16,2,128,128]{3,2,1,0:T(8,128)(2,1)} %copy-done, bf16[8,2,128,128]{3,2,1,0:T(8,128)(2,1)} %copy-done.7, ...), custom_call_target="tpu_custom_call" | custom-call | flops 1384120320 | bytes 4194304 | tf_op jit(solution)/shard_map/attention/pallas_call | solution.py:51
  84.1 5.2 %all-to-all-start.2 = ((bf16[16,144,128]{2,1,0:T(8,128)(2,1)}), bf16[16,144,128]{2,1,0:T(8,128)(2,1)S(1)}, u32[]{:S(2)}, u32[]{:S(2)}) async-start(bf16[16,144,128]{2,1,0:T(8,128)(2,1)} %get-tuple-element.17), calls=%async_computation.2 | async-start | bytes 1179648 | tf_op jit(solution)/shard_map/all_to_all | solution.py:354
  89.4 3.4 %collective-permute-start.2 = (bf16[8,2,128,128]{3,2,1,0:T(8,128)(2,1)}, bf16[8,2,128,128]{3,2,1,0:T(8,128)(2,1)S(1)}, u32[]{:S(2)}, u32[]{:S(2)}) collective-permute-start(bf16[8,2,128,128]{3,2,1,0:T(8,128)(2,1)} %get-tuple-element.20), channel_id=1, source_target_pairs={{0,16},{16,32},{32,48},{1,17},{17,33},{33,49},{2,18},{18,34},{34,5... | collective-permute-start | bytes 1572872 | tf_op jit(solution)/shard_map/ppermute | solution.py:382
  92.8 2.5 %collective-permute-start.3 = (bf16[8,2,128,128]{3,2,1,0:T(8,128)(2,1)}, bf16[8,2,128,128]{3,2,1,0:T(8,128)(2,1)S(1)}, u32[]{:S(2)}, u32[]{:S(2)}) collective-permute-start(bf16[8,2,128,128]{3,2,1,0:T(8,128)(2,1)} %get-tuple-element.21), channel_id=1, source_target_pairs={{16,0},{32,16},{48,32},{17,1},{33,17},{49,33},{18,2},{34,18},{50,3... | collective-permute-start | bytes 1572872 | tf_op jit(solution)/shard_map/ppermute | solution.py:383
  95.3 9.8 %collective-permute-done.2.low_ref = bf16[8,2,128,128]{3,2,1,0:T(8,128)(2,1)S(1)} collective-permute-done((bf16[8,2,128,128]{3,2,1,0:T(8,128)(2,1)}, bf16[8,2,128,128]{3,2,1,0:T(8,128)(2,1)S(1)}, u32[]{:S(2)}, u32[]{:S(2)}) %collective-permute-start.2) | collective-permute-done | bytes 524320 | tf_op jit(solution)/shard_map/ppermute | solution.py:382
  105.1 3.1 %collective-permute-done.3.high_ref = bf16[8,2,128,128]{3,2,1,0:T(8,128)(2,1)S(1)} collective-permute-done((bf16[8,2,128,128]{3,2,1,0:T(8,128)(2,1)}, bf16[8,2,128,128]{3,2,1,0:T(8,128)(2,1)S(1)}, u32[]{:S(2)}, u32[]{:S(2)}) %collective-permute-start.3) | collective-permute-done | bytes 524320 | tf_op jit(solution)/shard_map/ppermute | solution.py:383
  108.2 0.0 copy-done.4
  108.2 0.8 copy-done.5
  109.0 3.8 %finish.1 = bf16[16,2,128,128]{3,2,1,0:T(8,128)(2,1)} custom-call(bf16[16,2,128,128]{3,2,1,0:T(8,128)(2,1)} %copy-done, f32[8,2,256,128]{3,2,1,0:T(8,128)} %get-tuple-element.19.own_ref, bf16[8,2,128,128]{3,2,1,0:T(8,128)(2,1)} %copy-done.4, bf16[8,2,128,128]{3,2,1,0:T(8,128)(2,1)} %copy-done.5, f32[1,128]{1,0:T(1,128)} %bitcast.10), custom_call_target="tpu_custom_call" | custom-call | bytes 4194304 | tf_op jit(solution)/shard_map/finish/pallas_call | solution.py:51
  112.8 0.0 all-to-all-done.2.in_ref
  112.8 7.8 %all-to-all-start.3 = ((bf16[16,2,128,128]{3,2,1,0:T(8,128)(2,1)}), bf16[16,2,128,128]{3,2,1,0:T(8,128)(2,1)S(1)}, u32[]{:S(2)}, u32[]{:S(2)}) async-start(bf16[16,2,128,128]{3,2,1,0:T(8,128)(2,1)} %finish.1), calls=%async_computation.3 | async-start | bytes 2097152 | tf_op jit(solution)/shard_map/all_to_all | solution.py:354
  120.6 0.0 copy-done.2
  120.6 1.9 %unpack_query.1 = (bf16[1,128,1536]{2,1,0:T(8,128)(2,1)}, f32[8,128]{1,0:T(8,128)}) custom-call(bf16[16,144,128]{2,1,0:T(8,128)(2,1)} %copy-done.2), custom_call_target="tpu_custom_call" | custom-call | bytes 4194304 | tf_op jit(solution)/shard_map/unpack_query/pallas_call | solution.py:51
  122.5 0.5 collective-permute-start.6
  123.0 2.5 %collective-permute-start.5 = (f32[8,128]{1,0:T(8,128)}, f32[8,128]{1,0:T(8,128)S(1)}, u32[]{:S(2)}, u32[]{:S(2)}) collective-permute-start(f32[8,128]{1,0:T(8,128)} %get-tuple-element.24), channel_id=1, source_target_pairs={{0,128},{64,192},{128,0},{192,64},{1,129},{65,193},{129,1},{193,65... | collective-permute-start | bytes 12296 | tf_op jit(solution)/shard_map/ppermute | solution.py:361
  125.5 0.4 collective-permute-start.4
  125.9 1.5 collective-permute-done.6
  127.3 1.1 collective-permute-done.5
  128.4 0.0 collective-permute-done.4
  128.4 0.7 add_add_fusion.1
  129.1 1.2 collective-permute-start.9
  130.3 1.4 collective-permute-start.8
  131.7 1.5 collective-permute-start.7
  133.2 0.0 collective-permute-done.9
  133.2 2.2 %collective-permute-done.8 = f32[8,128]{1,0:T(8,128)S(1)} collective-permute-done((f32[8,128]{1,0:T(8,128)S(1)}, f32[8,128]{1,0:T(8,128)S(1)}, u32[]{:S(2)}, u32[]{:S(2)}) %collective-permute-start.8) | collective-permute-done | bytes 4128 | tf_op jit(solution)/shard_map/ppermute | solution.py:361
  135.4 0.0 collective-permute-done.7
  135.4 0.5 slice_bitcast_fusion
  136.0 10.2 %all-to-all-done.3.in_ref = bf16[16,2,128,128]{3,2,1,0:T(8,128)(2,1)S(1)} async-done(((bf16[16,2,128,128]{3,2,1,0:T(8,128)(2,1)}), bf16[16,2,128,128]{3,2,1,0:T(8,128)(2,1)S(1)}, u32[]{:S(2)}, u32[]{:S(2)}) %all-to-all-start.3) | async-done | bytes 1048608 | tf_op jit(solution)/shard_map/all_to_all | solution.py:354
  146.2 1.0 copy-done.1
  147.2 2.2 %unpack.1 = (bf16[1,128,1536]{2,1,0:T(8,128)(2,1)}, bf16[1,128,1536]{2,1,0:T(8,128)(2,1)}) custom-call(bf16[16,2,128,128]{3,2,1,0:T(8,128)(2,1)} %copy-done.1), custom_call_target="tpu_custom_call" | custom-call | bytes 4194304 | tf_op jit(solution)/shard_map/unpack/pallas_call | solution.py:51
  (5 shorter events, 0.0 us)
Async XLA Ops:
  39.8 4.7 %copy-start = (bf16[16,2,128,128]{3,2,1,0:T(8,128)(2,1)}, bf16[16,2,128,128]{3,2,1,0:T(8,128)(2,1)S(1)}, u32[]{:S(2)}) copy-start(bf16[16,2,128,128]{3,2,1,0:T(8,128)(2,1)S(1)} %all_to_all.20.kv_ref) | copy-start | bytes 3145732
  39.9 30.3 %all-to-all-start.1 = ((bf16[16,2,128,128]{3,2,1,0:T(8,128)(2,1)}), bf16[16,2,128,128]{3,2,1,0:T(8,128)(2,1)S(1)}, u32[]{:S(2)}, u32[]{:S(2)}) async-start(bf16[16,2,128,128]{3,2,1,0:T(8,128)(2,1)} %get-tuple-element.16), calls=%async_computation.1 | async-start | bytes 2097152 | tf_op jit(solution)/shard_map/all_to_all | solution.py:354
  44.5 25.6 %collective-permute-start.1 = (bf16[8,2,128,128]{3,2,1,0:T(8,128)(2,1)S(1)}, bf16[8,2,128,128]{3,2,1,0:T(8,128)(2,1)S(1)}, u32[]{:S(2)}, u32[]{:S(2)}) collective-permute-start(bf16[8,2,128,128]{3,2,1,0:T(8,128)(2,1)S(1)} %get-tuple-element.25), channel_id=1, source_target_pairs={{16,0},{32,16},{48,32},{17,1},{33,17},{49,33},{18,2},{34,18},{50,3... | collective-permute-start | bytes 1572872 | tf_op jit(solution)/shard_map/ppermute | solution.py:378
  47.0 23.1 %collective-permute-start = (bf16[8,2,128,128]{3,2,1,0:T(8,128)(2,1)S(1)}, bf16[8,2,128,128]{3,2,1,0:T(8,128)(2,1)S(1)}, u32[]{:S(2)}, u32[]{:S(2)}) collective-permute-start(bf16[8,2,128,128]{3,2,1,0:T(8,128)(2,1)S(1)} %get-tuple-element.26), channel_id=1, source_target_pairs={{0,16},{16,32},{32,48},{1,17},{17,33},{33,49},{2,18},{18,34},{34,5... | collective-permute-start | bytes 1572872 | tf_op jit(solution)/shard_map/ppermute | solution.py:377
  70.1 1.0 copy-start.3
  70.1 1.1 copy-start.6
  70.1 1.3 copy-start.7
  84.1 28.6 %all-to-all-start.2 = ((bf16[16,144,128]{2,1,0:T(8,128)(2,1)}), bf16[16,144,128]{2,1,0:T(8,128)(2,1)S(1)}, u32[]{:S(2)}, u32[]{:S(2)}) async-start(bf16[16,144,128]{2,1,0:T(8,128)(2,1)} %get-tuple-element.17), calls=%async_computation.2 | async-start | bytes 1179648 | tf_op jit(solution)/shard_map/all_to_all | solution.py:354
  89.4 15.7 %collective-permute-start.2 = (bf16[8,2,128,128]{3,2,1,0:T(8,128)(2,1)}, bf16[8,2,128,128]{3,2,1,0:T(8,128)(2,1)S(1)}, u32[]{:S(2)}, u32[]{:S(2)}) collective-permute-start(bf16[8,2,128,128]{3,2,1,0:T(8,128)(2,1)} %get-tuple-element.20), channel_id=1, source_target_pairs={{0,16},{16,32},{32,48},{1,17},{17,33},{33,49},{2,18},{18,34},{34,5... | collective-permute-start | bytes 1572872 | tf_op jit(solution)/shard_map/ppermute | solution.py:382
  92.8 15.4 %collective-permute-start.3 = (bf16[8,2,128,128]{3,2,1,0:T(8,128)(2,1)}, bf16[8,2,128,128]{3,2,1,0:T(8,128)(2,1)S(1)}, u32[]{:S(2)}, u32[]{:S(2)}) collective-permute-start(bf16[8,2,128,128]{3,2,1,0:T(8,128)(2,1)} %get-tuple-element.21), channel_id=1, source_target_pairs={{16,0},{32,16},{48,32},{17,1},{33,17},{49,33},{18,2},{34,18},{50,3... | collective-permute-start | bytes 1572872 | tf_op jit(solution)/shard_map/ppermute | solution.py:383
  105.1 3.1 %copy-start.4 = (bf16[8,2,128,128]{3,2,1,0:T(8,128)(2,1)}, bf16[8,2,128,128]{3,2,1,0:T(8,128)(2,1)S(1)}, u32[]{:S(2)}) copy-start(bf16[8,2,128,128]{3,2,1,0:T(8,128)(2,1)S(1)} %collective-permute-done.2.low_ref) | copy-start | bytes 1572868
  108.2 0.8 copy-start.5
  112.8 7.8 %copy-start.2 = (bf16[16,144,128]{2,1,0:T(8,128)(2,1)}, bf16[16,144,128]{2,1,0:T(8,128)(2,1)S(1)}, u32[]{:S(2)}) copy-start(bf16[16,144,128]{2,1,0:T(8,128)(2,1)S(1)} %all-to-all-done.2.in_ref) | copy-start | bytes 1769476
  112.8 33.4 %all-to-all-start.3 = ((bf16[16,2,128,128]{3,2,1,0:T(8,128)(2,1)}), bf16[16,2,128,128]{3,2,1,0:T(8,128)(2,1)S(1)}, u32[]{:S(2)}, u32[]{:S(2)}) async-start(bf16[16,2,128,128]{3,2,1,0:T(8,128)(2,1)} %finish.1), calls=%async_computation.3 | async-start | bytes 2097152 | tf_op jit(solution)/shard_map/all_to_all | solution.py:354
  122.5 4.8 %collective-permute-start.6 = (f32[8,128]{1,0:T(8,128)}, f32[8,128]{1,0:T(8,128)S(1)}, u32[]{:S(2)}, u32[]{:S(2)}) collective-permute-start(f32[8,128]{1,0:T(8,128)} %get-tuple-element.24), channel_id=1, source_target_pairs={{0,192},{64,128},{128,64},{192,0},{1,193},{65,129},{129,65},{193,1... | collective-permute-start | bytes 12296 | tf_op jit(solution)/shard_map/ppermute | solution.py:361
  123.0 5.4 %collective-permute-start.5 = (f32[8,128]{1,0:T(8,128)}, f32[8,128]{1,0:T(8,128)S(1)}, u32[]{:S(2)}, u32[]{:S(2)}) collective-permute-start(f32[8,128]{1,0:T(8,128)} %get-tuple-element.24), channel_id=1, source_target_pairs={{0,128},{64,192},{128,0},{192,64},{1,129},{65,193},{129,1},{193,65... | collective-permute-start | bytes 12296 | tf_op jit(solution)/shard_map/ppermute | solution.py:361
  125.5 3.0 %collective-permute-start.4 = (f32[8,128]{1,0:T(8,128)}, f32[8,128]{1,0:T(8,128)S(1)}, u32[]{:S(2)}, u32[]{:S(2)}) collective-permute-start(f32[8,128]{1,0:T(8,128)} %get-tuple-element.24), channel_id=1, source_target_pairs={{0,64},{64,0},{128,192},{192,128},{1,65},{65,1},{129,193},{193,129... | collective-permute-start | bytes 12296 | tf_op jit(solution)/shard_map/ppermute | solution.py:361
  129.1 4.1 %collective-permute-start.9 = (f32[8,128]{1,0:T(8,128)S(1)}, f32[8,128]{1,0:T(8,128)S(1)}, u32[]{:S(2)}, u32[]{:S(2)}) collective-permute-start(f32[8,128]{1,0:T(8,128)S(1)} %add_add_fusion.1), channel_id=1, source_target_pairs={{0,48},{16,32},{32,16},{48,0},{1,49},{17,33},{33,17},{49,1},{2,50}... | collective-permute-start | bytes 12296 | tf_op jit(solution)/shard_map/ppermute | solution.py:361
  130.3 5.1 %collective-permute-start.8 = (f32[8,128]{1,0:T(8,128)S(1)}, f32[8,128]{1,0:T(8,128)S(1)}, u32[]{:S(2)}, u32[]{:S(2)}) collective-permute-start(f32[8,128]{1,0:T(8,128)S(1)} %add_add_fusion.1), channel_id=1, source_target_pairs={{0,32},{16,48},{32,0},{48,16},{1,33},{17,49},{33,1},{49,17},{2,34}... | collective-permute-start | bytes 12296 | tf_op jit(solution)/shard_map/ppermute | solution.py:361
  131.7 3.7 %collective-permute-start.7 = (f32[8,128]{1,0:T(8,128)S(1)}, f32[8,128]{1,0:T(8,128)S(1)}, u32[]{:S(2)}, u32[]{:S(2)}) collective-permute-start(f32[8,128]{1,0:T(8,128)S(1)} %add_add_fusion.1), channel_id=1, source_target_pairs={{0,16},{16,0},{32,48},{48,32},{1,17},{17,1},{33,49},{49,33},{2,18}... | collective-permute-start | bytes 12296 | tf_op jit(solution)/shard_map/ppermute | solution.py:361
  146.2 1.0 copy-start.1

commit v3 on v2

v3 whole, which is shorter than its diff:
```python
import functools

import jax
import jax.numpy as jnp
from jax import lax
from jax.experimental import pallas as pl
from jax.experimental.pallas import tpu as pltpu
from jax.sharding import Mesh
from jax.sharding import PartitionSpec as P

HEADS = 12
HD = 128
TILE = 64
PAIR = 2 * TILE
GROUP = 16
HALF = 8
COLS = 4
EXTRA = 16
WIDE = 8
EPSILON = 1e-06
SCALE = HD ** (-0.5)
SCALE_LOG2E = SCALE * 1.4426950408889634
F32 = jnp.float32
BF16 = jnp.bfloat16
LIMIT = 60 * 1024 * 1024
SMALL = 8 * 1024 * 1024
FINISH_LIMIT = 52 * 1024 * 1024


def nt(left, right):
    return lax.dot_general(left, right, (((1,), (1,)), ((), ())), preferred_element_type=F32)


def nn(left, right):
    return lax.dot_general(left, right, (((1,), (0,)), ((), ())), preferred_element_type=F32)


def inverse_rms(inputs):
    return lax.rsqrt(jnp.mean(inputs * inputs, axis=-1, keepdims=True) + EPSILON)


def norm_back(inputs, inverse, gain, cotangent):
    scaled = cotangent * gain
    mean = jnp.mean(inputs * scaled, axis=-1, keepdims=True)
    return inverse * scaled - inputs * (inverse * inverse * inverse * mean)


def pack_kernel(first_ref, second_ref, out_ref, sem):
    copies = []
    for head in range(HEADS):
        lanes = pl.ds(head * HD, HD)
        for number, source in enumerate((first_ref, second_ref)):
            copies.append(pltpu.make_async_copy(source.at[0, :, lanes], out_ref.at[head, number], sem))
    for copy in copies:
        copy.start()
    for head in range(HEADS, GROUP):
        out_ref[head] = jnp.zeros(out_ref.shape[1:], out_ref.dtype)
    for copy in copies:
        copy.wait()


def pack(first, second):
    return pl.pallas_call(
        pack_kernel,
        in_specs=[pl.BlockSpec(memory_space=pl.ANY)] * 2,
        out_specs=pl.BlockSpec(memory_space=pltpu.VMEM),
        out_shape=jax.ShapeDtypeStruct((GROUP, 2, PAIR, HD), BF16),
        scratch_shapes=[pltpu.SemaphoreType.DMA],
        name="pack",
        compiler_params=pltpu.CompilerParams(vmem_limit_bytes=LIMIT),
    )(first, second)


def spread(parts):
    return parts[0] + jnp.concatenate(parts[1:], axis=1)


def raw_column(source, w, frame, col):
    place = slice((w % 2) * TILE, (w % 2 + 1) * TILE)
    rows = [source[frame, row, col, 0, place] for row in range(2)]
    return jnp.concatenate(rows, axis=0).astype(F32)


def attention_kernel(
    flags_ref,
    kv_hbm,
    low_hbm,
    high_hbm,
    qd_hbm,
    q_gain_ref,
    k_gain_ref,
    dq_hbm,
    own_hbm,
    to_low_hbm,
    to_high_hbm,
    kv_ref,
    low_ref,
    high_ref,
    qd_ref,
    dq_ref,
    own_ref,
    to_low,
    to_high,
    in_sems,
    out_sem,
    kn_own,
    knt_own,
    vv_own,
    kn_l,
    knt_l,
    vv_l,
    kn_h,
    knt_h,
    vv_h,
    qn,
    dd,
    q_side,
    d_side,
    chance_own,
    chance_l,
    chance_h,
    score_own,
    score_l,
    score_h,
    gains_ref,
):
    arrivals = []
    for col in range(COLS):
        pairs = ((kv_hbm, kv_ref), (low_hbm, low_ref), (high_hbm, high_ref), (qd_hbm, qd_ref))
        copies = [
            pltpu.make_async_copy(source.at[:, :, col], target.at[:, :, col], in_sems.at[col])
            for source, target in pairs
        ]
        for copy in copies:
            copy.start()
        arrivals.append(copies)
    departures = []

    def send(source, target):
        copy = pltpu.make_async_copy(source, target, out_sem)
        copy.start()
        departures.append(copy)

    q_gain = q_gain_ref[...]
    k_gain = k_gain_ref[...]
    def prepare(col):
        for copy in arrivals[col]:
            copy.wait()
        for source, frames, kn, knt, vv in (
            (kv_ref, 2, kn_own, knt_own, vv_own),
            (low_ref, 1, kn_l, knt_l, vv_l),
            (high_ref, 1, kn_h, knt_h, vv_h),
        ):
            for frame in range(frames):
                for row in range(2):
                    raw = source[frame, row, col, 0].astype(F32)
                    normed = (raw * inverse_rms(raw) * k_gain).astype(BF16)
                    for part in range(2):
                        at = ((2 * col + part) * frames + frame) * PAIR + row * TILE
                        kn[at : at + TILE] = normed[part * TILE : (part + 1) * TILE]
                        vv[at : at + TILE] = source[frame, row, col, 1, part * TILE : (part + 1) * TILE]
            for block in range(2 * col * frames, 2 * (col + 1) * frames):
                rows = slice(block * PAIR, (block + 1) * PAIR)
                knt[:, rows] = kn[rows].T
        for frame in range(2):
            for row in range(2):
                raw = qd_ref[frame, row, col, 0].astype(F32)
                normed = (raw * inverse_rms(raw) * q_gain).astype(BF16)
                for part in range(2):
                    place = slice(part * TILE, (part + 1) * TILE)
                    at = ((2 * col + part) * 2 + frame) * PAIR + row * TILE
                    qn[at : at + TILE] = normed[place]
                    dd[at : at + TILE] = qd_ref[frame, row, col, 1, place]
                    at = (2 * col + part) * PAIR + row * TILE
                    q_side[frame, at : at + TILE] = normed[place]
                    d_side[frame, at : at + TILE] = qd_ref[frame, row, col, 1, place]

    gains_ref[...] = jnp.zeros_like(gains_ref)
    sources = (
        (kn_own, knt_own, vv_own, chance_own, score_own, 2, 0, 2 * PAIR, None),
        (kn_l, knt_l, vv_l, chance_l, score_l, 1, 0, PAIR, flags_ref[0].astype(F32)),
        (kn_h, knt_h, vv_h, chance_h, score_h, 1, PAIR, PAIR, flags_ref[1].astype(F32)),
    )

    def first_half(w, before, count):
        q_rows = pl.ds(w * (2 * PAIR), 2 * PAIR)
        q_tile = qn[q_rows]
        d_tile = dd[q_rows]
        weights, weight_grads, sums = [], [], []
        for kn, _, vv, _, _, frames, first, width, valid in sources:
            rows = pl.ds((w - before) * (frames * PAIR), count * frames * PAIR)
            queries = slice(first, first + width)
            weight = jnp.exp2(nt(kn[rows], q_tile[queries]) * SCALE_LOG2E)
            if valid is not None:
                weight = weight * valid
            weights.append(weight)
            sums.append(jnp.sum(weight, axis=0, keepdims=True))
            weight_grads.append(nt(vv[rows], d_tile[queries]))
        return q_tile, d_tile, weights, weight_grads, sums

    def second_half(w, before, count, q_tile, d_tile, weights, weight_grads, sums):
        reciprocal = 1.0 / spread(sums)
        chances, dots = [], []
        for number, (_, _, _, store, _, frames, first, width, _) in enumerate(sources):
            chance = weights[number] * reciprocal[:, first : first + width]
            rounded = chance.astype(BF16)
            dots.append(jnp.sum(rounded.astype(F32) * weight_grads[number], axis=0, keepdims=True))
            chances.append(chance)
            for step in range(count):
                place = (1 - (step - before)) * width
                store[w - before + step, :, place : place + width] = rounded[
                    step * frames * PAIR : (step + 1) * frames * PAIR
                ]
        row_dot = spread(dots)
        grads = []
        for number, (_, knt, _, _, store, frames, first, width, _) in enumerate(sources):
            score = chances[number] * (weight_grads[number] - row_dot[:, first : first + width])
            score = score.astype(BF16)
            for step in range(count):
                place = (1 - (step - before)) * width
                store[w - before + step, :, place : place + width] = score[
                    step * frames * PAIR : (step + 1) * frames * PAIR
                ]
            lanes = pl.ds((w - before) * (frames * PAIR), count * frames * PAIR)
            grads.append(nn(knt[:, lanes], score))
        grad = spread(grads).T * SCALE
        col = w // 2
        place = pl.ds((w % 2) * TILE, TILE)
        for frame in range(2):
            for row in range(2):
                raw = qd_ref[frame, row, col, 0, place].astype(F32)
                inverse = inverse_rms(raw)
                part = grad[frame * PAIR + row * TILE : frame * PAIR + (row + 1) * TILE]
                gains_ref[...] += jnp.sum((part * raw * inverse).reshape(-1, 8, HD), axis=0)
                dq_ref[frame, row, col, place] = norm_back(raw, inverse, q_gain, part).astype(BF16)
        if w % 2:
            send(dq_ref.at[:, :, col, :PAIR], dq_hbm.at[:, :, col, :PAIR])

    def key_sums(chance, score, queries, cotangents, w, width):
        first, last = max(w - 1, 0), min(w + 1, WIDE - 1)
        lanes = slice((first - w + 1) * width, (last - w + 2) * width)
        rows = slice(first * width, (last + 1) * width)
        value_grad = nn(chance[w, :, lanes], cotangents[rows])
        key_grad = nn(score[w, :, lanes], queries[rows]) * SCALE
        return key_grad, value_grad

    def gain_part(key_grad, raw):
        return jnp.sum((key_grad * raw * inverse_rms(raw)).reshape(-1, 8, HD), axis=0)

    sides = (
        (chance_l, score_l, low_ref, to_low, to_low_hbm),
        (chance_h, score_h, high_ref, to_high, to_high_hbm),
    )

    def key_column(w, gain_sum):
        for frame, (chance, score, raw_ref, out_ref, out_hbm) in enumerate(sides):
            key_grad, value_grad = key_sums(chance, score, q_side.at[frame], d_side.at[frame], w, PAIR)
            out_ref[w, 0] = key_grad.astype(BF16)
            out_ref[w, 1] = value_grad.astype(BF16)
            send(out_ref.at[w], out_hbm.at[w])
            gain_sum += gain_part(key_grad, raw_column(raw_ref, w, 0, w // 2))
        key_grad, value_grad = key_sums(chance_own, score_own, qn, dd, w, 2 * PAIR)
        own_ref[w, 0] = key_grad.astype(BF16)
        own_ref[w, 1] = value_grad.astype(BF16)
        for frame in range(2):
            gain_sum += gain_part(key_grad[frame * PAIR : (frame + 1) * PAIR], raw_column(kv_ref, w, frame, w // 2))
        send(own_ref.at[w], own_hbm.at[w])
        return gain_sum

    def extent(w):
        return w, min(w, 1), 2 if w in (0, WIDE - 1) else 3

    gain_sum = jnp.zeros((8, HD), F32)
    prepare(0)
    held = first_half(*extent(0))
    for w in range(WIDE):
        if w % 2 == 0 and w // 2 + 1 < COLS:
            prepare(w // 2 + 1)
        following = first_half(*extent(w + 1)) if w + 1 < WIDE else None
        second_half(*extent(w), *held)
        held = following
        if w > 0:
            gain_sum = key_column(w - 1, gain_sum)
    gain_sum = key_column(WIDE - 1, gain_sum)


    q_sum = jnp.sum(gains_ref[...], axis=0, keepdims=True)
    k_sum = jnp.sum(gain_sum, axis=0, keepdims=True)
    lines = []
    for line in (q_sum, k_sum):
        line = jnp.where(flags_ref[2] > 0, line, 0.0)
        for _ in range(3):
            rounded = line.astype(BF16).astype(F32)
            lines.append(rounded)
            line = line - rounded
    lines.append(jnp.zeros((EXTRA - 6, HD), F32))
    block = jnp.concatenate(lines, axis=0).astype(BF16)
    dq_ref[:, :, :, PAIR:] = jnp.broadcast_to(block, (2, 2, COLS, EXTRA, HD))
    send(dq_ref.at[:, :, :, PAIR:], dq_hbm.at[:, :, :, PAIR:])
    for copy in departures:
        copy.wait()


def grid_of(array):
    return array.reshape((-1, 2, COLS) + array.shape[1:])


def attention(flags, kv, low, high, qd, q_gain, k_gain):
    own, halo = WIDE * 2 * PAIR, WIDE * PAIR
    arrays = [grid_of(array) for array in (kv, low, high, qd)]
    outs = [((2, 2, COLS, PAIR + EXTRA, HD), BF16), ((WIDE, 2, 2 * PAIR, HD), BF16)]
    outs += [((WIDE, 2, PAIR, HD), BF16)] * 2
    scratch = [pltpu.VMEM(array.shape, BF16) for array in arrays]
    scratch += [pltpu.VMEM(*out) for out in outs]
    scratch += [pltpu.SemaphoreType.DMA((COLS,)), pltpu.SemaphoreType.DMA]
    for rows in (own, halo, halo):
        scratch += [pltpu.VMEM((rows, HD), BF16), pltpu.VMEM((HD, rows), BF16), pltpu.VMEM((rows, HD), BF16)]
    scratch += [pltpu.VMEM((own, HD), BF16)] * 2 + [pltpu.VMEM((2, halo, HD), BF16)] * 2
    stores = [pltpu.VMEM((WIDE, 2 * PAIR, 6 * PAIR), BF16)] + [pltpu.VMEM((WIDE, PAIR, 3 * PAIR), BF16)] * 2
    scratch += stores + stores + [pltpu.VMEM((8, HD), F32)]
    dq, own, to_low, to_high = pl.pallas_call(
        attention_kernel,
        in_specs=[pl.BlockSpec(memory_space=pltpu.SMEM)]
        + [pl.BlockSpec(memory_space=pl.ANY)] * 4
        + [pl.BlockSpec(memory_space=pltpu.VMEM)] * 2,
        out_specs=[pl.BlockSpec(memory_space=pl.ANY)] * 4,
        out_shape=[pltpu.HBM(*out) for out in outs],
        scratch_shapes=scratch,
        name="attention",
        cost_estimate=pl.CostEstimate(
            flops=5 * 66 * PAIR * PAIR * PAIR * 2, bytes_accessed=8 << 20, transcendentals=0
        ),
        compiler_params=pltpu.CompilerParams(vmem_limit_bytes=FINISH_LIMIT),
    )(flags, *arrays, q_gain, k_gain)
    return dq.reshape(GROUP, PAIR + EXTRA, HD), own, to_low, to_high


def finish_kernel(frame, kv_hbm, own_hbm, halo_hbm, k_gain_ref, out_hbm, kv_ref, own_ref, halo_ref, out_ref, in_sems, out_sem):
    rows = slice(frame * PAIR, (frame + 1) * PAIR)
    arrivals = []
    for col in range(COLS):
        columns = slice(2 * col, 2 * col + 2)
        pairs = (
            (halo_hbm.at[columns], halo_ref.at[columns]),
            (kv_hbm.at[frame, :, col], kv_ref.at[0, :, col]),
            (own_hbm.at[columns, :, rows], own_ref.at[columns]),
        )
        copies = [pltpu.make_async_copy(source, target, in_sems.at[col]) for source, target in pairs]
        for copy in copies:
            copy.start()
        arrivals.append(copies)
    k_gain = k_gain_ref[...]
    departures = []
    for col in range(COLS):
        for copy in arrivals[col]:
            copy.wait()
        for part in range(2):
            w = 2 * col + part
            place = slice(part * TILE, (part + 1) * TILE)
            raw = raw_column(kv_ref, w, 0, col)
            key_grad = own_ref[w, 0].astype(F32) + halo_ref[w, 0].astype(F32)
            value_grad = (own_ref[w, 1].astype(F32) + halo_ref[w, 1].astype(F32)).astype(BF16)
            key_grad = norm_back(raw, inverse_rms(raw), k_gain, key_grad).astype(BF16)
            for row in range(2):
                out_ref[row, col, 0, place] = key_grad[row * TILE : (row + 1) * TILE]
                out_ref[row, col, 1, place] = value_grad[row * TILE : (row + 1) * TILE]
        copy = pltpu.make_async_copy(out_ref.at[:, col], out_hbm.at[frame, :, col], out_sem)
        copy.start()
        departures.append(copy)
    for copy in departures:
        copy.wait()


def second_finish_kernel(kv_hbm, own_hbm, halo_hbm, k_gain_ref, first_hbm, *refs):
    finish_kernel(1, kv_hbm, own_hbm, halo_hbm, k_gain_ref, *refs)


def finish(frame, kv, own, halo, k_gain, first=None):
    half = (2, COLS, 2, PAIR, HD)
    arguments = [grid_of(kv), own, halo, k_gain]
    in_specs = [pl.BlockSpec(memory_space=pl.ANY)] * 3 + [pl.BlockSpec(memory_space=pltpu.VMEM)]
    aliases = {}
    if frame:
        arguments.append(first)
        in_specs.append(pl.BlockSpec(memory_space=pl.ANY))
        aliases = {4: 0}
    return pl.pallas_call(
        second_finish_kernel if frame else functools.partial(finish_kernel, 0),
        in_specs=in_specs,
        out_specs=pl.BlockSpec(memory_space=pl.ANY),
        out_shape=pltpu.HBM((2,) + half, BF16),
        scratch_shapes=[
            pltpu.VMEM((1,) + half, BF16),
            pltpu.VMEM((WIDE, 2, PAIR, HD), BF16),
            pltpu.VMEM((WIDE, 2, PAIR, HD), BF16),
            pltpu.VMEM(half, BF16),
            pltpu.SemaphoreType.DMA((COLS,)),
            pltpu.SemaphoreType.DMA,
        ],
        input_output_aliases=aliases,
        name="finish_high" if frame else "finish_low",
        compiler_params=pltpu.CompilerParams(vmem_limit_bytes=FINISH_LIMIT),
    )(*arguments)


def unpack_query_kernel(in_ref, out_ref, lines_ref):
    for head in range(HEADS):
        out_ref[0, :, head * HD : (head + 1) * HD] = in_ref[head, :PAIR]
    total = in_ref[0, PAIR:].astype(F32)
    for index in range(1, GROUP):
        total = total + in_ref[index, PAIR:].astype(F32)
    sums = [jnp.sum(total[first : first + 3], axis=0, keepdims=True) for first in (0, 3)]
    lines_ref[...] = jnp.concatenate(sums + [jnp.zeros((6, HD), F32)], axis=0)


def unpack_query(arrived):
    tokens = jax.ShapeDtypeStruct((1, PAIR, HEADS * HD), BF16)
    return pl.pallas_call(
        unpack_query_kernel,
        out_shape=[tokens, jax.ShapeDtypeStruct((8, HD), F32)],
        name="unpack_query",
        compiler_params=pltpu.CompilerParams(vmem_limit_bytes=SMALL),
    )(arrived)


def unpack_kernel(in_ref, key_ref, value_ref, sem):
    copies = []
    for head in range(HEADS):
        lanes = pl.ds(head * HD, HD)
        for number, target in enumerate((key_ref, value_ref)):
            copies.append(pltpu.make_async_copy(in_ref.at[head, number], target.at[0, :, lanes], sem))
    for copy in copies:
        copy.start()
    for copy in copies:
        copy.wait()


def unpack(arrived):
    out = pltpu.HBM((1, PAIR, HEADS * HD), BF16)
    return pl.pallas_call(
        unpack_kernel,
        in_specs=[pl.BlockSpec(memory_space=pltpu.VMEM)],
        out_specs=[pl.BlockSpec(memory_space=pl.ANY)] * 2,
        out_shape=[out, out],
        scratch_shapes=[pltpu.SemaphoreType.DMA],
        name="unpack",
        compiler_params=pltpu.CompilerParams(vmem_limit_bytes=SMALL),
    )(arrived)


def swap(array):
    return lax.all_to_all(array, "g", 0, 0)


def sum_over(lines, axis, steps):
    count = lax.axis_size(axis)
    total = lines
    for step in steps:
        total = total + lax.ppermute(lines, axis, [(source, source ^ step) for source in range(count)])
    return total


def on_device(blocks, q_raw, k_raw, values, d_out, q_gain, k_gain):
    block = lax.axis_index("x")
    member = lax.axis_index("g")
    flags = jnp.stack([block > 0, block < blocks - 1, member < HEADS]).astype(jnp.int32)
    up = [(source, source + 1) for source in range(blocks - 1)]
    down = [(source + 1, source) for source in range(blocks - 1)]
    q_line = q_gain.reshape(1, HD)
    k_line = k_gain.reshape(1, HD)

    kv = swap(pack(k_raw, values))
    low = lax.ppermute(kv[HALF:], "x", up)
    high = lax.ppermute(kv[:HALF], "x", down)
    qd = swap(pack(q_raw, d_out))
    dq, own, to_low, to_high = attention(flags, kv, low, high, qd, q_line, k_line)
    arrived = swap(dq)
    from_low = lax.ppermute(to_high, "x", up)
    from_high = lax.ppermute(to_low, "x", down)
    q_grad, lines = unpack_query(arrived)
    grads = finish(0, kv, own, from_low, k_line)
    grads = finish(1, kv, own, from_high, k_line, grads).reshape(GROUP, 2, PAIR, HD)
    k_grad, v_grad = unpack(swap(grads))
    lines = sum_over(lines, "dp", (1, 2, 3))
    lines = sum_over(lines, "x", (1, 2, 3))
    return (q_grad, k_grad, v_grad, lines[0], lines[1])


def solution(mesh):
    videos, seq = mesh.devices.shape
    blocks = seq // GROUP
    split = Mesh(mesh.devices.reshape(videos, blocks, GROUP), ("dp", "x", "g"))
    tokens = P("dp", ("x", "g"), None)
    return jax.shard_map(
        functools.partial(on_device, blocks),
        mesh=split,
        in_specs=(tokens, tokens, tokens, tokens, P(), P()),
        out_specs=(tokens, tokens, tokens, P(), P()),
        check_vma=False,
    )
```

time: 150 us -> 145 us (0.967)
  blocking collectives: 36.5 us -> 0 us
  waiting for transfers between devices: 47 us -> 72.7 us
  starting transfers between devices: 36.8 us -> 45.9 us
  local copies, waits for them, and re-layouts: 3.74 us -> 1.57 us
    all_to_all x1 -> x0, blocking collectives: 36.5 us -> none  [swap(): return lax.all_to_all(array, 'g', 0, 0)]
    all_to_all x3 -> x4, waiting for transfers between devices: 29.4 us -> 57.9 us  [swap(): return lax.all_to_all(array, 'g', 0, 0)]
    all_to_all x3 -> x4, starting transfers between devices: 17.6 us -> 26.4 us  [swap(): return lax.all_to_all(array, 'g', 0, 0)]
    ppermute x1, waiting for transfers between devices: 3.12 us -> 0.33 us  [on_device(): from_high = lax.ppermute(to_low, 'x', down)]
    unnamed x16 -> x10, local copies, waits for them, and re-layouts: 3.12 us -> 0.98 us
    pallas_call x1 -> x2, Pallas kernels: 2.68 us -> 4.18 us  [pack(): pl.pallas_call(pack_kernel, in_specs=[pl.BlockSpec(memory_space=pl.ANY)]...]
    pallas_call x4 -> x5, Pallas kernels: 20.6 us -> 19.2 us  [the longest x1 11.9 us: attention(): pl.pallas_call(attention_kernel, in_specs=[pl.BlockSpec(memory_space=pltp...]
  transfers between devices with their start and end apart: 13 -> 14, of which waited for: 7 -> 8; matrix products, arithmetic and copies ran while one was open for 1% -> 0% of each run, Pallas kernels for 4% -> 6%
where the time goes in v3:
time: 145 us
  waiting for transfers between devices  72.7 us (50%)
  starting transfers between devices  45.9 us (32%)
  Pallas kernels  23.4 us (16%)
  local copies, waits for them, and re-layouts  1.57 us (1%)
    all_to_all x4, waiting for transfers between devices, swap(): return lax.all_to_all(array, 'g', 0, 0)  57.9 us
    all_to_all x4, starting transfers between devices, swap(): return lax.all_to_all(array, 'g', 0, 0)  26.4 us
    pallas_call x1, Pallas kernels, attention(): pl.pallas_call(attention_kernel, in_specs=[pl.BlockSpec(memory_space=pltp...  11.9 us
    ppermute x1, waiting for transfers between devices, on_device(): from_low = lax.ppermute(to_high, 'x', up)  9.55 us
    ppermute x6, starting transfers between devices, sum_over(): lax.ppermute(lines, axis, [(source, source ^ step) for source in range(co...  7.55 us
    pallas_call x2, Pallas kernels, finish(): pl.pallas_call(second_finish_kernel if frame else functools.partial(finis...  5.57 us
    ppermute x6, waiting for transfers between devices, sum_over(): lax.ppermute(lines, axis, [(source, source ^ step) for source in range(co...  4.96 us
    pallas_call x2, Pallas kernels, pack(): pl.pallas_call(pack_kernel, in_specs=[pl.BlockSpec(memory_space=pl.ANY)]...  4.18 us
  transfers between devices with their start and end apart: 14, of which 8 were waited for; matrix products, arithmetic and copies ran while one was open for 0% of the time, Pallas kernels for 6%

profile of v3, /device:TPU:2, one launch (start us, length us, event | category | flops | bytes accessed | tf_op | source)
XLA Modules:
  0.0 144.6 jit_solution(17486669940742215260)
XLA Ops:
  0.6 2.1 %pack.2 = bf16[16,2,128,128]{3,2,1,0:T(8,128)(2,1)} custom-call(bf16[1,128,1536]{2,1,0:T(8,128)(2,1)} %first_ref.2, bf16[1,128,1536]{2,1,0:T(8,128)(2,1)} %second_ref.2), custom_call_target="tpu_custom_call" | custom-call | tf_op jit(solution)/shard_map/pack/pallas_call | solution.py:63
  2.8 9.6 %all-to-all-start = ((bf16[16,2,128,128]{3,2,1,0:T(8,128)(2,1)}), bf16[16,2,128,128]{3,2,1,0:T(8,128)(2,1)S(1)}, u32[]{:S(2)}, u32[]{:S(2)}) async-start(bf16[16,2,128,128]{3,2,1,0:T(8,128)(2,1)} %pack.2), calls=%async_computation | async-start | bytes 2097152 | tf_op jit(solution)/shard_map/all_to_all | solution.py:452
  12.4 2.1 %pack.3 = bf16[16,2,128,128]{3,2,1,0:T(8,128)(2,1)} custom-call(bf16[1,128,1536]{2,1,0:T(8,128)(2,1)} %first_ref.3, bf16[1,128,1536]{2,1,0:T(8,128)(2,1)} %second_ref.3), custom_call_target="tpu_custom_call" | custom-call | tf_op jit(solution)/shard_map/pack/pallas_call | solution.py:63
  14.4 25.0 %all-to-all-done = bf16[16,2,128,128]{3,2,1,0:T(8,128)(2,1)S(1)} async-done(((bf16[16,2,128,128]{3,2,1,0:T(8,128)(2,1)}), bf16[16,2,128,128]{3,2,1,0:T(8,128)(2,1)S(1)}, u32[]{:S(2)}, u32[]{:S(2)}) %all-to-all-start) | async-done | bytes 1048608 | tf_op jit(solution)/shard_map/all_to_all | solution.py:452
  39.4 0.0 copy-start
  39.4 4.4 %all-to-all-start.1 = ((bf16[16,2,128,128]{3,2,1,0:T(8,128)(2,1)}), bf16[16,2,128,128]{3,2,1,0:T(8,128)(2,1)S(1)}, u32[]{:S(2)}, u32[]{:S(2)}) async-start(bf16[16,2,128,128]{3,2,1,0:T(8,128)(2,1)} %pack.3), calls=%async_computation.1 | async-start | bytes 2097152 | tf_op jit(solution)/shard_map/all_to_all | solution.py:452
  43.9 0.0 copy-done
  43.9 0.1 fusion
  43.9 2.4 %collective-permute-start.1 = (bf16[8,2,128,128]{3,2,1,0:T(8,128)(2,1)S(1)}, bf16[8,2,128,128]{3,2,1,0:T(8,128)(2,1)S(1)}, u32[]{:S(2)}, u32[]{:S(2)}) collective-permute-start(bf16[8,2,128,128]{3,2,1,0:T(8,128)(2,1)S(1)} %get-tuple-element.21), channel_id=1, source_target_pairs={{16,0},{32,16},{48,32},{17,1},{33,17},{49,33},{18,2},{34,18},{50,3... | collective-permute-start | bytes 1572872 | tf_op jit(solution)/shard_map/ppermute | solution.py:474
  46.4 3.4 %collective-permute-start = (bf16[8,2,128,128]{3,2,1,0:T(8,128)(2,1)S(1)}, bf16[8,2,128,128]{3,2,1,0:T(8,128)(2,1)S(1)}, u32[]{:S(2)}, u32[]{:S(2)}) collective-permute-start(bf16[8,2,128,128]{3,2,1,0:T(8,128)(2,1)S(1)} %get-tuple-element.22), channel_id=1, source_target_pairs={{0,16},{16,32},{32,48},{1,17},{17,33},{33,49},{2,18},{18,34},{34,5... | collective-permute-start | bytes 1572872 | tf_op jit(solution)/shard_map/ppermute | solution.py:473
  49.8 0.1 add_convert_fusion.flags_ref
  49.9 21.2 %all-to-all-done.1 = bf16[16,2,128,128]{3,2,1,0:T(8,128)(2,1)S(1)} async-done(((bf16[16,2,128,128]{3,2,1,0:T(8,128)(2,1)}), bf16[16,2,128,128]{3,2,1,0:T(8,128)(2,1)S(1)}, u32[]{:S(2)}, u32[]{:S(2)}) %all-to-all-start.1) | async-done | bytes 1048608 | tf_op jit(solution)/shard_map/all_to_all | solution.py:452
  71.1 0.0 copy-start.4
  71.1 0.0 collective-permute-done.1
  71.1 0.0 collective-permute-done
  71.1 0.0 copy-start.2
  71.1 0.0 copy-start.3
  71.2 1.0 copy-done.4
  72.1 0.0 copy-done.2
  72.1 0.0 copy-done.3
  72.1 11.9 %attention.1 = (bf16[2,2,4,144,128]{4,3,2,1,0:T(8,128)(2,1)}, bf16[8,2,256,128]{3,2,1,0:T(8,128)(2,1)}, bf16[8,2,128,128]{3,2,1,0:T(8,128)(2,1)}, bf16[8,2,128,128]{3,2,1,0:T(8,128)(2,1)}) custom-call(s32[3]{0:T(128)S(1)} %add_convert_fusion.flags_ref, bf16[2,2,4,2,128,128]{5,4,3,2,1,0:T(8,128)(2,1)} %bitcast.15, ...), custom_call_target="tpu_custom_call" | custom-call | flops 1384120320 | bytes 8388608 | tf_op jit(solution)/shard_map/attention/pallas_call | solution.py:321
  84.1 0.0 copy-start.1
  84.1 4.6 %all-to-all-start.2 = ((bf16[16,144,128]{2,1,0:T(8,128)(2,1)}), bf16[16,144,128]{2,1,0:T(8,128)(2,1)S(1)}, u32[]{:S(2)}, u32[]{:S(2)}) async-start(bf16[16,144,128]{2,1,0:T(8,128)(2,1)} %bitcast.26), calls=%async_computation.2 | async-start | bytes 1179648 | tf_op jit(solution)/shard_map/all_to_all | solution.py:452
  88.7 3.4 %collective-permute-start.3 = (bf16[8,2,128,128]{3,2,1,0:T(8,128)(2,1)}, bf16[8,2,128,128]{3,2,1,0:T(8,128)(2,1)S(1)}, u32[]{:S(2)}, u32[]{:S(2)}) collective-permute-start(bf16[8,2,128,128]{3,2,1,0:T(8,128)(2,1)} %get-tuple-element.17), channel_id=1, source_target_pairs={{0,16},{16,32},{32,48},{1,17},{17,33},{33,49},{2,18},{18,34},{34,5... | collective-permute-start | bytes 1572872 | tf_op jit(solution)/shard_map/ppermute | solution.py:478
  92.1 2.7 %collective-permute-start.2 = (bf16[8,2,128,128]{3,2,1,0:T(8,128)(2,1)}, bf16[8,2,128,128]{3,2,1,0:T(8,128)(2,1)S(1)}, u32[]{:S(2)}, u32[]{:S(2)}) collective-permute-start(bf16[8,2,128,128]{3,2,1,0:T(8,128)(2,1)} %get-tuple-element.16), channel_id=1, source_target_pairs={{16,0},{32,16},{48,32},{17,1},{33,17},{49,33},{18,2},{34,18},{50,3... | collective-permute-start | bytes 1572872 | tf_op jit(solution)/shard_map/ppermute | solution.py:479
  94.7 9.5 %collective-permute-done.3.halo_hbm = bf16[8,2,128,128]{3,2,1,0:T(8,128)(2,1)S(1)} collective-permute-done((bf16[8,2,128,128]{3,2,1,0:T(8,128)(2,1)}, bf16[8,2,128,128]{3,2,1,0:T(8,128)(2,1)S(1)}, u32[]{:S(2)}, u32[]{:S(2)}) %collective-permute-start.3) | collective-permute-done | bytes 524320 | tf_op jit(solution)/shard_map/ppermute | solution.py:478
  104.3 0.0 copy-done.1
  104.3 2.8 %finish_low.1.first_hbm = bf16[2,2,4,2,128,128]{5,4,3,2,1,0:T(8,128)(2,1)} custom-call(bf16[2,2,4,2,128,128]{5,4,3,2,1,0:T(8,128)(2,1)S(1)} %bitcast.16, bf16[8,2,256,128]{3,2,1,0:T(8,128)(2,1)} %get-tuple-element.15.own_hbm, bf16[8,2,128,128]{3,2,1,0:T(8,128)(2,1)S(1)} %collective-permute-done.3.halo_hbm, f32[1,128]{1,0:T(1,128)S(1)} %bitcast.19), custom_call_target="tpu_custom_call" | custom-call | tf_op jit(solution)/shard_map/finish_low/pallas_call | solution.py:387
  107.1 0.3 collective-permute-done.2.halo_hbm
  107.4 2.8 %finish_high.1 = bf16[2,2,4,2,128,128]{5,4,3,2,1,0:T(8,128)(2,1)} custom-call(bf16[2,2,4,2,128,128]{5,4,3,2,1,0:T(8,128)(2,1)S(1)} %bitcast.17, bf16[8,2,256,128]{3,2,1,0:T(8,128)(2,1)} %get-tuple-element.15.own_hbm, bf16[8,2,128,128]{3,2,1,0:T(8,128)(2,1)S(1)} %collective-permute-done.2.halo_hbm, ...), custom_call_target="tpu_custom_call", output_to_operand_aliasing={{}: (4, {})} | custom-call | tf_op jit(solution)/shard_map/finish_high/pallas_call | solution.py:387
  110.2 0.0 all-to-all-done.2.in_ref
  110.2 7.8 %all-to-all-start.3 = ((bf16[16,2,128,128]{3,2,1,0:T(8,128)(2,1)}), bf16[16,2,128,128]{3,2,1,0:T(8,128)(2,1)S(1)}, u32[]{:S(2)}, u32[]{:S(2)}) async-start(bf16[16,2,128,128]{3,2,1,0:T(8,128)(2,1)} %bitcast.24), calls=%async_computation.3 | async-start | bytes 2097152 | tf_op jit(solution)/shard_map/all_to_all | solution.py:452
  118.1 0.8 unpack_query.1
  118.9 0.4 collective-permute-start.6
  119.3 2.5 %collective-permute-start.5 = (f32[8,128]{1,0:T(8,128)S(1)}, f32[8,128]{1,0:T(8,128)S(1)}, u32[]{:S(2)}, u32[]{:S(2)}) collective-permute-start(f32[8,128]{1,0:T(8,128)S(1)} %get-tuple-element.20), channel_id=1, source_target_pairs={{0,128},{64,192},{128,0},{192,64},{1,129},{65,193},{129,1},{193,65... | collective-permute-start | bytes 12296 | tf_op jit(solution)/shard_map/ppermute | solution.py:459
  121.8 0.4 collective-permute-start.4
  122.2 1.2 collective-permute-done.6
  123.4 1.2 collective-permute-done.5
  124.7 0.0 collective-permute-done.4
  124.7 1.6 %collective-permute-start.9 = (f32[8,128]{1,0:T(8,128)S(1)}, f32[8,128]{1,0:T(8,128)S(1)}, u32[]{:S(2)}, u32[]{:S(2)}) collective-permute-start(f32[8,128]{1,0:T(8,128)S(1)} %add_add_fusion.1), channel_id=1, source_target_pairs={{0,48},{16,32},{32,16},{48,0},{1,49},{17,33},{33,17},{49,1},{2,50}... | collective-permute-start | bytes 12296 | tf_op jit(solution)/shard_map/ppermute | solution.py:459
  126.3 1.1 collective-permute-start.8
  127.4 1.5 %collective-permute-start.7 = (f32[8,128]{1,0:T(8,128)S(1)}, f32[8,128]{1,0:T(8,128)S(1)}, u32[]{:S(2)}, u32[]{:S(2)}) collective-permute-start(f32[8,128]{1,0:T(8,128)S(1)} %add_add_fusion.1), channel_id=1, source_target_pairs={{0,16},{16,0},{32,48},{48,32},{1,17},{17,1},{33,49},{49,33},{2,18}... | collective-permute-start | bytes 12296 | tf_op jit(solution)/shard_map/ppermute | solution.py:459
  128.9 0.0 collective-permute-done.9
  128.9 2.5 %collective-permute-done.8 = f32[8,128]{1,0:T(8,128)S(1)} collective-permute-done((f32[8,128]{1,0:T(8,128)S(1)}, f32[8,128]{1,0:T(8,128)S(1)}, u32[]{:S(2)}, u32[]{:S(2)}) %collective-permute-start.8) | collective-permute-done | bytes 4128 | tf_op jit(solution)/shard_map/ppermute | solution.py:459
  131.4 0.0 collective-permute-done.7
  131.4 0.5 slice_bitcast_fusion
  131.9 11.6 %all-to-all-done.3.in_ref = bf16[16,2,128,128]{3,2,1,0:T(8,128)(2,1)S(1)} async-done(((bf16[16,2,128,128]{3,2,1,0:T(8,128)(2,1)}), bf16[16,2,128,128]{3,2,1,0:T(8,128)(2,1)S(1)}, u32[]{:S(2)}, u32[]{:S(2)}) %all-to-all-start.3) | async-done | bytes 1048608 | tf_op jit(solution)/shard_map/all_to_all | solution.py:452
  143.6 0.9 unpack.1
  (2 shorter events, 0.0 us)
Async XLA Ops:
  2.8 36.7 %all-to-all-start = ((bf16[16,2,128,128]{3,2,1,0:T(8,128)(2,1)}), bf16[16,2,128,128]{3,2,1,0:T(8,128)(2,1)S(1)}, u32[]{:S(2)}, u32[]{:S(2)}) async-start(bf16[16,2,128,128]{3,2,1,0:T(8,128)(2,1)} %pack.2), calls=%async_computation | async-start | bytes 2097152 | tf_op jit(solution)/shard_map/all_to_all | solution.py:452
  39.4 4.4 %copy-start = (bf16[16,2,128,128]{3,2,1,0:T(8,128)(2,1)}, bf16[16,2,128,128]{3,2,1,0:T(8,128)(2,1)S(1)}, u32[]{:S(2)}) copy-start(bf16[16,2,128,128]{3,2,1,0:T(8,128)(2,1)S(1)} %all-to-all-done) | copy-start | bytes 3145732
  39.4 31.7 %all-to-all-start.1 = ((bf16[16,2,128,128]{3,2,1,0:T(8,128)(2,1)}), bf16[16,2,128,128]{3,2,1,0:T(8,128)(2,1)S(1)}, u32[]{:S(2)}, u32[]{:S(2)}) async-start(bf16[16,2,128,128]{3,2,1,0:T(8,128)(2,1)} %pack.3), calls=%async_computation.1 | async-start | bytes 2097152 | tf_op jit(solution)/shard_map/all_to_all | solution.py:452
  43.9 27.2 %collective-permute-start.1 = (bf16[8,2,128,128]{3,2,1,0:T(8,128)(2,1)S(1)}, bf16[8,2,128,128]{3,2,1,0:T(8,128)(2,1)S(1)}, u32[]{:S(2)}, u32[]{:S(2)}) collective-permute-start(bf16[8,2,128,128]{3,2,1,0:T(8,128)(2,1)S(1)} %get-tuple-element.21), channel_id=1, source_target_pairs={{16,0},{32,16},{48,32},{17,1},{33,17},{49,33},{18,2},{34,18},{50,3... | collective-permute-start | bytes 1572872 | tf_op jit(solution)/shard_map/ppermute | solution.py:474
  46.4 24.7 %collective-permute-start = (bf16[8,2,128,128]{3,2,1,0:T(8,128)(2,1)S(1)}, bf16[8,2,128,128]{3,2,1,0:T(8,128)(2,1)S(1)}, u32[]{:S(2)}, u32[]{:S(2)}) collective-permute-start(bf16[8,2,128,128]{3,2,1,0:T(8,128)(2,1)S(1)} %get-tuple-element.22), channel_id=1, source_target_pairs={{0,16},{16,32},{32,48},{1,17},{17,33},{33,49},{2,18},{18,34},{34,5... | collective-permute-start | bytes 1572872 | tf_op jit(solution)/shard_map/ppermute | solution.py:473
  71.1 1.0 copy-start.4
  71.1 1.0 copy-start.2
  71.1 1.0 copy-start.3
  84.1 20.2 %copy-start.1 = (bf16[16,2,128,128]{3,2,1,0:T(8,128)(2,1)S(1)}, bf16[16,2,128,128]{3,2,1,0:T(8,128)(2,1)}, u32[]{:S(2)}) copy-start(bf16[16,2,128,128]{3,2,1,0:T(8,128)(2,1)} %copy-done) | copy-start | bytes 3145732
  84.1 26.1 %all-to-all-start.2 = ((bf16[16,144,128]{2,1,0:T(8,128)(2,1)}), bf16[16,144,128]{2,1,0:T(8,128)(2,1)S(1)}, u32[]{:S(2)}, u32[]{:S(2)}) async-start(bf16[16,144,128]{2,1,0:T(8,128)(2,1)} %bitcast.26), calls=%async_computation.2 | async-start | bytes 1179648 | tf_op jit(solution)/shard_map/all_to_all | solution.py:452
  88.7 15.6 %collective-permute-start.3 = (bf16[8,2,128,128]{3,2,1,0:T(8,128)(2,1)}, bf16[8,2,128,128]{3,2,1,0:T(8,128)(2,1)S(1)}, u32[]{:S(2)}, u32[]{:S(2)}) collective-permute-start(bf16[8,2,128,128]{3,2,1,0:T(8,128)(2,1)} %get-tuple-element.17), channel_id=1, source_target_pairs={{0,16},{16,32},{32,48},{1,17},{17,33},{33,49},{2,18},{18,34},{34,5... | collective-permute-start | bytes 1572872 | tf_op jit(solution)/shard_map/ppermute | solution.py:478
  92.1 15.3 %collective-permute-start.2 = (bf16[8,2,128,128]{3,2,1,0:T(8,128)(2,1)}, bf16[8,2,128,128]{3,2,1,0:T(8,128)(2,1)S(1)}, u32[]{:S(2)}, u32[]{:S(2)}) collective-permute-start(bf16[8,2,128,128]{3,2,1,0:T(8,128)(2,1)} %get-tuple-element.16), channel_id=1, source_target_pairs={{16,0},{32,16},{48,32},{17,1},{33,17},{49,33},{18,2},{34,18},{50,3... | collective-permute-start | bytes 1572872 | tf_op jit(solution)/shard_map/ppermute | solution.py:479
  110.2 33.3 %all-to-all-start.3 = ((bf16[16,2,128,128]{3,2,1,0:T(8,128)(2,1)}), bf16[16,2,128,128]{3,2,1,0:T(8,128)(2,1)S(1)}, u32[]{:S(2)}, u32[]{:S(2)}) async-start(bf16[16,2,128,128]{3,2,1,0:T(8,128)(2,1)} %bitcast.24), calls=%async_computation.3 | async-start | bytes 2097152 | tf_op jit(solution)/shard_map/all_to_all | solution.py:452
  118.9 4.5 %collective-permute-start.6 = (f32[8,128]{1,0:T(8,128)S(1)}, f32[8,128]{1,0:T(8,128)S(1)}, u32[]{:S(2)}, u32[]{:S(2)}) collective-permute-start(f32[8,128]{1,0:T(8,128)S(1)} %get-tuple-element.20), channel_id=1, source_target_pairs={{0,192},{64,128},{128,64},{192,0},{1,193},{65,129},{129,65},{193,1... | collective-permute-start | bytes 12296 | tf_op jit(solution)/shard_map/ppermute | solution.py:459
  119.3 5.4 %collective-permute-start.5 = (f32[8,128]{1,0:T(8,128)S(1)}, f32[8,128]{1,0:T(8,128)S(1)}, u32[]{:S(2)}, u32[]{:S(2)}) collective-permute-start(f32[8,128]{1,0:T(8,128)S(1)} %get-tuple-element.20), channel_id=1, source_target_pairs={{0,128},{64,192},{128,0},{192,64},{1,129},{65,193},{129,1},{193,65... | collective-permute-start | bytes 12296 | tf_op jit(solution)/shard_map/ppermute | solution.py:459
  121.8 2.9 %collective-permute-start.4 = (f32[8,128]{1,0:T(8,128)S(1)}, f32[8,128]{1,0:T(8,128)S(1)}, u32[]{:S(2)}, u32[]{:S(2)}) collective-permute-start(f32[8,128]{1,0:T(8,128)S(1)} %get-tuple-element.20), channel_id=1, source_target_pairs={{0,64},{64,0},{128,192},{192,128},{1,65},{65,1},{129,193},{193,129... | collective-permute-start | bytes 12296 | tf_op jit(solution)/shard_map/ppermute | solution.py:459
  124.7 4.2 %collective-permute-start.9 = (f32[8,128]{1,0:T(8,128)S(1)}, f32[8,128]{1,0:T(8,128)S(1)}, u32[]{:S(2)}, u32[]{:S(2)}) collective-permute-start(f32[8,128]{1,0:T(8,128)S(1)} %add_add_fusion.1), channel_id=1, source_target_pairs={{0,48},{16,32},{32,16},{48,0},{1,49},{17,33},{33,17},{49,1},{2,50}... | collective-permute-start | bytes 12296 | tf_op jit(solution)/shard_map/ppermute | solution.py:459
  126.3 5.1 %collective-permute-start.8 = (f32[8,128]{1,0:T(8,128)S(1)}, f32[8,128]{1,0:T(8,128)S(1)}, u32[]{:S(2)}, u32[]{:S(2)}) collective-permute-start(f32[8,128]{1,0:T(8,128)S(1)} %add_add_fusion.1), channel_id=1, source_target_pairs={{0,32},{16,48},{32,0},{48,16},{1,33},{17,49},{33,1},{49,17},{2,34}... | collective-permute-start | bytes 12296 | tf_op jit(solution)/shard_map/ppermute | solution.py:459
  127.4 4.0 %collective-permute-start.7 = (f32[8,128]{1,0:T(8,128)S(1)}, f32[8,128]{1,0:T(8,128)S(1)}, u32[]{:S(2)}, u32[]{:S(2)}) collective-permute-start(f32[8,128]{1,0:T(8,128)S(1)} %add_add_fusion.1), channel_id=1, source_target_pairs={{0,16},{16,0},{32,48},{48,32},{1,17},{17,1},{33,49},{49,33},{2,18}... | collective-permute-start | bytes 12296 | tf_op jit(solution)/shard_map/ppermute | solution.py:459

commit v4 on v3

--- a/solution.py
+++ b/solution.py
@@ -24,7 +24,7 @@
 BF16 = jnp.bfloat16
 LIMIT = 60 * 1024 * 1024
 SMALL = 8 * 1024 * 1024
-FINISH_LIMIT = 52 * 1024 * 1024
+ATTENTION_LIMIT = 36 * 1024 * 1024
 
 
 def nt(left, right):
@@ -81,6 +81,15 @@
     return jnp.concatenate(rows, axis=0).astype(F32)
 
 
+def key_sums(chance, score, queries, cotangents, w, width):
+    first, last = max(w - 1, 0), min(w + 1, WIDE - 1)
+    lanes = slice((first - w + 1) * width, (last - w + 2) * width)
+    rows = slice(first * width, (last + 1) * width)
+    value_grad = nn(chance[w, :, lanes], cotangents[rows])
+    key_grad = nn(score[w, :, lanes], queries[rows]) * SCALE
+    return key_grad, value_grad
+
+
 def attention_kernel(
     flags_ref,
     kv_hbm,
@@ -90,15 +99,17 @@
     q_gain_ref,
     k_gain_ref,
     dq_hbm,
-    own_hbm,
     to_low_hbm,
     to_high_hbm,
+    qn_hbm,
+    dd_hbm,
+    chance_hbm,
+    score_hbm,
     kv_ref,
     low_ref,
     high_ref,
     qd_ref,
     dq_ref,
-    own_ref,
     to_low,
     to_high,
     in_sems,
@@ -112,17 +123,18 @@
     kn_h,
     knt_h,
     vv_h,
+    q_side,
+    d_side,
     qn,
     dd,
-    q_side,
-    d_side,
     chance_own,
+    score_own,
     chance_l,
     chance_h,
-    score_own,
     score_l,
     score_h,
     gains_ref,
+    q_inverse,
 ):
     arrivals = []
     for col in range(COLS):
@@ -165,10 +177,12 @@
         for frame in range(2):
             for row in range(2):
                 raw = qd_ref[frame, row, col, 0].astype(F32)
-                normed = (raw * inverse_rms(raw) * q_gain).astype(BF16)
+                inverse = jnp.broadcast_to(inverse_rms(raw), raw.shape)
+                normed = (raw * inverse * q_gain).astype(BF16)
                 for part in range(2):
                     place = slice(part * TILE, (part + 1) * TILE)
                     at = ((2 * col + part) * 2 + frame) * PAIR + row * TILE
+                    q_inverse[at : at + TILE] = inverse[place]
                     qn[at : at + TILE] = normed[place]
                     dd[at : at + TILE] = qd_ref[frame, row, col, 1, place]
                     at = (2 * col + part) * PAIR + row * TILE
@@ -200,12 +214,11 @@
 
     def second_half(w, before, count, q_tile, d_tile, weights, weight_grads, sums):
         reciprocal = 1.0 / spread(sums)
-        chances, dots = [], []
+        dots = []
         for number, (_, _, _, store, _, frames, first, width, _) in enumerate(sources):
             chance = weights[number] * reciprocal[:, first : first + width]
             rounded = chance.astype(BF16)
             dots.append(jnp.sum(rounded.astype(F32) * weight_grads[number], axis=0, keepdims=True))
-            chances.append(chance)
             for step in range(count):
                 place = (1 - (step - before)) * width
                 store[w - before + step, :, place : place + width] = rounded[
@@ -214,7 +227,8 @@
         row_dot = spread(dots)
         grads = []
         for number, (_, knt, _, _, store, frames, first, width, _) in enumerate(sources):
-            score = chances[number] * (weight_grads[number] - row_dot[:, first : first + width])
+            chance = weights[number] * reciprocal[:, first : first + width]
+            score = chance * (weight_grads[number] - row_dot[:, first : first + width])
             score = score.astype(BF16)
             for step in range(count):
                 place = (1 - (step - before)) * width
@@ -229,63 +243,47 @@
         for frame in range(2):
             for row in range(2):
                 raw = qd_ref[frame, row, col, 0, place].astype(F32)
-                inverse = inverse_rms(raw)
+                at = (2 * w + frame) * PAIR + row * TILE
+                inverse = q_inverse[at : at + TILE]
                 part = grad[frame * PAIR + row * TILE : frame * PAIR + (row + 1) * TILE]
-                gains_ref[...] += jnp.sum((part * raw * inverse).reshape(-1, 8, HD), axis=0)
+                gains_ref[0:8] += jnp.sum((part * raw * inverse).reshape(-1, 8, HD), axis=0)
+                gains_ref[8:16] += jnp.sum((part * qn[at : at + TILE].astype(F32)).reshape(-1, 8, HD), axis=0)
                 dq_ref[frame, row, col, place] = norm_back(raw, inverse, q_gain, part).astype(BF16)
         if w % 2:
             send(dq_ref.at[:, :, col, :PAIR], dq_hbm.at[:, :, col, :PAIR])
 
-    def key_sums(chance, score, queries, cotangents, w, width):
-        first, last = max(w - 1, 0), min(w + 1, WIDE - 1)
-        lanes = slice((first - w + 1) * width, (last - w + 2) * width)
-        rows = slice(first * width, (last + 1) * width)
-        value_grad = nn(chance[w, :, lanes], cotangents[rows])
-        key_grad = nn(score[w, :, lanes], queries[rows]) * SCALE
-        return key_grad, value_grad
-
-    def gain_part(key_grad, raw):
-        return jnp.sum((key_grad * raw * inverse_rms(raw)).reshape(-1, 8, HD), axis=0)
-
-    sides = (
-        (chance_l, score_l, low_ref, to_low, to_low_hbm),
-        (chance_h, score_h, high_ref, to_high, to_high_hbm),
-    )
-
-    def key_column(w, gain_sum):
-        for frame, (chance, score, raw_ref, out_ref, out_hbm) in enumerate(sides):
+    sides = ((chance_l, score_l, to_low, to_low_hbm), (chance_h, score_h, to_high, to_high_hbm))
+
+    def key_column(w):
+        for frame, (chance, score, out_ref, out_hbm) in enumerate(sides):
             key_grad, value_grad = key_sums(chance, score, q_side.at[frame], d_side.at[frame], w, PAIR)
             out_ref[w, 0] = key_grad.astype(BF16)
             out_ref[w, 1] = value_grad.astype(BF16)
             send(out_ref.at[w], out_hbm.at[w])
-            gain_sum += gain_part(key_grad, raw_column(raw_ref, w, 0, w // 2))
-        key_grad, value_grad = key_sums(chance_own, score_own, qn, dd, w, 2 * PAIR)
-        own_ref[w, 0] = key_grad.astype(BF16)
-        own_ref[w, 1] = value_grad.astype(BF16)
-        for frame in range(2):
-            gain_sum += gain_part(key_grad[frame * PAIR : (frame + 1) * PAIR], raw_column(kv_ref, w, frame, w // 2))
-        send(own_ref.at[w], own_hbm.at[w])
-        return gain_sum
+        send(chance_own.at[w], chance_hbm.at[w])
+        send(score_own.at[w], score_hbm.at[w])
 
     def extent(w):
         return w, min(w, 1), 2 if w in (0, WIDE - 1) else 3
 
-    gain_sum = jnp.zeros((8, HD), F32)
     prepare(0)
     held = first_half(*extent(0))
     for w in range(WIDE):
         if w % 2 == 0 and w // 2 + 1 < COLS:
             prepare(w // 2 + 1)
+            if w // 2 + 2 == COLS:
+                send(qn, qn_hbm)
+                send(dd, dd_hbm)
         following = first_half(*extent(w + 1)) if w + 1 < WIDE else None
         second_half(*extent(w), *held)
         held = following
         if w > 0:
-            gain_sum = key_column(w - 1, gain_sum)
-    gain_sum = key_column(WIDE - 1, gain_sum)
-
-
-    q_sum = jnp.sum(gains_ref[...], axis=0, keepdims=True)
-    k_sum = jnp.sum(gain_sum, axis=0, keepdims=True)
+            key_column(w - 1)
+    key_column(WIDE - 1)
+
+
+    q_sum = jnp.sum(gains_ref[0:8], axis=0, keepdims=True)
+    k_sum = jnp.sum(gains_ref[8:16], axis=0, keepdims=True) / k_gain
     lines = []
     for line in (q_sum, k_sum):
         line = jnp.where(flags_ref[2] > 0, line, 0.0)
@@ -308,77 +306,106 @@
 def attention(flags, kv, low, high, qd, q_gain, k_gain):
     own, halo = WIDE * 2 * PAIR, WIDE * PAIR
     arrays = [grid_of(array) for array in (kv, low, high, qd)]
-    outs = [((2, 2, COLS, PAIR + EXTRA, HD), BF16), ((WIDE, 2, 2 * PAIR, HD), BF16)]
-    outs += [((WIDE, 2, PAIR, HD), BF16)] * 2
+    side = ((WIDE, 2, PAIR, HD), BF16)
+    columns = ((WIDE, 2 * PAIR, 6 * PAIR), BF16)
+    queries = ((own, HD), BF16)
+    outs = [((2, 2, COLS, PAIR + EXTRA, HD), BF16), side, side, queries, queries, columns, columns]
     scratch = [pltpu.VMEM(array.shape, BF16) for array in arrays]
-    scratch += [pltpu.VMEM(*out) for out in outs]
+    scratch += [pltpu.VMEM(*out) for out in outs[:3]]
     scratch += [pltpu.SemaphoreType.DMA((COLS,)), pltpu.SemaphoreType.DMA]
     for rows in (own, halo, halo):
         scratch += [pltpu.VMEM((rows, HD), BF16), pltpu.VMEM((HD, rows), BF16), pltpu.VMEM((rows, HD), BF16)]
-    scratch += [pltpu.VMEM((own, HD), BF16)] * 2 + [pltpu.VMEM((2, halo, HD), BF16)] * 2
-    stores = [pltpu.VMEM((WIDE, 2 * PAIR, 6 * PAIR), BF16)] + [pltpu.VMEM((WIDE, PAIR, 3 * PAIR), BF16)] * 2
-    scratch += stores + stores + [pltpu.VMEM((8, HD), F32)]
-    dq, own, to_low, to_high = pl.pallas_call(
+    scratch += [pltpu.VMEM((2, halo, HD), BF16)] * 2 + [pltpu.VMEM(*out) for out in outs[3:]]
+    scratch += [pltpu.VMEM((WIDE, PAIR, 3 * PAIR), BF16)] * 4 + [pltpu.VMEM((16, HD), F32)]
+    scratch += [pltpu.VMEM((own, HD), F32)]
+    dq, *others = pl.pallas_call(
         attention_kernel,
         in_specs=[pl.BlockSpec(memory_space=pltpu.SMEM)]
         + [pl.BlockSpec(memory_space=pl.ANY)] * 4
         + [pl.BlockSpec(memory_space=pltpu.VMEM)] * 2,
-        out_specs=[pl.BlockSpec(memory_space=pl.ANY)] * 4,
+        out_specs=[pl.BlockSpec(memory_space=pl.ANY)] * len(outs),
         out_shape=[pltpu.HBM(*out) for out in outs],
         scratch_shapes=scratch,
         name="attention",
         cost_estimate=pl.CostEstimate(
             flops=5 * 66 * PAIR * PAIR * PAIR * 2, bytes_accessed=8 << 20, transcendentals=0
         ),
-        compiler_params=pltpu.CompilerParams(vmem_limit_bytes=FINISH_LIMIT),
+        compiler_params=pltpu.CompilerParams(vmem_limit_bytes=ATTENTION_LIMIT),
     )(flags, *arrays, q_gain, k_gain)
-    return dq.reshape(GROUP, PAIR + EXTRA, HD), own, to_low, to_high
-
-
-def finish_kernel(frame, kv_hbm, own_hbm, halo_hbm, k_gain_ref, out_hbm, kv_ref, own_ref, halo_ref, out_ref, in_sems, out_sem):
-    rows = slice(frame * PAIR, (frame + 1) * PAIR)
+    return dq.reshape(GROUP, PAIR + EXTRA, HD), *others
+
+
+def own_kernel(qn_hbm, dd_hbm, chance_hbm, score_hbm, own_hbm, qn, dd, chance, score, own_ref, sems, out_sem):
     arrivals = []
-    for col in range(COLS):
-        columns = slice(2 * col, 2 * col + 2)
-        pairs = (
-            (halo_hbm.at[columns], halo_ref.at[columns]),
-            (kv_hbm.at[frame, :, col], kv_ref.at[0, :, col]),
-            (own_hbm.at[columns, :, rows], own_ref.at[columns]),
-        )
-        copies = [pltpu.make_async_copy(source, target, in_sems.at[col]) for source, target in pairs]
+    for w in range(WIDE):
+        pairs = [(chance_hbm.at[w], chance.at[w]), (score_hbm.at[w], score.at[w])]
+        if w == 0:
+            pairs = [(qn_hbm, qn), (dd_hbm, dd)] + pairs
+        copies = [pltpu.make_async_copy(source, target, sems.at[w]) for source, target in pairs]
         for copy in copies:
             copy.start()
         arrivals.append(copies)
+    departures = []
+    for w in range(WIDE):
+        for copy in arrivals[w]:
+            copy.wait()
+        key_grad, value_grad = key_sums(chance, score, qn, dd, w, 2 * PAIR)
+        own_ref[w, 0] = key_grad.astype(BF16)
+        own_ref[w, 1] = value_grad.astype(BF16)
+        copy = pltpu.make_async_copy(own_ref.at[w], own_hbm.at[w], out_sem)
+        copy.start()
+        departures.append(copy)
+    for copy in departures:
+        copy.wait()
+
+
+def own_sums(*arguments):
+    out = ((WIDE, 2, 2 * PAIR, HD), BF16)
+    return pl.pallas_call(
+        own_kernel,
+        in_specs=[pl.BlockSpec(memory_space=pl.ANY)] * 4,
+        out_specs=pl.BlockSpec(memory_space=pl.ANY),
+        out_shape=pltpu.HBM(*out),
+        scratch_shapes=[pltpu.VMEM(array.shape, array.dtype) for array in arguments]
+        + [pltpu.VMEM(*out), pltpu.SemaphoreType.DMA((WIDE,)), pltpu.SemaphoreType.DMA],
+        name="own_sums",
+        cost_estimate=pl.CostEstimate(
+            flops=2 * 44 * PAIR * PAIR * PAIR * 2, bytes_accessed=8 << 20, transcendentals=0
+        ),
+        compiler_params=pltpu.CompilerParams(vmem_limit_bytes=LIMIT),
+    )(*arguments)
+
+
+def finish_kernel(frame, kv_ref, own_ref, halo_ref, k_gain_ref, out_hbm, out_ref, sem):
+    rows = slice(frame * PAIR, (frame + 1) * PAIR)
     k_gain = k_gain_ref[...]
     departures = []
     for col in range(COLS):
-        for copy in arrivals[col]:
-            copy.wait()
         for part in range(2):
             w = 2 * col + part
             place = slice(part * TILE, (part + 1) * TILE)
-            raw = raw_column(kv_ref, w, 0, col)
-            key_grad = own_ref[w, 0].astype(F32) + halo_ref[w, 0].astype(F32)
-            value_grad = (own_ref[w, 1].astype(F32) + halo_ref[w, 1].astype(F32)).astype(BF16)
+            raw = raw_column(kv_ref, w, frame, col)
+            key_grad = own_ref[w, 0, rows].astype(F32) + halo_ref[w, 0].astype(F32)
+            value_grad = (own_ref[w, 1, rows].astype(F32) + halo_ref[w, 1].astype(F32)).astype(BF16)
             key_grad = norm_back(raw, inverse_rms(raw), k_gain, key_grad).astype(BF16)
             for row in range(2):
                 out_ref[row, col, 0, place] = key_grad[row * TILE : (row + 1) * TILE]
                 out_ref[row, col, 1, place] = value_grad[row * TILE : (row + 1) * TILE]
-        copy = pltpu.make_async_copy(out_ref.at[:, col], out_hbm.at[frame, :, col], out_sem)
+        copy = pltpu.make_async_copy(out_ref.at[:, col], out_hbm.at[frame, :, col], sem)
         copy.start()
         departures.append(copy)
     for copy in departures:
         copy.wait()
 
 
-def second_finish_kernel(kv_hbm, own_hbm, halo_hbm, k_gain_ref, first_hbm, *refs):
-    finish_kernel(1, kv_hbm, own_hbm, halo_hbm, k_gain_ref, *refs)
+def second_finish_kernel(kv_ref, own_ref, halo_ref, k_gain_ref, first_hbm, out_hbm, out_ref, sem):
+    finish_kernel(1, kv_ref, own_ref, halo_ref, k_gain_ref, out_hbm, out_ref, sem)
 
 
 def finish(frame, kv, own, halo, k_gain, first=None):
     half = (2, COLS, 2, PAIR, HD)
     arguments = [grid_of(kv), own, halo, k_gain]
-    in_specs = [pl.BlockSpec(memory_space=pl.ANY)] * 3 + [pl.BlockSpec(memory_space=pltpu.VMEM)]
+    in_specs = [pl.BlockSpec(memory_space=pltpu.VMEM)] * 4
     aliases = {}
     if frame:
         arguments.append(first)
@@ -389,17 +416,10 @@
         in_specs=in_specs,
         out_specs=pl.BlockSpec(memory_space=pl.ANY),
         out_shape=pltpu.HBM((2,) + half, BF16),
-        scratch_shapes=[
-            pltpu.VMEM((1,) + half, BF16),
-            pltpu.VMEM((WIDE, 2, PAIR, HD), BF16),
-            pltpu.VMEM((WIDE, 2, PAIR, HD), BF16),
-            pltpu.VMEM(half, BF16),
-            pltpu.SemaphoreType.DMA((COLS,)),
-            pltpu.SemaphoreType.DMA,
-        ],
+        scratch_shapes=[pltpu.VMEM(half, BF16), pltpu.SemaphoreType.DMA],
         input_output_aliases=aliases,
         name="finish_high" if frame else "finish_low",
-        compiler_params=pltpu.CompilerParams(vmem_limit_bytes=FINISH_LIMIT),
+        compiler_params=pltpu.CompilerParams(vmem_limit_bytes=SMALL),
     )(*arguments)
 
 
@@ -473,10 +493,11 @@
     low = lax.ppermute(kv[HALF:], "x", up)
     high = lax.ppermute(kv[:HALF], "x", down)
     qd = swap(pack(q_raw, d_out))
-    dq, own, to_low, to_high = attention(flags, kv, low, high, qd, q_line, k_line)
+    dq, to_low, to_high, *stored = attention(flags, kv, low, high, qd, q_line, k_line)
     arrived = swap(dq)
     from_low = lax.ppermute(to_high, "x", up)
     from_high = lax.ppermute(to_low, "x", down)
+    own = own_sums(*stored)
     q_grad, lines = unpack_query(arrived)
     grads = finish(0, kv, own, from_low, k_line)
     grads = finish(1, kv, own, from_high, k_line, grads).reshape(GROUP, 2, PAIR, HD)

time: 145 us -> 142 us (0.979)
  waiting for transfers between devices: 72.7 us -> 67.3 us
    pallas_call x0 -> x1, Pallas kernels: none -> 4.9 us  [own_sums(): pl.pallas_call(own_kernel, in_specs=[pl.BlockSpec(memory_space=pl.ANY)] *...]
    ppermute x1, waiting for transfers between devices: 9.55 us -> 4.66 us  [on_device(): from_low = lax.ppermute(to_high, 'x', up)]
    pallas_call x2, Pallas kernels: 5.57 us -> 2.13 us  [finish(): pl.pallas_call(second_finish_kernel if frame else functools.partial(finis...]
  transfers between devices with their start and end apart: 14 -> 14, of which waited for: 8 -> 8; matrix products, arithmetic and copies ran while one was open for 0% -> 1% of each run, Pallas kernels for 6% -> 7%
where the time goes in v4:
time: 142 us; the launch traced here: 141 us
  waiting for transfers between devices  67.3 us (47%)
  starting transfers between devices  45.7 us (32%)
  Pallas kernels  24.1 us (17%)
  local copies, waits for them, and re-layouts  2.84 us (2%)
    all_to_all x4, waiting for transfers between devices, swap(): return lax.all_to_all(array, 'g', 0, 0)  57.1 us
    all_to_all x4, starting transfers between devices, swap(): return lax.all_to_all(array, 'g', 0, 0)  26.3 us
    pallas_call x1, Pallas kernels, attention(): pl.pallas_call(attention_kernel, in_specs=[pl.BlockSpec(memory_space=pltp...  11.2 us
    ppermute x6, starting transfers between devices, sum_over(): lax.ppermute(lines, axis, [(source, source ^ step) for source in range(co...  7.55 us
    pallas_call x1, Pallas kernels, own_sums(): pl.pallas_call(own_kernel, in_specs=[pl.BlockSpec(memory_space=pl.ANY)] *...  4.9 us
    ppermute x1, waiting for transfers between devices, on_device(): from_low = lax.ppermute(to_high, 'x', up)  4.66 us
    ppermute x6, waiting for transfers between devices, sum_over(): lax.ppermute(lines, axis, [(source, source ^ step) for source in range(co...  4.65 us
    pallas_call x2, Pallas kernels, pack(): pl.pallas_call(pack_kernel, in_specs=[pl.BlockSpec(memory_space=pl.ANY)]...  4.19 us
  transfers between devices with their start and end apart: 14, of which 8 were waited for; matrix products, arithmetic and copies ran while one was open for 1% of the time, Pallas kernels for 7%

profile of v4, /device:TPU:2, one launch (start us, length us, event | category | flops | bytes accessed | tf_op | source)
XLA Modules:
  0.0 141.0 jit_solution(14531257015307955268)
XLA Ops:
  0.6 2.1 %pack.2 = bf16[16,2,128,128]{3,2,1,0:T(8,128)(2,1)} custom-call(bf16[1,128,1536]{2,1,0:T(8,128)(2,1)} %first_ref.2, bf16[1,128,1536]{2,1,0:T(8,128)(2,1)} %second_ref.2), custom_call_target="tpu_custom_call" | custom-call | tf_op jit(solution)/shard_map/pack/pallas_call | solution.py:63
  2.7 9.6 %all-to-all-start = ((bf16[16,2,128,128]{3,2,1,0:T(8,128)(2,1)}), bf16[16,2,128,128]{3,2,1,0:T(8,128)(2,1)S(1)}, u32[]{:S(2)}, u32[]{:S(2)}) async-start(bf16[16,2,128,128]{3,2,1,0:T(8,128)(2,1)} %pack.2), calls=%async_computation | async-start | bytes 2097152 | tf_op jit(solution)/shard_map/all_to_all | solution.py:472
  12.3 0.0 copy-start.1
  12.3 0.0 copy-start.2
  12.3 2.1 %pack.3 = bf16[16,2,128,128]{3,2,1,0:T(8,128)(2,1)} custom-call(bf16[1,128,1536]{2,1,0:T(8,128)(2,1)} %first_ref.3, bf16[1,128,1536]{2,1,0:T(8,128)(2,1)} %second_ref.3), custom_call_target="tpu_custom_call" | custom-call | tf_op jit(solution)/shard_map/pack/pallas_call | solution.py:63
  14.5 24.9 %all-to-all-done = bf16[16,2,128,128]{3,2,1,0:T(8,128)(2,1)S(1)} async-done(((bf16[16,2,128,128]{3,2,1,0:T(8,128)(2,1)}), bf16[16,2,128,128]{3,2,1,0:T(8,128)(2,1)S(1)}, u32[]{:S(2)}, u32[]{:S(2)}) %all-to-all-start) | async-done | bytes 1048608 | tf_op jit(solution)/shard_map/all_to_all | solution.py:472
  39.4 4.4 %all-to-all-start.1 = ((bf16[16,2,128,128]{3,2,1,0:T(8,128)(2,1)}), bf16[16,2,128,128]{3,2,1,0:T(8,128)(2,1)S(1)}, u32[]{:S(2)}, u32[]{:S(2)}) async-start(bf16[16,2,128,128]{3,2,1,0:T(8,128)(2,1)} %pack.3), calls=%async_computation.1 | async-start | bytes 2097152 | tf_op jit(solution)/shard_map/all_to_all | solution.py:472
  43.8 1.1 fusion
  44.9 2.4 %collective-permute-start.1 = (bf16[8,2,128,128]{3,2,1,0:T(8,128)(2,1)}, bf16[8,2,128,128]{3,2,1,0:T(8,128)(2,1)S(1)}, u32[]{:S(2)}, u32[]{:S(2)}) collective-permute-start(bf16[8,2,128,128]{3,2,1,0:T(8,128)(2,1)} %get-tuple-element.27), channel_id=1, source_target_pairs={{16,0},{32,16},{48,32},{17,1},{33,17},{49,33},{18,2},{34,18},{50,3... | collective-permute-start | bytes 1572872 | tf_op jit(solution)/shard_map/ppermute | solution.py:494
  47.3 3.4 %collective-permute-start = (bf16[8,2,128,128]{3,2,1,0:T(8,128)(2,1)}, bf16[8,2,128,128]{3,2,1,0:T(8,128)(2,1)S(1)}, u32[]{:S(2)}, u32[]{:S(2)}) collective-permute-start(bf16[8,2,128,128]{3,2,1,0:T(8,128)(2,1)} %get-tuple-element.28), channel_id=1, source_target_pairs={{0,16},{16,32},{32,48},{1,17},{17,33},{33,49},{2,18},{18,34},{34,5... | collective-permute-start | bytes 1572872 | tf_op jit(solution)/shard_map/ppermute | solution.py:493
  50.7 0.1 add_convert_fusion.flags_ref
  50.8 20.3 %all-to-all-done.1 = bf16[16,2,128,128]{3,2,1,0:T(8,128)(2,1)S(1)} async-done(((bf16[16,2,128,128]{3,2,1,0:T(8,128)(2,1)}), bf16[16,2,128,128]{3,2,1,0:T(8,128)(2,1)S(1)}, u32[]{:S(2)}, u32[]{:S(2)}) %all-to-all-start.1) | async-done | bytes 1048608 | tf_op jit(solution)/shard_map/all_to_all | solution.py:472
  71.1 0.0 collective-permute-done.1
  71.1 0.0 collective-permute-done
  71.1 0.0 copy-done.1
  71.1 0.0 copy-done.2
  71.1 11.2 %attention.1 = (bf16[2,2,4,144,128]{4,3,2,1,0:T(8,128)(2,1)}, bf16[8,2,128,128]{3,2,1,0:T(8,128)(2,1)}, bf16[8,2,128,128]{3,2,1,0:T(8,128)(2,1)}, bf16[2048,128]...) custom-call(s32[3]{0:T(128)S(1)} %add_convert_fusion.flags_ref, ...), custom_call_target="tpu_custom_call" | custom-call | flops 1384120320 | bytes 8388608 | tf_op jit(solution)/shard_map/attention/pallas_call | solution.py:321
  82.3 4.4 %all-to-all-start.2 = ((bf16[16,144,128]{2,1,0:T(8,128)(2,1)}), bf16[16,144,128]{2,1,0:T(8,128)(2,1)S(1)}, u32[]{:S(2)}, u32[]{:S(2)}) async-start(bf16[16,144,128]{2,1,0:T(8,128)(2,1)} %bitcast.26), calls=%async_computation.2 | async-start | bytes 1179648 | tf_op jit(solution)/shard_map/all_to_all | solution.py:472
  86.8 3.4 %collective-permute-start.3 = (bf16[8,2,128,128]{3,2,1,0:T(8,128)(2,1)}, bf16[8,2,128,128]{3,2,1,0:T(8,128)(2,1)S(1)}, u32[]{:S(2)}, u32[]{:S(2)}) collective-permute-start(bf16[8,2,128,128]{3,2,1,0:T(8,128)(2,1)} %get-tuple-element.23), channel_id=1, source_target_pairs={{0,16},{16,32},{32,48},{1,17},{17,33},{33,49},{2,18},{18,34},{34,5... | collective-permute-start | bytes 1572872 | tf_op jit(solution)/shard_map/ppermute | solution.py:498
  90.2 2.6 %collective-permute-start.2 = (bf16[8,2,128,128]{3,2,1,0:T(8,128)(2,1)}, bf16[8,2,128,128]{3,2,1,0:T(8,128)(2,1)S(1)}, u32[]{:S(2)}, u32[]{:S(2)}) collective-permute-start(bf16[8,2,128,128]{3,2,1,0:T(8,128)(2,1)} %get-tuple-element.22), channel_id=1, source_target_pairs={{16,0},{32,16},{48,32},{17,1},{33,17},{49,33},{18,2},{34,18},{50,3... | collective-permute-start | bytes 1572872 | tf_op jit(solution)/shard_map/ppermute | solution.py:499
  92.8 4.9 %own_sums.1.own_ref = bf16[8,2,256,128]{3,2,1,0:T(8,128)(2,1)} custom-call(bf16[2048,128]{1,0:T(8,128)(2,1)} %get-tuple-element.18.qn_hbm, bf16[2048,128]{1,0:T(8,128)(2,1)} %get-tuple-element.19.dd_hbm, bf16[8,256,768]{2,1,0:T(8,128)(2,1)} %get-tuple-element.20.chance_hbm, bf16[8,256,768]{2,1,0:T(8,128)(2,1)} %get-tuple-element.21.score_hbm), custom_call_target="tpu_custom_call" | custom-call | flops 369098752 | bytes 8388608 | tf_op jit(solution)/shard_map/own_sums/pallas_call | solution.py:364
  97.7 4.7 %collective-permute-done.3.halo_ref = bf16[8,2,128,128]{3,2,1,0:T(8,128)(2,1)S(1)} collective-permute-done((bf16[8,2,128,128]{3,2,1,0:T(8,128)(2,1)}, bf16[8,2,128,128]{3,2,1,0:T(8,128)(2,1)S(1)}, u32[]{:S(2)}, u32[]{:S(2)}) %collective-permute-start.3) | collective-permute-done | bytes 524320 | tf_op jit(solution)/shard_map/ppermute | solution.py:498
  102.4 0.0 copy-start
  102.4 1.2 copy-done
  103.6 1.1 finish_low.1.first_hbm
  104.7 0.8 collective-permute-done.2.halo_ref
  105.5 1.1 finish_high.1
  106.6 0.0 all-to-all-done.2.in_ref
  106.6 7.8 %all-to-all-start.3 = ((bf16[16,2,128,128]{3,2,1,0:T(8,128)(2,1)}), bf16[16,2,128,128]{3,2,1,0:T(8,128)(2,1)S(1)}, u32[]{:S(2)}, u32[]{:S(2)}) async-start(bf16[16,2,128,128]{3,2,1,0:T(8,128)(2,1)} %bitcast.25), calls=%async_computation.3 | async-start | bytes 2097152 | tf_op jit(solution)/shard_map/all_to_all | solution.py:472
  114.5 0.8 unpack_query.1
  115.3 0.4 collective-permute-start.6
  115.7 2.5 %collective-permute-start.5 = (f32[8,128]{1,0:T(8,128)S(1)}, f32[8,128]{1,0:T(8,128)S(1)}, u32[]{:S(2)}, u32[]{:S(2)}) collective-permute-start(f32[8,128]{1,0:T(8,128)S(1)} %get-tuple-element.26), channel_id=1, source_target_pairs={{0,128},{64,192},{128,0},{192,64},{1,129},{65,193},{129,1},{193,65... | collective-permute-start | bytes 12296 | tf_op jit(solution)/shard_map/ppermute | solution.py:479
  118.2 0.4 collective-permute-start.4
  118.6 1.2 collective-permute-done.6
  119.8 1.2 collective-permute-done.5
  121.1 0.0 collective-permute-done.4
  121.1 1.3 collective-permute-start.9
  122.4 1.4 %collective-permute-start.8 = (f32[8,128]{1,0:T(8,128)S(1)}, f32[8,128]{1,0:T(8,128)S(1)}, u32[]{:S(2)}, u32[]{:S(2)}) collective-permute-start(f32[8,128]{1,0:T(8,128)S(1)} %add_add_fusion.1), channel_id=1, source_target_pairs={{0,32},{16,48},{32,0},{48,16},{1,33},{17,49},{33,1},{49,17},{2,34}... | collective-permute-start | bytes 12296 | tf_op jit(solution)/shard_map/ppermute | solution.py:479
  123.8 1.4 %collective-permute-start.7 = (f32[8,128]{1,0:T(8,128)S(1)}, f32[8,128]{1,0:T(8,128)S(1)}, u32[]{:S(2)}, u32[]{:S(2)}) collective-permute-start(f32[8,128]{1,0:T(8,128)S(1)} %add_add_fusion.1), channel_id=1, source_target_pairs={{0,16},{16,0},{32,48},{48,32},{1,17},{17,1},{33,49},{49,33},{2,18}... | collective-permute-start | bytes 12296 | tf_op jit(solution)/shard_map/ppermute | solution.py:479
  125.3 0.0 collective-permute-done.9
  125.3 2.2 %collective-permute-done.8 = f32[8,128]{1,0:T(8,128)S(1)} collective-permute-done((f32[8,128]{1,0:T(8,128)S(1)}, f32[8,128]{1,0:T(8,128)S(1)}, u32[]{:S(2)}, u32[]{:S(2)}) %collective-permute-start.8) | collective-permute-done | bytes 4128 | tf_op jit(solution)/shard_map/ppermute | solution.py:479
  127.5 0.0 collective-permute-done.7
  127.5 0.5 slice_bitcast_fusion
  128.0 11.9 %all-to-all-done.3.in_ref = bf16[16,2,128,128]{3,2,1,0:T(8,128)(2,1)S(1)} async-done(((bf16[16,2,128,128]{3,2,1,0:T(8,128)(2,1)}), bf16[16,2,128,128]{3,2,1,0:T(8,128)(2,1)S(1)}, u32[]{:S(2)}, u32[]{:S(2)}) %all-to-all-start.3) | async-done | bytes 1048608 | tf_op jit(solution)/shard_map/all_to_all | solution.py:472
  140.0 0.9 unpack.1
  (2 shorter events, 0.0 us)
Async XLA Ops:
  2.7 36.7 %all-to-all-start = ((bf16[16,2,128,128]{3,2,1,0:T(8,128)(2,1)}), bf16[16,2,128,128]{3,2,1,0:T(8,128)(2,1)S(1)}, u32[]{:S(2)}, u32[]{:S(2)}) async-start(bf16[16,2,128,128]{3,2,1,0:T(8,128)(2,1)} %pack.2), calls=%async_computation | async-start | bytes 2097152 | tf_op jit(solution)/shard_map/all_to_all | solution.py:472
  12.3 58.8 %copy-start.1 = (f32[128]{0:T(128)S(1)}, f32[128]{0:T(128)}, u32[]{:S(2)}) copy-start(f32[128]{0:T(128)} %param.11) | copy-start | bytes 1540
  12.3 58.8 %copy-start.2 = (f32[128]{0:T(128)S(1)}, f32[128]{0:T(128)}, u32[]{:S(2)}) copy-start(f32[128]{0:T(128)} %param.10) | copy-start | bytes 1540
  39.4 31.7 %all-to-all-start.1 = ((bf16[16,2,128,128]{3,2,1,0:T(8,128)(2,1)}), bf16[16,2,128,128]{3,2,1,0:T(8,128)(2,1)S(1)}, u32[]{:S(2)}, u32[]{:S(2)}) async-start(bf16[16,2,128,128]{3,2,1,0:T(8,128)(2,1)} %pack.3), calls=%async_computation.1 | async-start | bytes 2097152 | tf_op jit(solution)/shard_map/all_to_all | solution.py:472
  44.9 26.2 %collective-permute-start.1 = (bf16[8,2,128,128]{3,2,1,0:T(8,128)(2,1)}, bf16[8,2,128,128]{3,2,1,0:T(8,128)(2,1)S(1)}, u32[]{:S(2)}, u32[]{:S(2)}) collective-permute-start(bf16[8,2,128,128]{3,2,1,0:T(8,128)(2,1)} %get-tuple-element.27), channel_id=1, source_target_pairs={{16,0},{32,16},{48,32},{17,1},{33,17},{49,33},{18,2},{34,18},{50,3... | collective-permute-start | bytes 1572872 | tf_op jit(solution)/shard_map/ppermute | solution.py:494
  47.3 23.8 %collective-permute-start = (bf16[8,2,128,128]{3,2,1,0:T(8,128)(2,1)}, bf16[8,2,128,128]{3,2,1,0:T(8,128)(2,1)S(1)}, u32[]{:S(2)}, u32[]{:S(2)}) collective-permute-start(bf16[8,2,128,128]{3,2,1,0:T(8,128)(2,1)} %get-tuple-element.28), channel_id=1, source_target_pairs={{0,16},{16,32},{32,48},{1,17},{17,33},{33,49},{2,18},{18,34},{34,5... | collective-permute-start | bytes 1572872 | tf_op jit(solution)/shard_map/ppermute | solution.py:493
  82.3 24.3 %all-to-all-start.2 = ((bf16[16,144,128]{2,1,0:T(8,128)(2,1)}), bf16[16,144,128]{2,1,0:T(8,128)(2,1)S(1)}, u32[]{:S(2)}, u32[]{:S(2)}) async-start(bf16[16,144,128]{2,1,0:T(8,128)(2,1)} %bitcast.26), calls=%async_computation.2 | async-start | bytes 1179648 | tf_op jit(solution)/shard_map/all_to_all | solution.py:472
  86.8 15.6 %collective-permute-start.3 = (bf16[8,2,128,128]{3,2,1,0:T(8,128)(2,1)}, bf16[8,2,128,128]{3,2,1,0:T(8,128)(2,1)S(1)}, u32[]{:S(2)}, u32[]{:S(2)}) collective-permute-start(bf16[8,2,128,128]{3,2,1,0:T(8,128)(2,1)} %get-tuple-element.23), channel_id=1, source_target_pairs={{0,16},{16,32},{32,48},{1,17},{17,33},{33,49},{2,18},{18,34},{34,5... | collective-permute-start | bytes 1572872 | tf_op jit(solution)/shard_map/ppermute | solution.py:498
  90.2 15.3 %collective-permute-start.2 = (bf16[8,2,128,128]{3,2,1,0:T(8,128)(2,1)}, bf16[8,2,128,128]{3,2,1,0:T(8,128)(2,1)S(1)}, u32[]{:S(2)}, u32[]{:S(2)}) collective-permute-start(bf16[8,2,128,128]{3,2,1,0:T(8,128)(2,1)} %get-tuple-element.22), channel_id=1, source_target_pairs={{16,0},{32,16},{48,32},{17,1},{33,17},{49,33},{18,2},{34,18},{50,3... | collective-permute-start | bytes 1572872 | tf_op jit(solution)/shard_map/ppermute | solution.py:499
  102.4 1.2 copy-start
  106.6 33.3 %all-to-all-start.3 = ((bf16[16,2,128,128]{3,2,1,0:T(8,128)(2,1)}), bf16[16,2,128,128]{3,2,1,0:T(8,128)(2,1)S(1)}, u32[]{:S(2)}, u32[]{:S(2)}) async-start(bf16[16,2,128,128]{3,2,1,0:T(8,128)(2,1)} %bitcast.25), calls=%async_computation.3 | async-start | bytes 2097152 | tf_op jit(solution)/shard_map/all_to_all | solution.py:472
  115.3 4.5 %collective-permute-start.6 = (f32[8,128]{1,0:T(8,128)S(1)}, f32[8,128]{1,0:T(8,128)S(1)}, u32[]{:S(2)}, u32[]{:S(2)}) collective-permute-start(f32[8,128]{1,0:T(8,128)S(1)} %get-tuple-element.26), channel_id=1, source_target_pairs={{0,192},{64,128},{128,64},{192,0},{1,193},{65,129},{129,65},{193,1... | collective-permute-start | bytes 12296 | tf_op jit(solution)/shard_map/ppermute | solution.py:479
  115.7 5.4 %collective-permute-start.5 = (f32[8,128]{1,0:T(8,128)S(1)}, f32[8,128]{1,0:T(8,128)S(1)}, u32[]{:S(2)}, u32[]{:S(2)}) collective-permute-start(f32[8,128]{1,0:T(8,128)S(1)} %get-tuple-element.26), channel_id=1, source_target_pairs={{0,128},{64,192},{128,0},{192,64},{1,129},{65,193},{129,1},{193,65... | collective-permute-start | bytes 12296 | tf_op jit(solution)/shard_map/ppermute | solution.py:479
  118.2 2.9 %collective-permute-start.4 = (f32[8,128]{1,0:T(8,128)S(1)}, f32[8,128]{1,0:T(8,128)S(1)}, u32[]{:S(2)}, u32[]{:S(2)}) collective-permute-start(f32[8,128]{1,0:T(8,128)S(1)} %get-tuple-element.26), channel_id=1, source_target_pairs={{0,64},{64,0},{128,192},{192,128},{1,65},{65,1},{129,193},{193,129... | collective-permute-start | bytes 12296 | tf_op jit(solution)/shard_map/ppermute | solution.py:479
  121.1 4.2 %collective-permute-start.9 = (f32[8,128]{1,0:T(8,128)S(1)}, f32[8,128]{1,0:T(8,128)S(1)}, u32[]{:S(2)}, u32[]{:S(2)}) collective-permute-start(f32[8,128]{1,0:T(8,128)S(1)} %add_add_fusion.1), channel_id=1, source_target_pairs={{0,48},{16,32},{32,16},{48,0},{1,49},{17,33},{33,17},{49,1},{2,50}... | collective-permute-start | bytes 12296 | tf_op jit(solution)/shard_map/ppermute | solution.py:479
  122.4 5.1 %collective-permute-start.8 = (f32[8,128]{1,0:T(8,128)S(1)}, f32[8,128]{1,0:T(8,128)S(1)}, u32[]{:S(2)}, u32[]{:S(2)}) collective-permute-start(f32[8,128]{1,0:T(8,128)S(1)} %add_add_fusion.1), channel_id=1, source_target_pairs={{0,32},{16,48},{32,0},{48,16},{1,33},{17,49},{33,1},{49,17},{2,34}... | collective-permute-start | bytes 12296 | tf_op jit(solution)/shard_map/ppermute | solution.py:479
  123.8 3.7 %collective-permute-start.7 = (f32[8,128]{1,0:T(8,128)S(1)}, f32[8,128]{1,0:T(8,128)S(1)}, u32[]{:S(2)}, u32[]{:S(2)}) collective-permute-start(f32[8,128]{1,0:T(8,128)S(1)} %add_add_fusion.1), channel_id=1, source_target_pairs={{0,16},{16,0},{32,48},{48,32},{1,17},{17,1},{33,49},{49,33},{2,18}... | collective-permute-start | bytes 12296 | tf_op jit(solution)/shard_map/ppermute | solution.py:479

commit v5 on v4

--- a/solution.py
+++ b/solution.py
@@ -96,15 +96,14 @@
     low_hbm,
     high_hbm,
     qd_hbm,
-    q_gain_ref,
-    k_gain_ref,
+    both_gains_hbm,
     dq_hbm,
     to_low_hbm,
     to_high_hbm,
     qn_hbm,
     dd_hbm,
-    chance_hbm,
-    score_hbm,
+    stats_hbm,
+    same_gains_hbm,
     kv_ref,
     low_ref,
     high_ref,
@@ -127,15 +126,18 @@
     d_side,
     qn,
     dd,
-    chance_own,
-    score_own,
+    stats,
     chance_l,
     chance_h,
     score_l,
     score_h,
     gains_ref,
     q_inverse,
+    both_gains,
+    gain_sem,
 ):
+    gain_copy = pltpu.make_async_copy(both_gains_hbm, both_gains, gain_sem)
+    gain_copy.start()
     arrivals = []
     for col in range(COLS):
         pairs = ((kv_hbm, kv_ref), (low_hbm, low_ref), (high_hbm, high_ref), (qd_hbm, qd_ref))
@@ -153,8 +155,9 @@
         copy.start()
         departures.append(copy)
 
-    q_gain = q_gain_ref[...]
-    k_gain = k_gain_ref[...]
+    gain_copy.wait()
+    q_gain = both_gains[0:1]
+    k_gain = both_gains[1:2]
     def prepare(col):
         for copy in arrivals[col]:
             copy.wait()
@@ -190,8 +193,9 @@
                     d_side[frame, at : at + TILE] = qd_ref[frame, row, col, 1, place]
 
     gains_ref[...] = jnp.zeros_like(gains_ref)
+    stats[...] = jnp.zeros_like(stats)
     sources = (
-        (kn_own, knt_own, vv_own, chance_own, score_own, 2, 0, 2 * PAIR, None),
+        (kn_own, knt_own, vv_own, None, None, 2, 0, 2 * PAIR, None),
         (kn_l, knt_l, vv_l, chance_l, score_l, 1, 0, PAIR, flags_ref[0].astype(F32)),
         (kn_h, knt_h, vv_h, chance_h, score_h, 1, PAIR, PAIR, flags_ref[1].astype(F32)),
     )
@@ -219,18 +223,20 @@
             chance = weights[number] * reciprocal[:, first : first + width]
             rounded = chance.astype(BF16)
             dots.append(jnp.sum(rounded.astype(F32) * weight_grads[number], axis=0, keepdims=True))
-            for step in range(count):
+            for step in range(count if store is not None else 0):
                 place = (1 - (step - before)) * width
                 store[w - before + step, :, place : place + width] = rounded[
                     step * frames * PAIR : (step + 1) * frames * PAIR
                 ]
         row_dot = spread(dots)
+        stats[w, 0:1] = reciprocal
+        stats[w, 1:2] = row_dot
         grads = []
         for number, (_, knt, _, _, store, frames, first, width, _) in enumerate(sources):
             chance = weights[number] * reciprocal[:, first : first + width]
             score = chance * (weight_grads[number] - row_dot[:, first : first + width])
             score = score.astype(BF16)
-            for step in range(count):
+            for step in range(count if store is not None else 0):
                 place = (1 - (step - before)) * width
                 store[w - before + step, :, place : place + width] = score[
                     step * frames * PAIR : (step + 1) * frames * PAIR
@@ -260,8 +266,6 @@
             out_ref[w, 0] = key_grad.astype(BF16)
             out_ref[w, 1] = value_grad.astype(BF16)
             send(out_ref.at[w], out_hbm.at[w])
-        send(chance_own.at[w], chance_hbm.at[w])
-        send(score_own.at[w], score_hbm.at[w])
 
     def extent(w):
         return w, min(w, 1), 2 if w in (0, WIDE - 1) else 3
@@ -279,6 +283,7 @@
         held = following
         if w > 0:
             key_column(w - 1)
+    send(stats, stats_hbm)
     key_column(WIDE - 1)
 
 
@@ -303,77 +308,143 @@
     return array.reshape((-1, 2, COLS) + array.shape[1:])
 
 
-def attention(flags, kv, low, high, qd, q_gain, k_gain):
+def attention(flags, kv, low, high, qd, gains):
     own, halo = WIDE * 2 * PAIR, WIDE * PAIR
     arrays = [grid_of(array) for array in (kv, low, high, qd)]
     side = ((WIDE, 2, PAIR, HD), BF16)
-    columns = ((WIDE, 2 * PAIR, 6 * PAIR), BF16)
+    stats = ((WIDE, 8, 2 * PAIR), F32)
     queries = ((own, HD), BF16)
-    outs = [((2, 2, COLS, PAIR + EXTRA, HD), BF16), side, side, queries, queries, columns, columns]
+    outs = [((2, 2, COLS, PAIR + EXTRA, HD), BF16), side, side, queries, queries, stats, ((8, HD), F32)]
     scratch = [pltpu.VMEM(array.shape, BF16) for array in arrays]
     scratch += [pltpu.VMEM(*out) for out in outs[:3]]
     scratch += [pltpu.SemaphoreType.DMA((COLS,)), pltpu.SemaphoreType.DMA]
     for rows in (own, halo, halo):
         scratch += [pltpu.VMEM((rows, HD), BF16), pltpu.VMEM((HD, rows), BF16), pltpu.VMEM((rows, HD), BF16)]
-    scratch += [pltpu.VMEM((2, halo, HD), BF16)] * 2 + [pltpu.VMEM(*out) for out in outs[3:]]
+    scratch += [pltpu.VMEM((2, halo, HD), BF16)] * 2 + [pltpu.VMEM(*out) for out in outs[3:6]]
     scratch += [pltpu.VMEM((WIDE, PAIR, 3 * PAIR), BF16)] * 4 + [pltpu.VMEM((16, HD), F32)]
-    scratch += [pltpu.VMEM((own, HD), F32)]
-    dq, *others = pl.pallas_call(
+    scratch += [pltpu.VMEM((own, HD), F32)] + [pltpu.VMEM((8, HD), F32)] + [pltpu.SemaphoreType.DMA]
+    dq, *others, _ = pl.pallas_call(
         attention_kernel,
         in_specs=[pl.BlockSpec(memory_space=pltpu.SMEM)]
-        + [pl.BlockSpec(memory_space=pl.ANY)] * 4
-        + [pl.BlockSpec(memory_space=pltpu.VMEM)] * 2,
+        + [pl.BlockSpec(memory_space=pl.ANY)] * 5,
         out_specs=[pl.BlockSpec(memory_space=pl.ANY)] * len(outs),
         out_shape=[pltpu.HBM(*out) for out in outs],
         scratch_shapes=scratch,
+        input_output_aliases={5: len(outs) - 1},
         name="attention",
         cost_estimate=pl.CostEstimate(
             flops=5 * 66 * PAIR * PAIR * PAIR * 2, bytes_accessed=8 << 20, transcendentals=0
         ),
         compiler_params=pltpu.CompilerParams(vmem_limit_bytes=ATTENTION_LIMIT),
-    )(flags, *arrays, q_gain, k_gain)
+    )(flags, *arrays, gains)
     return dq.reshape(GROUP, PAIR + EXTRA, HD), *others
 
 
-def own_kernel(qn_hbm, dd_hbm, chance_hbm, score_hbm, own_hbm, qn, dd, chance, score, own_ref, sems, out_sem):
-    arrivals = []
-    for w in range(WIDE):
-        pairs = [(chance_hbm.at[w], chance.at[w]), (score_hbm.at[w], score.at[w])]
-        if w == 0:
-            pairs = [(qn_hbm, qn), (dd_hbm, dd)] + pairs
-        copies = [pltpu.make_async_copy(source, target, sems.at[w]) for source, target in pairs]
-        for copy in copies:
-            copy.start()
-        arrivals.append(copies)
+def own_kernel(
+    kv_hbm,
+    qn_hbm,
+    dd_hbm,
+    stats_hbm,
+    k_gain_ref,
+    own_hbm,
+    kv_ref,
+    qn,
+    dd,
+    stats,
+    own_ref,
+    kn,
+    vv,
+    chance_own,
+    score_own,
+    query_sem,
+    in_sems,
+    out_sem,
+):
+    queries = [
+        pltpu.make_async_copy(source, target, query_sem)
+        for source, target in ((qn_hbm, qn), (dd_hbm, dd), (stats_hbm, stats))
+    ]
+    arrivals = [
+        pltpu.make_async_copy(kv_hbm.at[:, :, col], kv_ref.at[:, :, col], in_sems.at[col]) for col in range(COLS)
+    ]
+    for copy in arrivals[:1] + queries + arrivals[1:]:
+        copy.start()
+    k_gain = k_gain_ref[...]
+
+    def prepare(col):
+        arrivals[col].wait()
+        for frame in range(2):
+            for row in range(2):
+                raw = kv_ref[frame, row, col, 0].astype(F32)
+                normed = (raw * inverse_rms(raw) * k_gain).astype(BF16)
+                for part in range(2):
+                    place = slice(part * TILE, (part + 1) * TILE)
+                    at = ((2 * col + part) * 2 + frame) * PAIR + row * TILE
+                    kn[at : at + TILE] = normed[place]
+                    vv[at : at + TILE] = kv_ref[frame, row, col, 1, place]
+
+    def products(w):
+        first, last = max(w - 1, 0), min(w + 1, WIDE - 1)
+        rows = slice(first * 2 * PAIR, (last + 1) * 2 * PAIR)
+        q_rows = slice(w * 2 * PAIR, (w + 1) * 2 * PAIR)
+        weights = jnp.exp2(nt(kn[rows], qn[q_rows]) * SCALE_LOG2E)
+        return first, last, weights, nt(vv[rows], dd[q_rows])
+
+    def scores(w, first, last, weights, weight_grads):
+        chance = weights * stats[w, 0:1]
+        rounded = chance.astype(BF16)
+        score = (chance * (weight_grads - stats[w, 1:2])).astype(BF16)
+        for column in range(first, last + 1):
+            part = slice((column - first) * 2 * PAIR, (column - first + 1) * 2 * PAIR)
+            place = (1 - (column - w)) * 2 * PAIR
+            chance_own[column, :, place : place + 2 * PAIR] = rounded[part]
+            score_own[column, :, place : place + 2 * PAIR] = score[part]
+
     departures = []
-    for w in range(WIDE):
-        for copy in arrivals[w]:
-            copy.wait()
-        key_grad, value_grad = key_sums(chance, score, qn, dd, w, 2 * PAIR)
+
+    def key_column(w):
+        key_grad, value_grad = key_sums(chance_own, score_own, qn, dd, w, 2 * PAIR)
         own_ref[w, 0] = key_grad.astype(BF16)
         own_ref[w, 1] = value_grad.astype(BF16)
         copy = pltpu.make_async_copy(own_ref.at[w], own_hbm.at[w], out_sem)
         copy.start()
         departures.append(copy)
+
+    prepare(0)
+    for copy in queries:
+        copy.wait()
+    held = products(0)
+    for w in range(WIDE):
+        if w % 2 == 0 and w // 2 + 1 < COLS:
+            prepare(w // 2 + 1)
+        following = products(w + 1) if w + 1 < WIDE else None
+        scores(w, *held)
+        held = following
+        if w > 0:
+            key_column(w - 1)
+    key_column(WIDE - 1)
     for copy in departures:
         copy.wait()
 
 
-def own_sums(*arguments):
+def own_sums(kv, qn, dd, stats, k_gain):
     out = ((WIDE, 2, 2 * PAIR, HD), BF16)
+    arrays = [grid_of(kv), qn, dd, stats]
+    scratch = [pltpu.VMEM(array.shape, array.dtype) for array in arrays] + [pltpu.VMEM(*out)]
+    scratch += [pltpu.VMEM(qn.shape, BF16)] * 2 + [pltpu.VMEM((WIDE, 2 * PAIR, 6 * PAIR), BF16)] * 2
+    scratch += [pltpu.SemaphoreType.DMA, pltpu.SemaphoreType.DMA((COLS,)), pltpu.SemaphoreType.DMA]
     return pl.pallas_call(
         own_kernel,
-        in_specs=[pl.BlockSpec(memory_space=pl.ANY)] * 4,
+        in_specs=[pl.BlockSpec(memory_space=pl.ANY)] * 4 + [pl.BlockSpec(memory_space=pltpu.VMEM)],
         out_specs=pl.BlockSpec(memory_space=pl.ANY),
         out_shape=pltpu.HBM(*out),
-        scratch_shapes=[pltpu.VMEM(array.shape, array.dtype) for array in arguments]
-        + [pltpu.VMEM(*out), pltpu.SemaphoreType.DMA((WIDE,)), pltpu.SemaphoreType.DMA],
+        scratch_shapes=scratch,
         name="own_sums",
         cost_estimate=pl.CostEstimate(
-            flops=2 * 44 * PAIR * PAIR * PAIR * 2, bytes_accessed=8 << 20, transcendentals=0
+            flops=4 * 44 * PAIR * PAIR * PAIR * 2, bytes_accessed=8 << 20, transcendentals=0
         ),
         compiler_params=pltpu.CompilerParams(vmem_limit_bytes=LIMIT),
-    )(*arguments)
+    )(*arrays, k_gain)
 
 
 def finish_kernel(frame, kv_ref, own_ref, halo_ref, k_gain_ref, out_hbm, out_ref, sem):
@@ -488,16 +559,17 @@
     down = [(source + 1, source) for source in range(blocks - 1)]
     q_line = q_gain.reshape(1, HD)
     k_line = k_gain.reshape(1, HD)
+    gains = jnp.concatenate([q_line, k_line, jnp.ones((6, HD), F32)], axis=0)
 
     kv = swap(pack(k_raw, values))
     low = lax.ppermute(kv[HALF:], "x", up)
     high = lax.ppermute(kv[:HALF], "x", down)
     qd = swap(pack(q_raw, d_out))
-    dq, to_low, to_high, *stored = attention(flags, kv, low, high, qd, q_line, k_line)
+    dq, to_low, to_high, *stored = attention(flags, kv, low, high, qd, gains)
     arrived = swap(dq)
     from_low = lax.ppermute(to_high, "x", up)
     from_high = lax.ppermute(to_low, "x", down)
-    own = own_sums(*stored)
+    own = own_sums(kv, *stored, k_line)
     q_grad, lines = unpack_query(arrived)
     grads = finish(0, kv, own, from_low, k_line)
     grads = finish(1, kv, own, from_high, k_line, grads).reshape(GROUP, 2, PAIR, HD)

time: 142 us -> 141 us (level)
  waiting for transfers between devices: 67.3 us -> 63.9 us
    ppermute x1, waiting for transfers between devices: 4.66 us -> 2.58 us  [on_device(): from_low = lax.ppermute(to_high, 'x', up)]
    pallas_call x1, Pallas kernels: 4.9 us -> 6.72 us  [own_sums(): pl.pallas_call(own_kernel, in_specs=[pl.BlockSpec(memory_space=pl.ANY)] *...]
  transfers between devices with their start and end apart: 14 -> 14, of which waited for: 8 -> 8; matrix products, arithmetic and copies ran while one was open for 1% -> 2% of each run, Pallas kernels for 7% -> 8%
where the time goes in v5:
time: 141 us; the launch traced here: 140 us
  waiting for transfers between devices  63.9 us (45%)
  starting transfers between devices  45.9 us (33%)
  Pallas kernels  25 us (18%)
  local copies, waits for them, and re-layouts  3.57 us (3%)
    all_to_all x4, waiting for transfers between devices, swap(): return lax.all_to_all(array, 'g', 0, 0)  55.9 us
    all_to_all x4, starting transfers between devices, swap(): return lax.all_to_all(array, 'g', 0, 0)  26.4 us
    pallas_call x1, Pallas kernels, attention(): pl.pallas_call(attention_kernel, in_specs=[pl.BlockSpec(memory_space=pltp...  10.3 us
    ppermute x6, starting transfers between devices, sum_over(): lax.ppermute(lines, axis, [(source, source ^ step) for source in range(co...  7.55 us
    pallas_call x1, Pallas kernels, own_sums(): pl.pallas_call(own_kernel, in_specs=[pl.BlockSpec(memory_space=pl.ANY)] *...  6.72 us
    ppermute x6, waiting for transfers between devices, sum_over(): lax.ppermute(lines, axis, [(source, source ^ step) for source in range(co...  4.64 us
    pallas_call x2, Pallas kernels, pack(): pl.pallas_call(pack_kernel, in_specs=[pl.BlockSpec(memory_space=pl.ANY)]...  4.17 us
    ppermute x1, starting transfers between devices, on_device(): low = lax.ppermute(kv[HALF:], 'x', up)  3.4 us
  transfers between devices with their start and end apart: 14, of which 8 were waited for; matrix products, arithmetic and copies ran while one was open for 2% of the time, Pallas kernels for 8%

profile of v5, /device:TPU:2, one launch (start us, length us, event | category | flops | bytes accessed | tf_op | source)
XLA Modules:
  0.0 140.1 jit_solution(2055924738575501688)
XLA Ops:
  0.6 2.1 %pack.2 = bf16[16,2,128,128]{3,2,1,0:T(8,128)(2,1)} custom-call(bf16[1,128,1536]{2,1,0:T(8,128)(2,1)} %first_ref.2, bf16[1,128,1536]{2,1,0:T(8,128)(2,1)} %second_ref.2), custom_call_target="tpu_custom_call" | custom-call | tf_op jit(solution)/shard_map/pack/pallas_call | solution.py:63
  2.7 9.6 %all-to-all-start = ((bf16[16,2,128,128]{3,2,1,0:T(8,128)(2,1)}), bf16[16,2,128,128]{3,2,1,0:T(8,128)(2,1)S(1)}, u32[]{:S(2)}, u32[]{:S(2)}) async-start(bf16[16,2,128,128]{3,2,1,0:T(8,128)(2,1)} %pack.2), calls=%async_computation | async-start | bytes 2097152 | tf_op jit(solution)/shard_map/all_to_all | solution.py:543
  12.3 2.1 %pack.3 = bf16[16,2,128,128]{3,2,1,0:T(8,128)(2,1)} custom-call(bf16[1,128,1536]{2,1,0:T(8,128)(2,1)} %first_ref.3, bf16[1,128,1536]{2,1,0:T(8,128)(2,1)} %second_ref.3), custom_call_target="tpu_custom_call" | custom-call | tf_op jit(solution)/shard_map/pack/pallas_call | solution.py:63
  14.4 25.0 %all-to-all-done = bf16[16,2,128,128]{3,2,1,0:T(8,128)(2,1)S(1)} async-done(((bf16[16,2,128,128]{3,2,1,0:T(8,128)(2,1)}), bf16[16,2,128,128]{3,2,1,0:T(8,128)(2,1)S(1)}, u32[]{:S(2)}, u32[]{:S(2)}) %all-to-all-start) | async-done | bytes 1048608 | tf_op jit(solution)/shard_map/all_to_all | solution.py:543
  39.4 4.4 %all-to-all-start.1 = ((bf16[16,2,128,128]{3,2,1,0:T(8,128)(2,1)}), bf16[16,2,128,128]{3,2,1,0:T(8,128)(2,1)S(1)}, u32[]{:S(2)}, u32[]{:S(2)}) async-start(bf16[16,2,128,128]{3,2,1,0:T(8,128)(2,1)} %pack.3), calls=%async_computation.1 | async-start | bytes 2097152 | tf_op jit(solution)/shard_map/all_to_all | solution.py:543
  43.8 1.1 fusion
  44.9 2.4 %collective-permute-start.1 = (bf16[8,2,128,128]{3,2,1,0:T(8,128)(2,1)}, bf16[8,2,128,128]{3,2,1,0:T(8,128)(2,1)S(1)}, u32[]{:S(2)}, u32[]{:S(2)}) collective-permute-start(bf16[8,2,128,128]{3,2,1,0:T(8,128)(2,1)} %get-tuple-element.25), channel_id=1, source_target_pairs={{16,0},{32,16},{48,32},{17,1},{33,17},{49,33},{18,2},{34,18},{50,3... | collective-permute-start | bytes 1572872 | tf_op jit(solution)/shard_map/ppermute | solution.py:566
  47.3 3.4 %collective-permute-start = (bf16[8,2,128,128]{3,2,1,0:T(8,128)(2,1)}, bf16[8,2,128,128]{3,2,1,0:T(8,128)(2,1)S(1)}, u32[]{:S(2)}, u32[]{:S(2)}) collective-permute-start(bf16[8,2,128,128]{3,2,1,0:T(8,128)(2,1)} %get-tuple-element.26), channel_id=1, source_target_pairs={{0,16},{16,32},{32,48},{1,17},{17,33},{33,49},{2,18},{18,34},{34,5... | collective-permute-start | bytes 1572872 | tf_op jit(solution)/shard_map/ppermute | solution.py:565
  50.7 0.1 pad.2.clone
  50.8 0.1 add_convert_fusion.flags_ref
  50.9 0.7 copy-done.3
  51.6 0.0 copy-done.5
  51.6 0.7 maximum_maximum_fusion.both_gains_hbm
  52.2 18.9 %all-to-all-done.1 = bf16[16,2,128,128]{3,2,1,0:T(8,128)(2,1)S(1)} async-done(((bf16[16,2,128,128]{3,2,1,0:T(8,128)(2,1)}), bf16[16,2,128,128]{3,2,1,0:T(8,128)(2,1)S(1)}, u32[]{:S(2)}, u32[]{:S(2)}) %all-to-all-start.1) | async-done | bytes 1048608 | tf_op jit(solution)/shard_map/all_to_all | solution.py:543
  71.1 0.0 collective-permute-done.1
  71.1 0.0 collective-permute-done
  71.1 0.0 copy-done
  71.1 10.3 %attention.1 = (bf16[2,2,4,144,128]{4,3,2,1,0:T(8,128)(2,1)}, bf16[8,2,128,128]{3,2,1,0:T(8,128)(2,1)}, bf16[8,2,128,128]{3,2,1,0:T(8,128)(2,1)}, bf16[2048,128]...) custom-call(s32[3]{0:T(128)S(1)} %add_convert_fusion.flags_ref, ...), custom_call_target="tpu_custom_call", output_to_operand_aliasing={{6}: (5, {})} | custom-call | flops 1384120320 | bytes 8388608 | tf_op jit(solution)/shard_map/attention/pallas_call | solution.py:326
  81.4 0.0 copy-start.7
  81.4 0.0 copy-start.6
  81.4 4.6 %all-to-all-start.2 = ((bf16[16,144,128]{2,1,0:T(8,128)(2,1)}), bf16[16,144,128]{2,1,0:T(8,128)(2,1)S(1)}, u32[]{:S(2)}, u32[]{:S(2)}) async-start(bf16[16,144,128]{2,1,0:T(8,128)(2,1)} %bitcast.27), calls=%async_computation.2 | async-start | bytes 1179648 | tf_op jit(solution)/shard_map/all_to_all | solution.py:543
  86.0 3.4 %collective-permute-start.3 = (bf16[8,2,128,128]{3,2,1,0:T(8,128)(2,1)S(1)}, bf16[8,2,128,128]{3,2,1,0:T(8,128)(2,1)S(1)}, u32[]{:S(2)}, u32[]{:S(2)}) collective-permute-start(bf16[8,2,128,128]{3,2,1,0:T(8,128)(2,1)S(1)} %copy-done.7), channel_id=1, source_target_pairs={{0,16},{16,32},{32,48},{1,17},{17,33},{33,49},{2,18},{18,34},{34,5... | collective-permute-start | bytes 1572872 | tf_op jit(solution)/shard_map/ppermute | solution.py:570
  89.4 2.7 %collective-permute-start.2 = (bf16[8,2,128,128]{3,2,1,0:T(8,128)(2,1)S(1)}, bf16[8,2,128,128]{3,2,1,0:T(8,128)(2,1)S(1)}, u32[]{:S(2)}, u32[]{:S(2)}) collective-permute-start(bf16[8,2,128,128]{3,2,1,0:T(8,128)(2,1)S(1)} %copy-done.6), channel_id=1, source_target_pairs={{16,0},{32,16},{48,32},{17,1},{33,17},{49,33},{18,2},{34,18},{50,3... | collective-permute-start | bytes 1572872 | tf_op jit(solution)/shard_map/ppermute | solution.py:571
  92.1 0.0 copy-start.4
  92.1 6.7 %own_sums.1.own_ref = bf16[8,2,256,128]{3,2,1,0:T(8,128)(2,1)} custom-call(bf16[2,2,4,2,128,128]{5,4,3,2,1,0:T(8,128)(2,1)} %bitcast.16, bf16[2048,128]{1,0:T(8,128)(2,1)} %get-tuple-element.17.qn_hbm, bf16[2048,128]{1,0:T(8,128)(2,1)} %get-tuple-element.18.dd_hbm, f32[8,8,256]{2,1,0:T(8,128)} %get-tuple-element.19.stats_hbm, f32[1,128]{1,0:T(1,128)} %bitcast.20), custom_call_target="tpu_custom_call" | custom-call | flops 738197504 | bytes 8388608 | tf_op jit(solution)/shard_map/own_sums/pallas_call | solution.py:436
  98.9 2.6 %collective-permute-done.3.halo_ref = bf16[8,2,128,128]{3,2,1,0:T(8,128)(2,1)S(1)} collective-permute-done((bf16[8,2,128,128]{3,2,1,0:T(8,128)(2,1)S(1)}, bf16[8,2,128,128]{3,2,1,0:T(8,128)(2,1)S(1)}, u32[]{:S(2)}, u32[]{:S(2)}) %collective-permute-start.3) | collective-permute-done | bytes 524320 | tf_op jit(solution)/shard_map/ppermute | solution.py:570
  101.4 1.2 copy-done.2
  102.7 1.1 finish_low.1.first_hbm
  103.7 0.8 collective-permute-done.2.halo_ref
  104.6 1.1 finish_high.1
  105.7 0.0 all-to-all-done.2.in_ref
  105.7 7.8 %all-to-all-start.3 = ((bf16[16,2,128,128]{3,2,1,0:T(8,128)(2,1)}), bf16[16,2,128,128]{3,2,1,0:T(8,128)(2,1)S(1)}, u32[]{:S(2)}, u32[]{:S(2)}) async-start(bf16[16,2,128,128]{3,2,1,0:T(8,128)(2,1)} %bitcast.26), calls=%async_computation.3 | async-start | bytes 2097152 | tf_op jit(solution)/shard_map/all_to_all | solution.py:543
  113.5 0.8 unpack_query.1
  114.3 0.4 collective-permute-start.6
  114.8 2.5 %collective-permute-start.5 = (f32[8,128]{1,0:T(8,128)S(1)}, f32[8,128]{1,0:T(8,128)S(1)}, u32[]{:S(2)}, u32[]{:S(2)}) collective-permute-start(f32[8,128]{1,0:T(8,128)S(1)} %get-tuple-element.24), channel_id=1, source_target_pairs={{0,128},{64,192},{128,0},{192,64},{1,129},{65,193},{129,1},{193,65... | collective-permute-start | bytes 12296 | tf_op jit(solution)/shard_map/ppermute | solution.py:550
  117.3 0.4 collective-permute-start.4
  117.7 1.2 collective-permute-done.6
  118.9 1.2 collective-permute-done.5
  120.2 0.0 collective-permute-done.4
  120.2 1.3 collective-permute-start.9
  121.4 1.5 %collective-permute-start.8 = (f32[8,128]{1,0:T(8,128)S(1)}, f32[8,128]{1,0:T(8,128)S(1)}, u32[]{:S(2)}, u32[]{:S(2)}) collective-permute-start(f32[8,128]{1,0:T(8,128)S(1)} %add_add_fusion.1), channel_id=1, source_target_pairs={{0,32},{16,48},{32,0},{48,16},{1,33},{17,49},{33,1},{49,17},{2,34}... | collective-permute-start | bytes 12296 | tf_op jit(solution)/shard_map/ppermute | solution.py:550
  122.9 1.5 %collective-permute-start.7 = (f32[8,128]{1,0:T(8,128)S(1)}, f32[8,128]{1,0:T(8,128)S(1)}, u32[]{:S(2)}, u32[]{:S(2)}) collective-permute-start(f32[8,128]{1,0:T(8,128)S(1)} %add_add_fusion.1), channel_id=1, source_target_pairs={{0,16},{16,0},{32,48},{48,32},{1,17},{17,1},{33,49},{49,33},{2,18}... | collective-permute-start | bytes 12296 | tf_op jit(solution)/shard_map/ppermute | solution.py:550
  124.3 0.0 collective-permute-done.9
  124.4 2.2 %collective-permute-done.8 = f32[8,128]{1,0:T(8,128)S(1)} collective-permute-done((f32[8,128]{1,0:T(8,128)S(1)}, f32[8,128]{1,0:T(8,128)S(1)}, u32[]{:S(2)}, u32[]{:S(2)}) %collective-permute-start.8) | collective-permute-done | bytes 4128 | tf_op jit(solution)/shard_map/ppermute | solution.py:550
  126.5 0.0 collective-permute-done.7
  126.5 0.5 slice_bitcast_fusion
  127.1 12.0 %all-to-all-done.3.in_ref = bf16[16,2,128,128]{3,2,1,0:T(8,128)(2,1)S(1)} async-done(((bf16[16,2,128,128]{3,2,1,0:T(8,128)(2,1)}), bf16[16,2,128,128]{3,2,1,0:T(8,128)(2,1)S(1)}, u32[]{:S(2)}, u32[]{:S(2)}) %all-to-all-start.3) | async-done | bytes 1048608 | tf_op jit(solution)/shard_map/all_to_all | solution.py:543
  139.1 0.9 unpack.1
  (12 shorter events, 0.0 us)
Async XLA Ops:
  2.7 36.7 %all-to-all-start = ((bf16[16,2,128,128]{3,2,1,0:T(8,128)(2,1)}), bf16[16,2,128,128]{3,2,1,0:T(8,128)(2,1)S(1)}, u32[]{:S(2)}, u32[]{:S(2)}) async-start(bf16[16,2,128,128]{3,2,1,0:T(8,128)(2,1)} %pack.2), calls=%async_computation | async-start | bytes 2097152 | tf_op jit(solution)/shard_map/all_to_all | solution.py:543
  39.4 31.7 %copy-start = (bf16[16,2,128,128]{3,2,1,0:T(8,128)(2,1)}, bf16[16,2,128,128]{3,2,1,0:T(8,128)(2,1)S(1)}, u32[]{:S(2)}) copy-start(bf16[16,2,128,128]{3,2,1,0:T(8,128)(2,1)S(1)} %all-to-all-done) | copy-start | bytes 3145732
  39.4 31.7 %all-to-all-start.1 = ((bf16[16,2,128,128]{3,2,1,0:T(8,128)(2,1)}), bf16[16,2,128,128]{3,2,1,0:T(8,128)(2,1)S(1)}, u32[]{:S(2)}, u32[]{:S(2)}) async-start(bf16[16,2,128,128]{3,2,1,0:T(8,128)(2,1)} %pack.3), calls=%async_computation.1 | async-start | bytes 2097152 | tf_op jit(solution)/shard_map/all_to_all | solution.py:543
  44.9 26.2 %collective-permute-start.1 = (bf16[8,2,128,128]{3,2,1,0:T(8,128)(2,1)}, bf16[8,2,128,128]{3,2,1,0:T(8,128)(2,1)S(1)}, u32[]{:S(2)}, u32[]{:S(2)}) collective-permute-start(bf16[8,2,128,128]{3,2,1,0:T(8,128)(2,1)} %get-tuple-element.25), channel_id=1, source_target_pairs={{16,0},{32,16},{48,32},{17,1},{33,17},{49,33},{18,2},{34,18},{50,3... | collective-permute-start | bytes 1572872 | tf_op jit(solution)/shard_map/ppermute | solution.py:566
  47.3 23.8 %collective-permute-start = (bf16[8,2,128,128]{3,2,1,0:T(8,128)(2,1)}, bf16[8,2,128,128]{3,2,1,0:T(8,128)(2,1)S(1)}, u32[]{:S(2)}, u32[]{:S(2)}) collective-permute-start(bf16[8,2,128,128]{3,2,1,0:T(8,128)(2,1)} %get-tuple-element.26), channel_id=1, source_target_pairs={{0,16},{16,32},{32,48},{1,17},{17,33},{33,49},{2,18},{18,34},{34,5... | collective-permute-start | bytes 1572872 | tf_op jit(solution)/shard_map/ppermute | solution.py:565
  50.9 0.7 copy-start.3
  50.9 0.7 copy-start.5
  81.4 4.6 %copy-start.7 = (bf16[8,2,128,128]{3,2,1,0:T(8,128)(2,1)S(1)}, bf16[8,2,128,128]{3,2,1,0:T(8,128)(2,1)}, u32[]{:S(2)}) copy-start(bf16[8,2,128,128]{3,2,1,0:T(8,128)(2,1)} %get-tuple-element.21) | copy-start | bytes 1572868
  81.4 8.0 %copy-start.6 = (bf16[8,2,128,128]{3,2,1,0:T(8,128)(2,1)S(1)}, bf16[8,2,128,128]{3,2,1,0:T(8,128)(2,1)}, u32[]{:S(2)}) copy-start(bf16[8,2,128,128]{3,2,1,0:T(8,128)(2,1)} %get-tuple-element.20) | copy-start | bytes 1572868
  81.4 24.2 %all-to-all-start.2 = ((bf16[16,144,128]{2,1,0:T(8,128)(2,1)}), bf16[16,144,128]{2,1,0:T(8,128)(2,1)S(1)}, u32[]{:S(2)}, u32[]{:S(2)}) async-start(bf16[16,144,128]{2,1,0:T(8,128)(2,1)} %bitcast.27), calls=%async_computation.2 | async-start | bytes 1179648 | tf_op jit(solution)/shard_map/all_to_all | solution.py:543
  86.0 15.4 %collective-permute-start.3 = (bf16[8,2,128,128]{3,2,1,0:T(8,128)(2,1)S(1)}, bf16[8,2,128,128]{3,2,1,0:T(8,128)(2,1)S(1)}, u32[]{:S(2)}, u32[]{:S(2)}) collective-permute-start(bf16[8,2,128,128]{3,2,1,0:T(8,128)(2,1)S(1)} %copy-done.7), channel_id=1, source_target_pairs={{0,16},{16,32},{32,48},{1,17},{17,33},{33,49},{2,18},{18,34},{34,5... | collective-permute-start | bytes 1572872 | tf_op jit(solution)/shard_map/ppermute | solution.py:570
  89.4 15.1 %collective-permute-start.2 = (bf16[8,2,128,128]{3,2,1,0:T(8,128)(2,1)S(1)}, bf16[8,2,128,128]{3,2,1,0:T(8,128)(2,1)S(1)}, u32[]{:S(2)}, u32[]{:S(2)}) collective-permute-start(bf16[8,2,128,128]{3,2,1,0:T(8,128)(2,1)S(1)} %copy-done.6), channel_id=1, source_target_pairs={{16,0},{32,16},{48,32},{17,1},{33,17},{49,33},{18,2},{34,18},{50,3... | collective-permute-start | bytes 1572872 | tf_op jit(solution)/shard_map/ppermute | solution.py:571
  92.1 9.3 %copy-start.1 = (bf16[16,2,128,128]{3,2,1,0:T(8,128)(2,1)S(1)}, bf16[16,2,128,128]{3,2,1,0:T(8,128)(2,1)}, u32[]{:S(2)}) copy-start(bf16[16,2,128,128]{3,2,1,0:T(8,128)(2,1)} %copy-done) | copy-start | bytes 3145732
  92.1 9.3 %copy-start.4 = (f32[128]{0:T(128)S(1)}, f32[128]{0:T(128)}, u32[]{:S(2)}) copy-start(f32[128]{0:T(128)} %param.11) | copy-start | bytes 1540
  101.4 1.2 copy-start.2
  105.7 33.4 %all-to-all-start.3 = ((bf16[16,2,128,128]{3,2,1,0:T(8,128)(2,1)}), bf16[16,2,128,128]{3,2,1,0:T(8,128)(2,1)S(1)}, u32[]{:S(2)}, u32[]{:S(2)}) async-start(bf16[16,2,128,128]{3,2,1,0:T(8,128)(2,1)} %bitcast.26), calls=%async_computation.3 | async-start | bytes 2097152 | tf_op jit(solution)/shard_map/all_to_all | solution.py:543
  114.3 4.6 %collective-permute-start.6 = (f32[8,128]{1,0:T(8,128)S(1)}, f32[8,128]{1,0:T(8,128)S(1)}, u32[]{:S(2)}, u32[]{:S(2)}) collective-permute-start(f32[8,128]{1,0:T(8,128)S(1)} %get-tuple-element.24), channel_id=1, source_target_pairs={{0,192},{64,128},{128,64},{192,0},{1,193},{65,129},{129,65},{193,1... | collective-permute-start | bytes 12296 | tf_op jit(solution)/shard_map/ppermute | solution.py:550
  114.8 5.4 %collective-permute-start.5 = (f32[8,128]{1,0:T(8,128)S(1)}, f32[8,128]{1,0:T(8,128)S(1)}, u32[]{:S(2)}, u32[]{:S(2)}) collective-permute-start(f32[8,128]{1,0:T(8,128)S(1)} %get-tuple-element.24), channel_id=1, source_target_pairs={{0,128},{64,192},{128,0},{192,64},{1,129},{65,193},{129,1},{193,65... | collective-permute-start | bytes 12296 | tf_op jit(solution)/shard_map/ppermute | solution.py:550
  117.3 2.9 %collective-permute-start.4 = (f32[8,128]{1,0:T(8,128)S(1)}, f32[8,128]{1,0:T(8,128)S(1)}, u32[]{:S(2)}, u32[]{:S(2)}) collective-permute-start(f32[8,128]{1,0:T(8,128)S(1)} %get-tuple-element.24), channel_id=1, source_target_pairs={{0,64},{64,0},{128,192},{192,128},{1,65},{65,1},{129,193},{193,129... | collective-permute-start | bytes 12296 | tf_op jit(solution)/shard_map/ppermute | solution.py:550
  120.2 4.2 %collective-permute-start.9 = (f32[8,128]{1,0:T(8,128)S(1)}, f32[8,128]{1,0:T(8,128)S(1)}, u32[]{:S(2)}, u32[]{:S(2)}) collective-permute-start(f32[8,128]{1,0:T(8,128)S(1)} %add_add_fusion.1), channel_id=1, source_target_pairs={{0,48},{16,32},{32,16},{48,0},{1,49},{17,33},{33,17},{49,1},{2,50}... | collective-permute-start | bytes 12296 | tf_op jit(solution)/shard_map/ppermute | solution.py:550
  121.4 5.1 %collective-permute-start.8 = (f32[8,128]{1,0:T(8,128)S(1)}, f32[8,128]{1,0:T(8,128)S(1)}, u32[]{:S(2)}, u32[]{:S(2)}) collective-permute-start(f32[8,128]{1,0:T(8,128)S(1)} %add_add_fusion.1), channel_id=1, source_target_pairs={{0,32},{16,48},{32,0},{48,16},{1,33},{17,49},{33,1},{49,17},{2,34}... | collective-permute-start | bytes 12296 | tf_op jit(solution)/shard_map/ppermute | solution.py:550
  122.9 3.7 %collective-permute-start.7 = (f32[8,128]{1,0:T(8,128)S(1)}, f32[8,128]{1,0:T(8,128)S(1)}, u32[]{:S(2)}, u32[]{:S(2)}) collective-permute-start(f32[8,128]{1,0:T(8,128)S(1)} %add_add_fusion.1), channel_id=1, source_target_pairs={{0,16},{16,0},{32,48},{48,32},{1,17},{17,1},{33,49},{49,33},{2,18}... | collective-permute-start | bytes 12296 | tf_op jit(solution)/shard_map/ppermute | solution.py:550

commit v6 on v5

--- a/solution.py
+++ b/solution.py
@@ -346,19 +346,17 @@
     dd_hbm,
     stats_hbm,
     k_gain_ref,
-    own_hbm,
+    own_ref,
     kv_ref,
     qn,
     dd,
     stats,
-    own_ref,
     kn,
     vv,
     chance_own,
     score_own,
     query_sem,
     in_sems,
-    out_sem,
 ):
     queries = [
         pltpu.make_async_copy(source, target, query_sem)
@@ -400,15 +398,10 @@
             chance_own[column, :, place : place + 2 * PAIR] = rounded[part]
             score_own[column, :, place : place + 2 * PAIR] = score[part]
 
-    departures = []
-
     def key_column(w):
         key_grad, value_grad = key_sums(chance_own, score_own, qn, dd, w, 2 * PAIR)
         own_ref[w, 0] = key_grad.astype(BF16)
         own_ref[w, 1] = value_grad.astype(BF16)
-        copy = pltpu.make_async_copy(own_ref.at[w], own_hbm.at[w], out_sem)
-        copy.start()
-        departures.append(copy)
 
     prepare(0)
     for copy in queries:
@@ -423,27 +416,25 @@
         if w > 0:
             key_column(w - 1)
     key_column(WIDE - 1)
-    for copy in departures:
-        copy.wait()
 
 
 def own_sums(kv, qn, dd, stats, k_gain):
     out = ((WIDE, 2, 2 * PAIR, HD), BF16)
     arrays = [grid_of(kv), qn, dd, stats]
-    scratch = [pltpu.VMEM(array.shape, array.dtype) for array in arrays] + [pltpu.VMEM(*out)]
+    scratch = [pltpu.VMEM(array.shape, array.dtype) for array in arrays]
     scratch += [pltpu.VMEM(qn.shape, BF16)] * 2 + [pltpu.VMEM((WIDE, 2 * PAIR, 6 * PAIR), BF16)] * 2
-    scratch += [pltpu.SemaphoreType.DMA, pltpu.SemaphoreType.DMA((COLS,)), pltpu.SemaphoreType.DMA]
+    scratch += [pltpu.SemaphoreType.DMA, pltpu.SemaphoreType.DMA((COLS,))]
     return pl.pallas_call(
         own_kernel,
         in_specs=[pl.BlockSpec(memory_space=pl.ANY)] * 4 + [pl.BlockSpec(memory_space=pltpu.VMEM)],
-        out_specs=pl.BlockSpec(memory_space=pl.ANY),
-        out_shape=pltpu.HBM(*out),
+        out_specs=pl.BlockSpec(memory_space=pltpu.VMEM),
+        out_shape=jax.ShapeDtypeStruct(*out),
         scratch_shapes=scratch,
         name="own_sums",
         cost_estimate=pl.CostEstimate(
             flops=4 * 44 * PAIR * PAIR * PAIR * 2, bytes_accessed=8 << 20, transcendentals=0
         ),
-        compiler_params=pltpu.CompilerParams(vmem_limit_bytes=LIMIT),
+        compiler_params=pltpu.CompilerParams(vmem_limit_bytes=ATTENTION_LIMIT),
     )(*arrays, k_gain)
 
 

time: 141 us -> 141 us (level)
  waiting for transfers between devices: 63.9 us -> 67.7 us
  Pallas kernels: 25 us -> 22.6 us
    ppermute x1, waiting for transfers between devices: 2.58 us -> 5.17 us  [on_device(): from_low = lax.ppermute(to_high, 'x', up)]
    pallas_call x1, Pallas kernels: 6.72 us -> 4.33 us  [own_sums(): pl.pallas_call(own_kernel, in_specs=[pl.BlockSpec(memory_space=pl.ANY)] *...]
  transfers between devices with their start and end apart: 14 -> 14, of which waited for: 8 -> 8; matrix products, arithmetic and copies ran while one was open for 2% -> 2% of each run, Pallas kernels for 8% -> 7%
where the time goes in v6:
time: 141 us; the launch traced here: 140 us
  waiting for transfers between devices  67.7 us (48%)
  starting transfers between devices  45.8 us (32%)
  Pallas kernels  22.6 us (16%)
  local copies, waits for them, and re-layouts  2.3 us (2%)
    all_to_all x4, waiting for transfers between devices, swap(): return lax.all_to_all(array, 'g', 0, 0)  55.8 us
    all_to_all x4, starting transfers between devices, swap(): return lax.all_to_all(array, 'g', 0, 0)  26.4 us
    pallas_call x1, Pallas kernels, attention(): pl.pallas_call(attention_kernel, in_specs=[pl.BlockSpec(memory_space=pltp...  10.3 us
    ppermute x6, starting transfers between devices, sum_over(): lax.ppermute(lines, axis, [(source, source ^ step) for source in range(co...  7.55 us
    ppermute x1, waiting for transfers between devices, on_device(): from_low = lax.ppermute(to_high, 'x', up)  5.17 us
    ppermute x6, waiting for transfers between devices, sum_over(): lax.ppermute(lines, axis, [(source, source ^ step) for source in range(co...  4.67 us
    pallas_call x1, Pallas kernels, own_sums(): pl.pallas_call(own_kernel, in_specs=[pl.BlockSpec(memory_space=pl.ANY)] *...  4.33 us
    pallas_call x2, Pallas kernels, pack(): pl.pallas_call(pack_kernel, in_specs=[pl.BlockSpec(memory_space=pl.ANY)]...  4.18 us
  transfers between devices with their start and end apart: 14, of which 8 were waited for; matrix products, arithmetic and copies ran while one was open for 2% of the time, Pallas kernels for 7%

profile of v6, /device:TPU:2, one launch (start us, length us, event | category | flops | bytes accessed | tf_op | source)
XLA Modules:
  0.0 140.2 jit_solution(16192951648936413257)
XLA Ops:
  0.6 2.1 %pack.2 = bf16[16,2,128,128]{3,2,1,0:T(8,128)(2,1)} custom-call(bf16[1,128,1536]{2,1,0:T(8,128)(2,1)} %first_ref.2, bf16[1,128,1536]{2,1,0:T(8,128)(2,1)} %second_ref.2), custom_call_target="tpu_custom_call" | custom-call | tf_op jit(solution)/shard_map/pack/pallas_call | solution.py:63
  2.7 9.6 %all-to-all-start = ((bf16[16,2,128,128]{3,2,1,0:T(8,128)(2,1)}), bf16[16,2,128,128]{3,2,1,0:T(8,128)(2,1)S(1)}, u32[]{:S(2)}, u32[]{:S(2)}) async-start(bf16[16,2,128,128]{3,2,1,0:T(8,128)(2,1)} %pack.2), calls=%async_computation | async-start | bytes 2097152 | tf_op jit(solution)/shard_map/all_to_all | solution.py:534
  12.3 2.1 %pack.3 = bf16[16,2,128,128]{3,2,1,0:T(8,128)(2,1)} custom-call(bf16[1,128,1536]{2,1,0:T(8,128)(2,1)} %first_ref.3, bf16[1,128,1536]{2,1,0:T(8,128)(2,1)} %second_ref.3), custom_call_target="tpu_custom_call" | custom-call | tf_op jit(solution)/shard_map/pack/pallas_call | solution.py:63
  14.4 24.9 %all-to-all-done = bf16[16,2,128,128]{3,2,1,0:T(8,128)(2,1)S(1)} async-done(((bf16[16,2,128,128]{3,2,1,0:T(8,128)(2,1)}), bf16[16,2,128,128]{3,2,1,0:T(8,128)(2,1)S(1)}, u32[]{:S(2)}, u32[]{:S(2)}) %all-to-all-start) | async-done | bytes 1048608 | tf_op jit(solution)/shard_map/all_to_all | solution.py:534
  39.4 4.4 %all-to-all-start.1 = ((bf16[16,2,128,128]{3,2,1,0:T(8,128)(2,1)}), bf16[16,2,128,128]{3,2,1,0:T(8,128)(2,1)S(1)}, u32[]{:S(2)}, u32[]{:S(2)}) async-start(bf16[16,2,128,128]{3,2,1,0:T(8,128)(2,1)} %pack.3), calls=%async_computation.1 | async-start | bytes 2097152 | tf_op jit(solution)/shard_map/all_to_all | solution.py:534
  43.8 1.0 fusion
  44.8 2.4 %collective-permute-start.1 = (bf16[8,2,128,128]{3,2,1,0:T(8,128)(2,1)}, bf16[8,2,128,128]{3,2,1,0:T(8,128)(2,1)S(1)}, u32[]{:S(2)}, u32[]{:S(2)}) collective-permute-start(bf16[8,2,128,128]{3,2,1,0:T(8,128)(2,1)} %get-tuple-element.25), channel_id=1, source_target_pairs={{16,0},{32,16},{48,32},{17,1},{33,17},{49,33},{18,2},{34,18},{50,3... | collective-permute-start | bytes 1572872 | tf_op jit(solution)/shard_map/ppermute | solution.py:557
  47.2 3.4 %collective-permute-start = (bf16[8,2,128,128]{3,2,1,0:T(8,128)(2,1)}, bf16[8,2,128,128]{3,2,1,0:T(8,128)(2,1)S(1)}, u32[]{:S(2)}, u32[]{:S(2)}) collective-permute-start(bf16[8,2,128,128]{3,2,1,0:T(8,128)(2,1)} %get-tuple-element.26), channel_id=1, source_target_pairs={{0,16},{16,32},{32,48},{1,17},{17,33},{33,49},{2,18},{18,34},{34,5... | collective-permute-start | bytes 1572872 | tf_op jit(solution)/shard_map/ppermute | solution.py:556
  50.7 0.1 pad.2.clone
  50.7 0.1 add_convert_fusion.flags_ref
  50.8 0.7 copy-done.3
  51.5 0.0 copy-done.4
  51.5 0.7 maximum_maximum_fusion.both_gains_hbm
  52.2 18.9 %all-to-all-done.1 = bf16[16,2,128,128]{3,2,1,0:T(8,128)(2,1)S(1)} async-done(((bf16[16,2,128,128]{3,2,1,0:T(8,128)(2,1)}), bf16[16,2,128,128]{3,2,1,0:T(8,128)(2,1)S(1)}, u32[]{:S(2)}, u32[]{:S(2)}) %all-to-all-start.1) | async-done | bytes 1048608 | tf_op jit(solution)/shard_map/all_to_all | solution.py:534
  71.1 0.0 collective-permute-done.1
  71.1 0.0 collective-permute-done
  71.1 10.3 %attention.1 = (bf16[2,2,4,144,128]{4,3,2,1,0:T(8,128)(2,1)}, bf16[8,2,128,128]{3,2,1,0:T(8,128)(2,1)}, bf16[8,2,128,128]{3,2,1,0:T(8,128)(2,1)}, bf16[2048,128]...) custom-call(s32[3]{0:T(128)S(1)} %add_convert_fusion.flags_ref, ...), custom_call_target="tpu_custom_call", output_to_operand_aliasing={{6}: (5, {})} | custom-call | flops 1384120320 | bytes 8388608 | tf_op jit(solution)/shard_map/attention/pallas_call | solution.py:326
  81.4 0.0 copy-start
  81.4 0.0 copy-start.1
  81.4 0.0 copy-start.2
  81.4 4.6 %all-to-all-start.2 = ((bf16[16,144,128]{2,1,0:T(8,128)(2,1)}), bf16[16,144,128]{2,1,0:T(8,128)(2,1)S(1)}, u32[]{:S(2)}, u32[]{:S(2)}) async-start(bf16[16,144,128]{2,1,0:T(8,128)(2,1)} %bitcast.27), calls=%async_computation.2 | async-start | bytes 1179648 | tf_op jit(solution)/shard_map/all_to_all | solution.py:534
  86.0 3.4 %collective-permute-start.3 = (bf16[8,2,128,128]{3,2,1,0:T(8,128)(2,1)}, bf16[8,2,128,128]{3,2,1,0:T(8,128)(2,1)S(1)}, u32[]{:S(2)}, u32[]{:S(2)}) collective-permute-start(bf16[8,2,128,128]{3,2,1,0:T(8,128)(2,1)} %get-tuple-element.21), channel_id=1, source_target_pairs={{0,16},{16,32},{32,48},{1,17},{17,33},{33,49},{2,18},{18,34},{34,5... | collective-permute-start | bytes 1572872 | tf_op jit(solution)/shard_map/ppermute | solution.py:561
  89.4 2.6 %collective-permute-start.2 = (bf16[8,2,128,128]{3,2,1,0:T(8,128)(2,1)}, bf16[8,2,128,128]{3,2,1,0:T(8,128)(2,1)S(1)}, u32[]{:S(2)}, u32[]{:S(2)}) collective-permute-start(bf16[8,2,128,128]{3,2,1,0:T(8,128)(2,1)} %get-tuple-element.20), channel_id=1, source_target_pairs={{16,0},{32,16},{48,32},{17,1},{33,17},{49,33},{18,2},{34,18},{50,3... | collective-permute-start | bytes 1572872 | tf_op jit(solution)/shard_map/ppermute | solution.py:562
  92.0 0.0 copy-done
  92.1 0.0 copy-done.1
  92.1 4.3 %own_sums.1.own_ref = bf16[8,2,256,128]{3,2,1,0:T(8,128)(2,1)S(1)} custom-call(bf16[2,2,4,2,128,128]{5,4,3,2,1,0:T(8,128)(2,1)S(1)} %bitcast.16, bf16[2048,128]{1,0:T(8,128)(2,1)S(1)} %copy-done, bf16[2048,128]{1,0:T(8,128)(2,1)S(1)} %copy-done.1, f32[8,8,256]{2,1,0:T(8,128)S(1)} %copy-done.2, f32[1,128]{1,0:T(1,128)S(1)} %bitcast.21), custom_call_target="tpu_custom_call" | custom-call | flops 738197504 | bytes 8388608 | tf_op jit(solution)/shard_map/own_sums/pallas_call | solution.py:427
  96.4 5.2 %collective-permute-done.3.halo_ref = bf16[8,2,128,128]{3,2,1,0:T(8,128)(2,1)S(1)} collective-permute-done((bf16[8,2,128,128]{3,2,1,0:T(8,128)(2,1)}, bf16[8,2,128,128]{3,2,1,0:T(8,128)(2,1)S(1)}, u32[]{:S(2)}, u32[]{:S(2)}) %collective-permute-start.3) | collective-permute-done | bytes 524320 | tf_op jit(solution)/shard_map/ppermute | solution.py:561
  101.6 1.1 finish_low.1.first_hbm
  102.7 2.1 %collective-permute-done.2.halo_ref = bf16[8,2,128,128]{3,2,1,0:T(8,128)(2,1)S(1)} collective-permute-done((bf16[8,2,128,128]{3,2,1,0:T(8,128)(2,1)}, bf16[8,2,128,128]{3,2,1,0:T(8,128)(2,1)S(1)}, u32[]{:S(2)}, u32[]{:S(2)}) %collective-permute-start.2) | collective-permute-done | bytes 524320 | tf_op jit(solution)/shard_map/ppermute | solution.py:562
  104.7 1.1 finish_high.1
  105.8 0.0 all-to-all-done.2.in_ref
  105.8 7.8 %all-to-all-start.3 = ((bf16[16,2,128,128]{3,2,1,0:T(8,128)(2,1)}), bf16[16,2,128,128]{3,2,1,0:T(8,128)(2,1)S(1)}, u32[]{:S(2)}, u32[]{:S(2)}) async-start(bf16[16,2,128,128]{3,2,1,0:T(8,128)(2,1)} %bitcast.26), calls=%async_computation.3 | async-start | bytes 2097152 | tf_op jit(solution)/shard_map/all_to_all | solution.py:534
  113.7 0.8 unpack_query.1
  114.5 0.4 collective-permute-start.6
  114.9 2.5 %collective-permute-start.5 = (f32[8,128]{1,0:T(8,128)S(1)}, f32[8,128]{1,0:T(8,128)S(1)}, u32[]{:S(2)}, u32[]{:S(2)}) collective-permute-start(f32[8,128]{1,0:T(8,128)S(1)} %get-tuple-element.24), channel_id=1, source_target_pairs={{0,128},{64,192},{128,0},{192,64},{1,129},{65,193},{129,1},{193,65... | collective-permute-start | bytes 12296 | tf_op jit(solution)/shard_map/ppermute | solution.py:541
  117.4 0.4 collective-permute-start.4
  117.8 1.2 collective-permute-done.6
  119.0 1.2 collective-permute-done.5
  120.3 0.0 collective-permute-done.4
  120.3 1.3 collective-permute-start.9
  121.6 1.4 collective-permute-start.8
  123.0 1.5 %collective-permute-start.7 = (f32[8,128]{1,0:T(8,128)S(1)}, f32[8,128]{1,0:T(8,128)S(1)}, u32[]{:S(2)}, u32[]{:S(2)}) collective-permute-start(f32[8,128]{1,0:T(8,128)S(1)} %add_add_fusion.1), channel_id=1, source_target_pairs={{0,16},{16,0},{32,48},{48,32},{1,17},{17,1},{33,49},{49,33},{2,18}... | collective-permute-start | bytes 12296 | tf_op jit(solution)/shard_map/ppermute | solution.py:541
  124.4 0.0 collective-permute-done.9
  124.4 2.2 %collective-permute-done.8 = f32[8,128]{1,0:T(8,128)S(1)} collective-permute-done((f32[8,128]{1,0:T(8,128)S(1)}, f32[8,128]{1,0:T(8,128)S(1)}, u32[]{:S(2)}, u32[]{:S(2)}) %collective-permute-start.8) | collective-permute-done | bytes 4128 | tf_op jit(solution)/shard_map/ppermute | solution.py:541
  126.7 0.0 collective-permute-done.7
  126.7 0.5 slice_bitcast_fusion
  127.2 11.9 %all-to-all-done.3.in_ref = bf16[16,2,128,128]{3,2,1,0:T(8,128)(2,1)S(1)} async-done(((bf16[16,2,128,128]{3,2,1,0:T(8,128)(2,1)}), bf16[16,2,128,128]{3,2,1,0:T(8,128)(2,1)S(1)}, u32[]{:S(2)}, u32[]{:S(2)}) %all-to-all-start.3) | async-done | bytes 1048608 | tf_op jit(solution)/shard_map/all_to_all | solution.py:534
  139.2 0.9 unpack.1
  (6 shorter events, 0.0 us)
Async XLA Ops:
  2.7 36.7 %all-to-all-start = ((bf16[16,2,128,128]{3,2,1,0:T(8,128)(2,1)}), bf16[16,2,128,128]{3,2,1,0:T(8,128)(2,1)S(1)}, u32[]{:S(2)}, u32[]{:S(2)}) async-start(bf16[16,2,128,128]{3,2,1,0:T(8,128)(2,1)} %pack.2), calls=%async_computation | async-start | bytes 2097152 | tf_op jit(solution)/shard_map/all_to_all | solution.py:534
  39.4 31.7 %all-to-all-start.1 = ((bf16[16,2,128,128]{3,2,1,0:T(8,128)(2,1)}), bf16[16,2,128,128]{3,2,1,0:T(8,128)(2,1)S(1)}, u32[]{:S(2)}, u32[]{:S(2)}) async-start(bf16[16,2,128,128]{3,2,1,0:T(8,128)(2,1)} %pack.3), calls=%async_computation.1 | async-start | bytes 2097152 | tf_op jit(solution)/shard_map/all_to_all | solution.py:534
  44.8 26.3 %collective-permute-start.1 = (bf16[8,2,128,128]{3,2,1,0:T(8,128)(2,1)}, bf16[8,2,128,128]{3,2,1,0:T(8,128)(2,1)S(1)}, u32[]{:S(2)}, u32[]{:S(2)}) collective-permute-start(bf16[8,2,128,128]{3,2,1,0:T(8,128)(2,1)} %get-tuple-element.25), channel_id=1, source_target_pairs={{16,0},{32,16},{48,32},{17,1},{33,17},{49,33},{18,2},{34,18},{50,3... | collective-permute-start | bytes 1572872 | tf_op jit(solution)/shard_map/ppermute | solution.py:557
  47.2 23.8 %collective-permute-start = (bf16[8,2,128,128]{3,2,1,0:T(8,128)(2,1)}, bf16[8,2,128,128]{3,2,1,0:T(8,128)(2,1)S(1)}, u32[]{:S(2)}, u32[]{:S(2)}) collective-permute-start(bf16[8,2,128,128]{3,2,1,0:T(8,128)(2,1)} %get-tuple-element.26), channel_id=1, source_target_pairs={{0,16},{16,32},{32,48},{1,17},{17,33},{33,49},{2,18},{18,34},{34,5... | collective-permute-start | bytes 1572872 | tf_op jit(solution)/shard_map/ppermute | solution.py:556
  50.8 0.7 copy-start.3
  50.8 0.7 copy-start.4
  81.4 10.7 %copy-start = (bf16[2048,128]{1,0:T(8,128)(2,1)S(1)}, bf16[2048,128]{1,0:T(8,128)(2,1)}, u32[]{:S(2)}) copy-start(bf16[2048,128]{1,0:T(8,128)(2,1)} %get-tuple-element.17.qn_hbm) | copy-start | bytes 1572868
  81.4 10.7 %copy-start.1 = (bf16[2048,128]{1,0:T(8,128)(2,1)S(1)}, bf16[2048,128]{1,0:T(8,128)(2,1)}, u32[]{:S(2)}) copy-start(bf16[2048,128]{1,0:T(8,128)(2,1)} %get-tuple-element.18.dd_hbm) | copy-start | bytes 1572868
  81.4 10.7 %copy-start.2 = (f32[8,8,256]{2,1,0:T(8,128)S(1)}, f32[8,8,256]{2,1,0:T(8,128)}, u32[]{:S(2)}) copy-start(f32[8,8,256]{2,1,0:T(8,128)} %get-tuple-element.19.stats_hbm) | copy-start | bytes 196612
  81.4 24.4 %all-to-all-start.2 = ((bf16[16,144,128]{2,1,0:T(8,128)(2,1)}), bf16[16,144,128]{2,1,0:T(8,128)(2,1)S(1)}, u32[]{:S(2)}, u32[]{:S(2)}) async-start(bf16[16,144,128]{2,1,0:T(8,128)(2,1)} %bitcast.27), calls=%async_computation.2 | async-start | bytes 1179648 | tf_op jit(solution)/shard_map/all_to_all | solution.py:534
  86.0 15.6 %collective-permute-start.3 = (bf16[8,2,128,128]{3,2,1,0:T(8,128)(2,1)}, bf16[8,2,128,128]{3,2,1,0:T(8,128)(2,1)S(1)}, u32[]{:S(2)}, u32[]{:S(2)}) collective-permute-start(bf16[8,2,128,128]{3,2,1,0:T(8,128)(2,1)} %get-tuple-element.21), channel_id=1, source_target_pairs={{0,16},{16,32},{32,48},{1,17},{17,33},{33,49},{2,18},{18,34},{34,5... | collective-permute-start | bytes 1572872 | tf_op jit(solution)/shard_map/ppermute | solution.py:561
  89.4 15.3 %collective-permute-start.2 = (bf16[8,2,128,128]{3,2,1,0:T(8,128)(2,1)}, bf16[8,2,128,128]{3,2,1,0:T(8,128)(2,1)S(1)}, u32[]{:S(2)}, u32[]{:S(2)}) collective-permute-start(bf16[8,2,128,128]{3,2,1,0:T(8,128)(2,1)} %get-tuple-element.20), channel_id=1, source_target_pairs={{16,0},{32,16},{48,32},{17,1},{33,17},{49,33},{18,2},{34,18},{50,3... | collective-permute-start | bytes 1572872 | tf_op jit(solution)/shard_map/ppermute | solution.py:562
  105.8 33.3 %all-to-all-start.3 = ((bf16[16,2,128,128]{3,2,1,0:T(8,128)(2,1)}), bf16[16,2,128,128]{3,2,1,0:T(8,128)(2,1)S(1)}, u32[]{:S(2)}, u32[]{:S(2)}) async-start(bf16[16,2,128,128]{3,2,1,0:T(8,128)(2,1)} %bitcast.26), calls=%async_computation.3 | async-start | bytes 2097152 | tf_op jit(solution)/shard_map/all_to_all | solution.py:534
  114.5 4.5 %collective-permute-start.6 = (f32[8,128]{1,0:T(8,128)S(1)}, f32[8,128]{1,0:T(8,128)S(1)}, u32[]{:S(2)}, u32[]{:S(2)}) collective-permute-start(f32[8,128]{1,0:T(8,128)S(1)} %get-tuple-element.24), channel_id=1, source_target_pairs={{0,192},{64,128},{128,64},{192,0},{1,193},{65,129},{129,65},{193,1... | collective-permute-start | bytes 12296 | tf_op jit(solution)/shard_map/ppermute | solution.py:541
  114.9 5.4 %collective-permute-start.5 = (f32[8,128]{1,0:T(8,128)S(1)}, f32[8,128]{1,0:T(8,128)S(1)}, u32[]{:S(2)}, u32[]{:S(2)}) collective-permute-start(f32[8,128]{1,0:T(8,128)S(1)} %get-tuple-element.24), channel_id=1, source_target_pairs={{0,128},{64,192},{128,0},{192,64},{1,129},{65,193},{129,1},{193,65... | collective-permute-start | bytes 12296 | tf_op jit(solution)/shard_map/ppermute | solution.py:541
  117.4 2.9 %collective-permute-start.4 = (f32[8,128]{1,0:T(8,128)S(1)}, f32[8,128]{1,0:T(8,128)S(1)}, u32[]{:S(2)}, u32[]{:S(2)}) collective-permute-start(f32[8,128]{1,0:T(8,128)S(1)} %get-tuple-element.24), channel_id=1, source_target_pairs={{0,64},{64,0},{128,192},{192,128},{1,65},{65,1},{129,193},{193,129... | collective-permute-start | bytes 12296 | tf_op jit(solution)/shard_map/ppermute | solution.py:541
  120.3 4.2 %collective-permute-start.9 = (f32[8,128]{1,0:T(8,128)S(1)}, f32[8,128]{1,0:T(8,128)S(1)}, u32[]{:S(2)}, u32[]{:S(2)}) collective-permute-start(f32[8,128]{1,0:T(8,128)S(1)} %add_add_fusion.1), channel_id=1, source_target_pairs={{0,48},{16,32},{32,16},{48,0},{1,49},{17,33},{33,17},{49,1},{2,50}... | collective-permute-start | bytes 12296 | tf_op jit(solution)/shard_map/ppermute | solution.py:541
  121.6 5.1 %collective-permute-start.8 = (f32[8,128]{1,0:T(8,128)S(1)}, f32[8,128]{1,0:T(8,128)S(1)}, u32[]{:S(2)}, u32[]{:S(2)}) collective-permute-start(f32[8,128]{1,0:T(8,128)S(1)} %add_add_fusion.1), channel_id=1, source_target_pairs={{0,32},{16,48},{32,0},{48,16},{1,33},{17,49},{33,1},{49,17},{2,34}... | collective-permute-start | bytes 12296 | tf_op jit(solution)/shard_map/ppermute | solution.py:541
  123.0 3.7 %collective-permute-start.7 = (f32[8,128]{1,0:T(8,128)S(1)}, f32[8,128]{1,0:T(8,128)S(1)}, u32[]{:S(2)}, u32[]{:S(2)}) collective-permute-start(f32[8,128]{1,0:T(8,128)S(1)} %add_add_fusion.1), channel_id=1, source_target_pairs={{0,16},{16,0},{32,48},{48,32},{1,17},{17,1},{33,49},{49,33},{2,18}... | collective-permute-start | bytes 12296 | tf_op jit(solution)/shard_map/ppermute | solution.py:541
